TPU v7x, 32 devices: a whole 2x2x4 slice. The times are simulated.
32 devices in a mesh: ctx: 4 (over y, core), fsdp: 8 (over z, x).
Axes of the slice: x: 2, y: 2, z: 4, core: 2. Of those that a mesh axis runs over, the one named last changes fastest.
Arguments:
- hidden: bfloat16 [8, 1024, 2048], P('fsdp', 'ctx'), may hold values from -6 to 6
- cotangent: bfloat16 [8, 1024, 2048], P('fsdp', 'ctx'), may hold values from -6 to 6
- seq_lens: int32 [8], P('fsdp'), may hold values from 512 to 1024, as said below
- norm_gain: bfloat16 [2048], P('fsdp'), may hold values from 0.5 to 1.5
- in_weight: bfloat16 [2048, 8512], P('fsdp'), may hold values from -0.125 to 0.125
- conv_weight: bfloat16 [4, 4352], P(None, 'fsdp'), may hold values from -3 to 3
- conv_bias: bfloat16 [4352], P('fsdp'), may hold values from -3 to 3
- dt_bias: bfloat16 [64], P('fsdp'), may hold values from -6 to -4
- a_log: bfloat16 [64], P('fsdp'), may hold values from -3 to 1.59375
- d_skip: bfloat16 [64], P('fsdp'), may hold values from 0.5 to 4
- gate_gain: bfloat16 [4096], P('fsdp'), may hold values from 0.5 to 1.5
- out_weight: bfloat16 [4096, 2048], P('fsdp'), may hold values from -0.09375 to 0.09375
Outputs:
- layer_out: bfloat16 [8, 1024, 2048], P('fsdp', 'ctx')
- hidden_grad: bfloat16 [8, 1024, 2048], P('fsdp', 'ctx')
- norm_gain_grad: float32 [2048], P('fsdp')
- in_weight_grad: float32 [2048, 8512], P('fsdp')
- conv_weight_grad: float32 [4, 4352], P(None, 'fsdp')
- conv_bias_grad: float32 [4352], P('fsdp')
- dt_bias_grad: float32 [64], P('fsdp')
- a_log_grad: float32 [64], P('fsdp')
- d_skip_grad: float32 [64], P('fsdp')
- gate_gain_grad: float32 [4096], P('fsdp')
- out_weight_grad: float32 [4096, 2048], P('fsdp')
Inputs may be any that keep to these rules, and one draw needn't show every extreme that they name: A sequence's first seq_lens tokens are valid, the rest padding; some sequence is full and some holds exactly 512 valid tokens.
All inputs are finite; a program needn't handle non-finite values.
Results may differ from a plain program's by a relative error of at most 0.015.
Values may be sent and summed in bfloat16 or wider, within the bound.
A program may use at most 224 MiB of HBM per device.

v0:
```python
import jax
import jax.numpy as jnp
from jax import lax
from jax.sharding import PartitionSpec as P

H = 64
P_SIZE = 64
N = 128
BLOCK = 256


epsilon_norm = 1e-05


def passed_along(value, axis, by):
    length = lax.axis_size(axis)
    pairs = [(i, i + by) for i in range(length) if 0 <= i + by < length]
    return lax.ppermute(value, axis, pairs)


def prefix(value, axis, combine, identity):
    length, here = (lax.axis_size(axis), lax.axis_index(axis))
    everything = jax.tree.map(
        lambda part, kind: lax.all_gather(part.astype(kind), axis),
        value,
        (jnp.bfloat16, jnp.bfloat16),
    )
    start = jax.tree.map(
        lambda part, zero: jnp.broadcast_to(jnp.asarray(zero, part.dtype), part.shape),
        value,
        identity,
    )

    def step(k, before):
        reached = k < here
        new = combine(
            before, jax.tree.map(lambda part, own: part[k].astype(own.dtype), everything, value)
        )
        return jax.tree.map(lambda a, b: jnp.where(reached, a, b), new, before)

    return lax.fori_loop(0, length, step, start)


def prefix_2(value, axis, combine, identity):
    length, here = (lax.axis_size(axis), lax.axis_index(axis))
    everything = jax.tree.map(
        lambda part, kind: lax.all_gather(part.astype(kind), axis),
        value,
        jax.tree.map(lambda a: jnp.bfloat16 if a.dtype == jnp.float32 else a.dtype, value),
    )
    start = jax.tree.map(
        lambda part, zero: jnp.broadcast_to(jnp.asarray(zero, part.dtype), part.shape),
        value,
        identity,
    )

    def step(k, before):
        at = length - 1 - k
        reached = at > here
        new = combine(
            before, jax.tree.map(lambda part, own: part[at].astype(own.dtype), everything, value)
        )
        return jax.tree.map(lambda a, b: jnp.where(reached, a, b), new, before)

    return lax.fori_loop(0, length, step, start)


def block_step(carried, pieces):
    values, b_rows, c_rows, decay_rate, step_size, gram = pieces
    level = jnp.cumsum(decay_rate, axis=0)
    across = level.T
    spread = jnp.exp(-jnp.abs(across[:, :, None] - across[:, None, :]))
    mixing = gram[None, :, :] * spread * step_size.T[:, None, :]
    inner = jnp.einsum("hts,shp->thp", mixing, values, precision=lax.Precision.HIGHEST)
    entering = jnp.exp(-level)[:, :, None] * jnp.einsum(
        "tn,hpn->thp", c_rows, carried, precision=lax.Precision.HIGHEST
    )
    final = level[-1]
    weights = jnp.exp(level - final[None, :]) * step_size
    update = jnp.einsum("sh,shp,sn->hpn", weights, values, b_rows, precision=lax.Precision.HIGHEST)
    return (carried * jnp.exp(-final)[:, None, None] + update, inner + entering)


def front_norm(resid, gain):
    return resid * lax.rsqrt(jnp.mean(resid * resid, axis=-1, keepdims=True) + epsilon_norm) * gain


def conv_act(extended, weight, bias):
    taps = weight.shape[0]
    length = extended.shape[0] - taps + 1
    convolved = bias
    for offset in range(taps):
        convolved = convolved + weight[offset] * extended[offset : offset + length]
    return jax.nn.silu(convolved)


def decay_terms(step_raw, bias, log_rate, valid):
    step_size = jax.nn.softplus(step_raw + bias) * valid[:, None]
    return (step_size * jnp.exp(log_rate), step_size)


def local_scan(values, b_rows, c_rows, decay_rate, step_size, gram, skip):
    length = values.shape[0]
    count = length // BLOCK
    blocks = (
        values.reshape(count, BLOCK, H, P_SIZE),
        b_rows.reshape(count, BLOCK, N),
        c_rows.reshape(count, BLOCK, N),
        decay_rate.reshape(count, BLOCK, H),
        step_size.reshape(count, BLOCK, H),
        gram,
    )
    state, outputs = lax.scan(
        jax.checkpoint(block_step), jnp.zeros((H, P_SIZE, N), jnp.float32), blocks
    )
    mixed_ssd = outputs.reshape(length, H, P_SIZE) + skip[:, None] * values
    return (mixed_ssd, state, jnp.sum(decay_rate, axis=0))


def carry_in(c_rows, decay_rate, entry_state):
    level = jnp.cumsum(decay_rate, axis=0)
    return jnp.exp(-level)[:, :, None] * jnp.einsum(
        "tn,hpn->thp", c_rows, entry_state, precision=lax.Precision.HIGHEST
    )


def gated_norm(mixed_ssd, gate_raw, gain):
    gated = mixed_ssd * jax.nn.silu(gate_raw)
    return gated * lax.rsqrt(jnp.mean(gated * gated, axis=-1, keepdims=True) + epsilon_norm) * gain


def combine(earlier, later):
    return (earlier[0] * later[1][:, None, None] + later[0], earlier[1] * later[1])


def on_device(
    hidden,
    cotangent,
    seq_lens,
    norm_gain,
    in_weight,
    conv_weight,
    conv_bias,
    dt_bias,
    a_log,
    d_skip,
    gate_gain,
    out_weight,
):
    gathered = (
        lax.all_gather(norm_gain, "fsdp", axis=0, tiled=True),
        lax.all_gather(in_weight, "fsdp", axis=0, tiled=True),
        lax.all_gather(conv_weight, "fsdp", axis=1, tiled=True),
        lax.all_gather(conv_bias, "fsdp", axis=0, tiled=True),
        lax.all_gather(dt_bias, "fsdp", axis=0, tiled=True),
        lax.all_gather(a_log, "fsdp", axis=0, tiled=True),
        lax.all_gather(d_skip, "fsdp", axis=0, tiled=True),
        lax.all_gather(gate_gain, "fsdp", axis=0, tiled=True),
        lax.all_gather(out_weight, "fsdp", axis=0, tiled=True),
    )
    (
        gain_norm,
        weight_in,
        weight_conv,
        bias_conv,
        bias_step,
        log_rate,
        skip_coef,
        gain_gate,
        weight_out,
    ) = gathered
    length = hidden.shape[1]
    width = weight_out.shape[0]
    channels = weight_conv.shape[1]
    taps = weight_conv.shape[0]
    count = length // BLOCK
    resid = hidden[0].astype(jnp.float32)
    places = lax.axis_index("ctx") * length + jnp.arange(length, dtype=jnp.int32)
    valid = (places < seq_lens[0]).astype(jnp.float32)
    normed, pull_norm = jax.vjp(front_norm, resid, gain_norm.astype(jnp.float32))
    normed_low = normed.astype(jnp.bfloat16)
    projected = jnp.dot(normed_low, weight_in, preferred_element_type=jnp.float32).astype(
        jnp.bfloat16
    )
    gate_raw = projected[:, :width].astype(jnp.float32)
    conv_in = projected[:, width : width + channels]
    step_raw = projected[:, width + channels :].astype(jnp.float32)
    border = passed_along(conv_in[length - (taps - 1) :], "ctx", 1)
    extended = jnp.concatenate([border, conv_in], axis=0).astype(jnp.float32)
    activated, pull_conv = jax.vjp(
        conv_act, extended, weight_conv.astype(jnp.float32), bias_conv.astype(jnp.float32)
    )
    activated_low = activated.astype(jnp.bfloat16)
    activated = activated_low.astype(jnp.float32)
    values = activated[:, :width].reshape(length, H, P_SIZE)
    b_rows = activated[:, width : width + N]
    c_rows = activated[:, width + N :]
    b_low = activated_low[:, width : width + N].reshape(count, BLOCK, N)
    c_low = activated_low[:, width + N :].reshape(count, BLOCK, N)
    gram = jnp.einsum("btn,bsn->bts", c_low, b_low, preferred_element_type=jnp.float32)
    (decay_rate, step_size), pull_decay = jax.vjp(
        lambda raw, bias, rate: decay_terms(raw, bias, rate, valid),
        step_raw,
        bias_step.astype(jnp.float32),
        log_rate.astype(jnp.float32),
    )
    (local_out, state, total), pull_scan = jax.vjp(
        local_scan,
        values,
        b_rows,
        c_rows,
        decay_rate,
        step_size,
        gram,
        skip_coef.astype(jnp.float32),
    )
    fade = jnp.exp(-total)
    entry_state = prefix(
        (state, fade), "ctx", combine, (jnp.zeros_like(state), jnp.ones_like(fade))
    )[0]
    entering, pull_carry = jax.vjp(carry_in, c_rows, decay_rate, entry_state)
    mixed_ssd = (local_out + entering).reshape(length, width)
    normed_gate, pull_gate = jax.vjp(gated_norm, mixed_ssd, gate_raw, gain_gate.astype(jnp.float32))
    gate_low = normed_gate.astype(jnp.bfloat16)
    mixed = jnp.dot(gate_low, weight_out, preferred_element_type=jnp.float32)
    layer_out = (resid + valid[:, None] * mixed).astype(jnp.bfloat16)
    upstream = cotangent[0]
    d_mixed = upstream * valid[:, None].astype(jnp.bfloat16)
    weight_in_back, weight_out_back = (
        lax.all_gather(in_weight, "fsdp", axis=0, tiled=True),
        lax.all_gather(out_weight, "fsdp", axis=0, tiled=True),
    )
    grad_out_weight = lax.dot_general(
        gate_low, d_mixed, (((0,), (0,)), ((), ())), preferred_element_type=jnp.float32
    )
    d_gate_in = lax.dot_general(
        d_mixed, weight_out_back, (((1,), (1,)), ((), ())), preferred_element_type=jnp.float32
    )
    d_ssd, d_gate_raw, d_gain_gate = pull_gate(d_gate_in)
    d_ssd = d_ssd.reshape(length, H, P_SIZE)
    d_c_carry, d_rate_carry, d_entry = pull_carry(d_ssd)
    d_exit = prefix_2(
        (d_entry, fade), "ctx", combine, (jnp.zeros_like(d_entry), jnp.ones_like(fade))
    )[0]
    d_total = -fade * jnp.sum(d_exit * entry_state, axis=(1, 2))
    d_values, d_b_rows, d_c_rows, d_rate, d_step, d_gram, d_skip_coef = pull_scan(
        (d_ssd, d_exit, d_total)
    )
    b_blocks = b_rows.reshape(count, BLOCK, N)
    c_blocks = c_rows.reshape(count, BLOCK, N)
    d_c_gram = jnp.einsum(
        "bts,bsn->btn", d_gram, b_blocks, precision=lax.Precision.HIGHEST
    ).reshape(length, N)
    d_b_gram = jnp.einsum(
        "bts,btn->bsn", d_gram, c_blocks, precision=lax.Precision.HIGHEST
    ).reshape(length, N)
    d_b_rows = d_b_rows + d_b_gram
    d_c_rows = d_c_rows + d_c_carry + d_c_gram
    d_rate = d_rate + d_rate_carry
    d_step_raw, d_bias_step, d_log_rate = pull_decay((d_rate, d_step))
    d_activated = jnp.concatenate([d_values.reshape(length, width), d_b_rows, d_c_rows], axis=1)
    d_extended, d_weight_conv, d_bias_conv = pull_conv(d_activated)
    back_border = passed_along(d_extended[: taps - 1].astype(jnp.bfloat16), "ctx", -1).astype(
        jnp.float32
    )
    d_conv_in = d_extended[taps - 1 :]
    d_conv_in = jnp.concatenate(
        [d_conv_in[: length - (taps - 1)], d_conv_in[length - (taps - 1) :] + back_border], axis=0
    )
    d_projected = jnp.concatenate([d_gate_raw, d_conv_in, d_step_raw], axis=1).astype(jnp.bfloat16)
    d_normed = lax.dot_general(
        d_projected, weight_in_back, (((1,), (1,)), ((), ())), preferred_element_type=jnp.float32
    )
    d_resid, d_gain_norm = pull_norm(d_normed)
    hidden_grad = (upstream.astype(jnp.float32) + d_resid).astype(jnp.bfloat16)
    grad_in_weight = lax.psum_scatter(
        lax.dot_general(
            normed_low, d_projected, (((0,), (0,)), ((), ())), preferred_element_type=jnp.float32
        ),
        "fsdp",
        scatter_dimension=0,
        tiled=True,
    )
    shares = (
        lax.psum_scatter(d_gain_norm, "fsdp", scatter_dimension=0, tiled=True),
        lax.psum_scatter(d_weight_conv, "fsdp", scatter_dimension=1, tiled=True),
        lax.psum_scatter(d_bias_conv, "fsdp", scatter_dimension=0, tiled=True),
        lax.psum_scatter(d_bias_step, "fsdp", scatter_dimension=0, tiled=True),
        lax.psum_scatter(d_log_rate, "fsdp", scatter_dimension=0, tiled=True),
        lax.psum_scatter(d_skip_coef, "fsdp", scatter_dimension=0, tiled=True),
        lax.psum_scatter(d_gain_gate, "fsdp", scatter_dimension=0, tiled=True),
        lax.psum_scatter(grad_out_weight, "fsdp", scatter_dimension=0, tiled=True),
    )
    summed = (
        lax.psum(grad_in_weight.astype(jnp.bfloat16), "ctx").astype(jnp.float32),
        lax.psum(shares[0].astype(jnp.bfloat16), "ctx").astype(jnp.float32),
        lax.psum(shares[1].astype(jnp.bfloat16), "ctx").astype(jnp.float32),
        lax.psum(shares[2].astype(jnp.bfloat16), "ctx").astype(jnp.float32),
        lax.psum(shares[3].astype(jnp.bfloat16), "ctx").astype(jnp.float32),
        lax.psum(shares[4].astype(jnp.bfloat16), "ctx").astype(jnp.float32),
        lax.psum(shares[5].astype(jnp.bfloat16), "ctx").astype(jnp.float32),
        lax.psum(shares[6].astype(jnp.bfloat16), "ctx").astype(jnp.float32),
        lax.psum(shares[7].astype(jnp.bfloat16), "ctx").astype(jnp.float32),
    )
    return (
        layer_out[None],
        hidden_grad[None],
        summed[1],
        summed[0],
        summed[2],
        summed[3],
        summed[4],
        summed[5],
        summed[6],
        summed[7],
        summed[8],
    )


def solution(mesh):
    placed = (
        P("fsdp", "ctx", None),
        P("fsdp", "ctx", None),
        P("fsdp"),
        P("fsdp"),
        P("fsdp", None),
        P(None, "fsdp"),
        P("fsdp"),
        P("fsdp"),
        P("fsdp"),
        P("fsdp"),
        P("fsdp"),
        P("fsdp", None),
    )
    return jax.shard_map(
        on_device,
        mesh=mesh,
        in_specs=placed,
        out_specs=(
            P("fsdp", "ctx", None),
            P("fsdp", "ctx", None),
            P("fsdp"),
            P("fsdp", None),
            P(None, "fsdp"),
            P("fsdp"),
            P("fsdp"),
            P("fsdp"),
            P("fsdp"),
            P("fsdp"),
            P("fsdp", None),
        ),
        check_vma=False,
    )
```

profile of v0, /device:TPU:17, one launch (start us, length us, event | category | flops | bytes accessed | tf_op | source)
XLA Modules:
  0.0 2917.3 jit_solution(17397235780102694787)
XLA Ops:
  11.7 69.1 %all-reduce.21 = (bf16[64]{0:T(256)(128)(2,1)S(1)}, bf16[64]{0:T(256)(128)(2,1)S(1)}, bf16[4352]{0:T(1024)(128)(2,1)S(1)}, bf16[64]{0:T(256)(128)(2,1)S(1)}) all-reduce(bf16[64]{0:T(256)(128)(2,1)S(1)} %dynamic-update-slice.2, bf16[64]{0:T(256)(128)(2,1)S(1)} %dynamic-update-slice.1, ...), channel_id=1, replica_groups=mesh['ctx'=4,'fsdp'=8] {'fsdp'}, use_global_device_ids=true, to_apply=%add.11 | all-reduce | flops 4544 | bytes 18176
  80.8 13.6 all-gather.4
  94.4 67.9 %all-gather.3 = bf16[8,544,4]{1,2,0:T(4,128)(2,1)S(1)} all-gather(bf16[1,544,4]{1,2,0:T(4,128)(2,1)S(1)} %bitcast.248), channel_id=1, replica_groups=mesh['ctx'=4,'fsdp'=8] {'fsdp'}, dimensions={0}, use_global_device_ids=true | all-gather | bytes 39168 | tf_op jit(solution)/shard_map/all_gather | solution.py:153
  163.1 513.4 %all-gather.11.cloned.1.call-done = bf16[2048,8512]{0,1:T(8,128)(2,1)} async-done(((bf16[256,8512]{0,1:T(8,128)(2,1)}), bf16[2048,8512]{0,1:T(8,128)(2,1)}) %all-gather.11.cloned.1.call-update) | async-done | bytes 34865168 | tf_op jit(solution)/shard_map/all_gather | solution.py:152
  676.5 17.3 convolution_convert_fusion
  702.0 4.9 fusion.148
  708.7 4.1 copy.176
  712.8 4.8 add_convert_fusion
  719.0 18.8 all-gather.5
  738.8 9.1 all-reduce.13
  748.2 4.1 slice.148
  752.3 5.6 copy.183
  758.9 4.9 fusion.98
  763.8 7.5 while.20
  775.0 15.8 fusion.45
  790.7 5.6 copy.185
  796.4 6.4 multiply_reduce_fusion.10
  802.8 176.7 %all-gather.13.cloned.1.call-done = bf16[4096,2048]{1,0:T(8,128)(2,1)} async-done(((bf16[512,2048]{1,0:T(8,128)(2,1)}), bf16[4096,2048]{1,0:T(8,128)(2,1)}) %all-gather.13.cloned.1.call-update) | async-done | bytes 16777232 | tf_op jit(solution)/shard_map/all_gather | solution.py:159
  979.5 20.6 multiply_reduce_fusion.5
  1000.1 10.6 multiply_reduce_fusion.6
  1010.7 5.6 copy.187
  1016.3 5.2 fusion.82
  1021.7 16.8 fusion.100
  1040.4 4.6 multiply_reduce_fusion.7
  1048.1 9.3 fusion.85
  1057.5 7.3 while.21
  1066.0 31.3 %fusion.105 = (f32[64,256]{1,0:T(8,128)S(1)}, f32[64,256]{1,0:T(8,128)S(1)}, f32[64,256]{1,0:T(8,128)}, f32[256,256]{1,0:T(8,128)S(1)}) fusion(f32[64,256]{1,0:T(8,128)S(1)} %copy.193, f32[256,256]{1,0:T(8,128)S(1)} %fusion.130, f32[64,256]{1,0:T(8,128)S(1)} %copy.191, f32[256,64,64]{0,2,1:T(8,128)} %bitcast.214, f32[256,64,64]{0,2,1:T(8,128)} %bitcast.210), kind=kOutput, calls=%fused_computation.138 | convolution fusion | flops 3300802560 | bytes 9240576 | tf_op jit(solution)/shard_map/transpose(jvp())/while/body/eval_jaxpr/checkpoint/hts,shp->thp/dot_general | solution.py:74
  1099.2 5.9 multiply_reduce_fusion.8
  1106.0 6.6 multiply_reduce_fusion.4
  1124.4 17.1 bitcast_add_fusion
  1141.5 5.7 copy.194
  1147.2 9.6 fusion.94
  1158.1 6.7 fusion.88
  1167.6 4.9 multiply_reduce_fusion.3
  1172.6 5.2 broadcast_multiply_fusion
  1177.8 5.8 fusion.152
  1189.4 27.0 fusion.102
  1220.5 12.8 fusion.60
  1235.6 365.0 %reduce-scatter.8.cloned.1.call-done = f32[512,2048]{1,0:T(8,128)} async-done(((f32[4096,2048]{1,0:T(8,128)}), f32[512,2048]{1,0:T(8,128)}) %reduce-scatter.8.cloned.1.call-update) | async-done | bytes 4194320 | tf_op jit(solution)/shard_map/reduce_scatter | solution.py:292
  1600.6 3.8 convert_element_type.254
  1604.4 1099.9 %reduce-scatter.6.cloned.1.call-done = f32[256,8512]{0,1:T(8,128)} async-done(((f32[2048,8512]{0,1:T(8,128)}), f32[256,8512]{0,1:T(8,128)}) %reduce-scatter.6.cloned.1.call-update) | async-done | bytes 8716304 | tf_op jit(solution)/shard_map/reduce_scatter | solution.py:276
  2704.3 5.3 convert_element_type.240
  2709.7 17.6 fusion.64
  2727.4 25.2 all-reduce.20
  2756.6 18.6 reduce-scatter.10.cloned.1.call-done
  2776.3 10.8 all-reduce.22
  2790.9 110.9 %all-reduce.26.cloned.1.call-done = (bf16[256,8512]{0,1:T(8,128)(2,1)}, bf16[512,2048]{1,0:T(8,128)(2,1)}) async-done(((bf16[256,8512]{0,1:T(8,128)(2,1)}, bf16[512,2048]{1,0:T(8,128)(2,1)}), (bf16[256,8512]{0,1:T(8,128)(2,1)}, bf16[512,2048]{1,0:T(8,128)(2,1)})) %all-reduce.26.cloned.1.call-update) | async-done | bytes 6455312 | tf_op jit(solution)/shard_map/psum | solution.py:295
  2901.9 5.6 convert_element_type.241
  (295 shorter events, 80.0 us)
Async XLA Ops:
  7.2 73.5 %copy-start.54 = (bf16[256]{0:T(256)(128)(2,1)S(1)}, bf16[256]{0:T(256)(128)(2,1)}, u32[]{:S(2)}) copy-start(bf16[256]{0:T(256)(128)(2,1)} %param.19) | copy-start | bytes 1540
  7.2 87.2 %copy-start.39 = (bf16[4,544]{1,0:T(4,128)(2,1)S(1)}, bf16[4,544]{1,0:T(4,128)(2,1)}, u32[]{:S(2)}) copy-start(bf16[4,544]{1,0:T(4,128)(2,1)} %param.21) | copy-start | bytes 13060
  7.3 155.4 %copy-start.9 = (bf16[1,256,2048]{2,1,0:T(8,128)(2,1)S(1)}, bf16[1,256,2048]{2,1,0:T(8,128)(2,1)}, u32[]{:S(2)}) copy-start(bf16[1,256,2048]{2,1,0:T(8,128)(2,1)} %param.16) | copy-start | bytes 3145732
  7.3 669.2 %all-gather.11.cloned.1.call-start = ((), (), s32[]{:S(2)}) async-start(), calls=%async_computation.3 | async-start | bytes 39223296 | tf_op jit(solution)/shard_map/all_gather | solution.py:152
  8.0 755.8 %all-gather.15.cloned.1.call-start = ((), (), s32[]{:S(2)}) async-start(), calls=%async_computation.7 | async-start | bytes 5242880 | tf_op jit(solution)/shard_map/all_gather | solution.py:24
  80.7 613.0 %copy-start.55 = (bf16[64]{0:T(256)(128)(2,1)}, bf16[64]{0:T(256)(128)(2,1)S(1)}, u32[]{:S(2)}) copy-start(bf16[64]{0:T(256)(128)(2,1)S(1)} %get-tuple-element.414) | copy-start | bytes 388
  80.7 619.6 %copy-start.40 = (f32[64]{0:T(128)}, f32[64]{0:T(128)S(1)}, u32[]{:S(2)}) copy-start(f32[64]{0:T(128)S(1)} %convert_element_type.222) | copy-start | bytes 772
  94.4 582.1 %copy-start.14 = (f32[8,1,256]{2,1,0:T(1,128)}, f32[8,1,256]{2,1,0:T(1,128)S(1)}, u32[]{:S(2)}) copy-start(f32[8,1,256]{2,1,0:T(1,128)S(1)} %convert_element_type.262) | copy-start | bytes 24580
  162.5 537.9 %copy-start.34 = (f32[256]{0:T(256)}, f32[256]{0:T(256)S(1)}, u32[]{:S(2)}) copy-start(f32[256]{0:T(256)S(1)} %compare_convert_fusion) | copy-start | bytes 3076
  162.7 539.3 %copy-start.22 = (f32[4352]{0:T(1024)}, f32[4352]{0:T(1024)S(1)}, u32[]{:S(2)}) copy-start(f32[4352]{0:T(1024)S(1)} %get-tuple-element.384) | copy-start | bytes 52228
  162.7 539.3 %copy-start.24 = (f32[4352]{0:T(1024)}, f32[4352]{0:T(1024)S(1)}, u32[]{:S(2)}) copy-start(f32[4352]{0:T(1024)S(1)} %get-tuple-element.385) | copy-start | bytes 52228
  162.7 539.3 %copy-start.26 = (f32[4352]{0:T(1024)}, f32[4352]{0:T(1024)S(1)}, u32[]{:S(2)}) copy-start(f32[4352]{0:T(1024)S(1)} %get-tuple-element.386) | copy-start | bytes 52228
  162.7 539.3 %copy-start.28 = (f32[4352]{0:T(1024)}, f32[4352]{0:T(1024)S(1)}, u32[]{:S(2)}) copy-start(f32[4352]{0:T(1024)S(1)} %get-tuple-element.387) | copy-start | bytes 52228
  163.0 513.5 %copy-start.37 = (f32[256]{0:T(256)}, f32[256]{0:T(256)S(1)}, u32[]{:S(2)}) copy-start(f32[256]{0:T(256)S(1)} %fusion.67) | copy-start | bytes 3076
  163.0 535.2 %copy-start.44 = (f32[64]{0:T(128)}, f32[64]{0:T(128)S(1)}, u32[]{:S(2)}) copy-start(f32[64]{0:T(128)S(1)} %convert_exponential_fusion) | copy-start | bytes 772
  163.1 513.4 %copy-start.17 = (f32[256]{0:T(256)}, f32[256]{0:T(256)S(1)}, u32[]{:S(2)}) copy-start(f32[256]{0:T(256)S(1)} %fusion.137) | copy-start | bytes 3076
  693.8 7.7 slice-start.4
  694.8 6.6 collective-permute-start
  699.2 39.2 %copy-start.50 = (f32[64]{0:T(128)}, f32[64]{0:T(128)S(1)}, u32[]{:S(2)}) copy-start(f32[64]{0:T(128)S(1)} %get-tuple-element.441) | copy-start | bytes 772
  712.8 6.2 copy-start.48
  717.6 261.9 %all-gather.13.cloned.1.call-start = ((), (), s32[]{:S(2)}) async-start(), calls=%async_computation.4 | async-start | bytes 18874368 | tf_op jit(solution)/shard_map/all_gather | solution.py:159
  718.3 339.1 %all-gather.17.cloned.1.call-start = ((), (), s32[]{:S(2)}) async-start(), calls=%async_computation.8 | async-start | bytes 5242880 | tf_op jit(solution)/shard_map/all_gather | solution.py:47
  737.8 283.8 %copy-start.19 = (f32[8,1,512]{2,1,0:T(1,128)}, f32[8,1,512]{2,1,0:T(1,128)S(1)}, u32[]{:S(2)}) copy-start(f32[8,1,512]{2,1,0:T(1,128)S(1)} %convert_element_type.263) | copy-start | bytes 49156
  758.9 307.1 %copy-start.21 = (f32[256,256]{1,0:T(8,128)}, f32[256,256]{1,0:T(8,128)S(1)}, u32[]{:S(2)}) copy-start(f32[256,256]{1,0:T(8,128)S(1)} %fusion.130) | copy-start | bytes 786436
  771.3 19.5 copy-start.1
  774.2 16.6 copy-start.7
  796.4 183.1 %copy-start.11 = (bf16[1,256,2048]{2,1,0:T(8,128)(2,1)S(1)}, bf16[1,256,2048]{2,1,0:T(8,128)(2,1)}, u32[]{:S(2)}) copy-start(bf16[1,256,2048]{2,1,0:T(8,128)(2,1)} %param.17) | copy-start | bytes 3145732
  802.8 218.8 %copy-start.32 = (f32[256]{0:T(256)}, f32[256]{0:T(256)S(1)}, u32[]{:S(2)}) copy-start(f32[256]{0:T(256)S(1)} %fusion.138) | copy-start | bytes 3076
  1021.6 579.0 %reduce-scatter.8.cloned.1.call-start = ((), (), s32[]{:S(2)}) async-start(), calls=%async_computation.6 | async-start | bytes 37748736 | tf_op jit(solution)/shard_map/reduce_scatter | solution.py:292
  1038.5 1665.8 %reduce-scatter.6.cloned.1.call-start = ((), (), s32[]{:S(2)}) async-start(), calls=%async_computation.5 | async-start | bytes 78446592 | tf_op jit(solution)/shard_map/reduce_scatter | solution.py:276
  1064.8 32.5 %copy-start.30 = (f32[64,256]{1,0:T(8,128)}, f32[64,256]{1,0:T(8,128)S(1)}, u32[]{:S(2)}) copy-start(f32[64,256]{1,0:T(8,128)S(1)} %copy.193) | copy-start | bytes 196612
  1066.0 31.3 %copy-start.31 = (f32[64,256]{1,0:T(8,128)}, f32[64,256]{1,0:T(8,128)S(1)}, u32[]{:S(2)}) copy-start(f32[64,256]{1,0:T(8,128)S(1)} %copy.191) | copy-start | bytes 196612
  1097.5 8.4 copy-start.16
  1115.5 7.2 copy-start.43
  1147.2 10.9 copy-start.5
  1147.2 19.0 copy-start.8
  1156.8 9.4 copy-start.3
  1158.0 9.0 slice-start.2
  1183.6 5.9 copy-start.10
  1183.6 5.9 copy-start.15
  1183.6 5.9 copy-start.18
  1183.6 5.8 collective-permute-start.1
  1216.5 1558.7 %reduce-scatter.10.cloned.1.call-start = ((), (), s32[]{:S(2)}) async-start(), calls=%async_computation.9 | async-start | bytes 2506752
  1235.5 1666.3 %all-reduce.26.cloned.1.call-start = ((), (), s32[]{:S(2)}) async-start(), calls=%async_computation.10 | async-start | bytes 12910592 | tf_op jit(solution)/shard_map/psum | solution.py:295
  2709.7 17.7 copy-start.36
  2709.7 17.7 copy-start.41
  2709.7 17.7 copy-start.45
  2709.7 43.3 %copy-start.38 = (f32[256]{0:T(256)S(1)}, f32[256]{0:T(256)}, u32[]{:S(2)}) copy-start(f32[256]{0:T(256)} %copy-done.37) | copy-start | bytes 3076
  (25 other events, 89.2 us)
Sparse Core Ops, SparseCore 0:
  9.6 666.8 all-gather.10
  717.7 33.6 all-gather.14
  753.6 225.8 all-gather.12
  1021.7 34.3 all-gather.16
  1059.7 540.8 reduce-scatter.7
  1604.4 1099.8 reduce-scatter.5
  2708.8 66.3 reduce-scatter.9
  2778.4 123.4 all-reduce.25
where the time goes:
time: 2930 us; the launch traced here: 2920 us
  waiting for transfers between devices  2290 us (78%)
  matrix products  236 us (8%)
  blocking collectives  214 us (7%)
  other arithmetic  99.8 us (3%)
  local copies, waits for them, and re-layouts  50.8 us (2%)
    reduce_scatter x1, waiting for transfers between devices, on_device(): lax.psum_scatter(lax.dot_general(normed_low, d_projected, (((0,), (0,)),...  1100 us
    all_gather x1, waiting for transfers between devices, on_device(): lax.all_gather(in_weight, 'fsdp', axis=0, tiled=True)  513 us
    reduce_scatter x1, waiting for transfers between devices, on_device(): lax.psum_scatter(grad_out_weight, 'fsdp', scatter_dimension=0, tiled=True)  365 us
    all_gather x1, waiting for transfers between devices, on_device(): lax.all_gather(out_weight, 'fsdp', axis=0, tiled=True)  177 us
    psum x1, waiting for transfers between devices, on_device(): lax.psum(grad_in_weight.astype(jnp.bfloat16), 'ctx').astype(jnp.float32)  111 us
    unnamed x3, blocking collectives  103 us
    all_gather x1, blocking collectives, on_device(): lax.all_gather(conv_weight, 'fsdp', axis=1, tiled=True)  67.9 us
    dot_general x3, matrix products, block_step(): jnp.einsum('hts,shp->thp', mixing, values, precision=lax.Precision.HIGHEST)  64.2 us
  transfers between devices with their start and end apart: 10, of which 7 were waited for; matrix products, arithmetic and copies ran while one was open for 10% of the time, Pallas kernels for 0%

commit v1 on v0

v1 whole, which is shorter than its diff:
```python
import functools

import jax
import jax.numpy as jnp
from jax import lax
from jax.experimental import pallas as pl
from jax.experimental.pallas import tpu as pltpu
from jax.sharding import PartitionSpec as P

HEAD = 64
STATE = 128
BLOCK = 256
LANES = 128
EPS = 1e-05
F32 = jnp.float32
BF16 = jnp.bfloat16


def mm(a, b, contract=((1,), (0,))):
    return lax.dot_general(a, b, (contract, ((), ())), preferred_element_type=F32)


def mm_exact(a, b, contract=((1,), (0,))):
    return lax.dot_general(
        a, b, (contract, ((), ())), precision=lax.Precision.HIGHEST, preferred_element_type=F32
    )


def iota2(shape, axis):
    return lax.broadcasted_iota(jnp.int32, shape, axis)


def levels(lam, step):
    tri = (iota2((BLOCK, BLOCK), 0) >= iota2((BLOCK, BLOCK), 1)).astype(F32)
    level = mm_exact(tri, lam)
    across = level.T
    last = level[BLOCK - 1 : BLOCK, :]
    weight = jnp.exp(level - last) * step
    return level, across, jnp.exp(-last), weight, jnp.exp(-level)


def pair_of(array, first, low_half):
    return jnp.where(low_half, array[:, first : first + 1], array[:, first + 1 : first + 2])


def spread(level, across, head):
    return jnp.exp(-jnp.abs(level[:, head : head + 1] - across[head : head + 1, :]))


def forward_kernel(heads, x_ref, b_ref, c_ref, lam_ref, step_ref, skip_ref, y_ref, kept_ref, state):
    @pl.when(pl.program_id(0) == 0)
    def _():
        state[...] = jnp.zeros_like(state)

    rows_b, rows_c = b_ref[...], c_ref[...]
    step = step_ref[...]
    gram = mm(rows_c, rows_b, ((1,), (1,)))
    level, across, last, weight, fade = levels(lam_ref[...], step)
    kept_ref[0] = state[...].astype(BF16)
    entering = mm(rows_c, state[...].astype(BF16))
    by_state = rows_b.T
    low_half = iota2((1, LANES), 1) < HEAD
    for first in range(0, heads, 2):
        lanes = slice(first * HEAD, (first + 2) * HEAD)
        x = x_ref[:, lanes].astype(F32)
        scaled = x * pair_of(step, first, low_half)
        total = pair_of(fade, first, low_half) * entering[:, lanes] + skip_ref[:, lanes] * x
        for head, keep in ((first, low_half), (first + 1, jnp.logical_not(low_half))):
            mixing = (gram * spread(level, across, head)).astype(BF16)
            total += mm(mixing, jnp.where(keep, scaled, 0.0).astype(BF16))
        y_ref[:, lanes] = total
        update = mm(by_state, (x * pair_of(weight, first, low_half)).astype(BF16))
        state[:, lanes] = state[:, lanes] * pair_of(last, first, low_half) + update


def scan_forward(x, rows_b, rows_c, lam, step, skip):
    tokens, width = x.shape
    heads = width // HEAD
    count = tokens // BLOCK
    by_block = lambda i: (i, 0)
    return pl.pallas_call(
        functools.partial(forward_kernel, heads),
        grid=(count,),
        in_specs=[
            pl.BlockSpec((BLOCK, width), by_block),
            pl.BlockSpec((BLOCK, STATE), by_block),
            pl.BlockSpec((BLOCK, STATE), by_block),
            pl.BlockSpec((BLOCK, LANES), by_block),
            pl.BlockSpec((BLOCK, LANES), by_block),
            pl.BlockSpec((1, width), lambda i: (0, 0)),
        ],
        out_specs=[
            pl.BlockSpec((BLOCK, width), by_block),
            pl.BlockSpec((1, STATE, width), lambda i: (i, 0, 0)),
        ],
        out_shape=[
            jax.ShapeDtypeStruct((tokens, width), F32),
            jax.ShapeDtypeStruct((count, STATE, width), BF16),
        ],
        scratch_shapes=[pltpu.VMEM((STATE, width), F32)],
        compiler_params=pltpu.CompilerParams(vmem_limit_bytes=32 * 1024 * 1024),
        cost_estimate=pl.CostEstimate(
            flops=2 * tokens * width * (2 * BLOCK + 2 * STATE),
            bytes_accessed=tokens * width * 6,
            transcendentals=tokens * heads * BLOCK,
        ),
        name="scan_forward",
    )(x, rows_b, rows_c, lam, step, skip)


def head_sums(product, chooser):
    high = product.astype(BF16)
    rest = (product - high.astype(F32)).astype(BF16)
    return mm(high, chooser) + mm(rest, chooser)


def backward_kernel(
    heads,
    x_ref,
    b_ref,
    c_ref,
    lam_ref,
    step_ref,
    skip_ref,
    grad_ref,
    kept_ref,
    dx_ref,
    db_ref,
    dc_ref,
    dstep_ref,
    dlam_ref,
    dskip_ref,
    back,
    mixed_grads,
    for_step,
    for_level,
    left,
    right,
    sums,
):
    @pl.when(pl.program_id(0) == 0)
    def _():
        back[...] = jnp.zeros_like(back)
        dskip_ref[...] = jnp.zeros_like(dskip_ref)

    rows_b, rows_c = b_ref[...], c_ref[...]
    step = step_ref[...]
    gram = mm(rows_c, rows_b, ((1,), (1,)))
    gram_t = mm(rows_b, rows_c, ((1,), (1,)))
    level, across, last, weight, fade = levels(lam_ref[...], step)
    step_across = step.T
    at_row, at_col = iota2((BLOCK, BLOCK), 0), iota2((BLOCK, BLOCK), 1)
    order = (at_row > at_col).astype(F32) - (at_row < at_col).astype(F32)
    low_half = iota2((1, LANES), 1) < HEAD
    lane = iota2((1, LANES), 1)
    by_state = rows_c.T
    kept = kept_ref[0]
    old_back = back[...].astype(BF16)
    entering = mm(rows_c, kept)
    leaving = mm(rows_b, old_back)
    at_last = jnp.sum(kept.astype(F32) * back[...], axis=0, keepdims=True)
    mixed_grads[...] = jnp.zeros_like(mixed_grads)
    left[...] = jnp.zeros_like(left)
    right[...] = jnp.zeros_like(right)
    sums[...] = jnp.zeros_like(sums)
    d_b = jnp.zeros((BLOCK, STATE), F32)
    d_c = jnp.zeros((BLOCK, STATE), F32)
    for first in range(0, heads, 2):
        lanes = slice(first * HEAD, (first + 2) * HEAD)
        x_low = x_ref[:, lanes]
        grad_low = grad_ref[:, lanes]
        x, grad = x_low.astype(F32), grad_low.astype(F32)
        through = jnp.zeros((BLOCK, LANES), F32)
        for head, keep in ((first, low_half), (first + 1, jnp.logical_not(low_half))):
            decay = spread(level, across, head)
            grad_own = jnp.where(keep, grad, 0.0).astype(BF16)
            pairs = mm(grad_own, x_low, ((1,), (1,)))
            through += mm((gram_t * decay).astype(BF16), grad_own)
            scaled = decay * pairs * step_across[head : head + 1, :]
            mixed_grads[...] += scaled
            ordered = gram * scaled * order
            left[...] = jnp.where(
                lane == head, jnp.sum(ordered, axis=1, keepdims=True), left[...]
            )
            right[head : head + 1, :] = jnp.sum(ordered, axis=0, keepdims=True)
        weight_pair = pair_of(weight, first, low_half)
        step_pair = pair_of(step, first, low_half)
        fade_pair = pair_of(fade, first, low_half)
        out_pair = pair_of(jnp.exp(level - level[BLOCK - 1 : BLOCK, :]), first, low_half)
        leave = leaving[:, lanes]
        dx_ref[:, lanes] = step_pair * through + weight_pair * leave + skip_ref[:, lanes] * grad
        for_step[:, lanes] = x * (through + out_pair * leave)
        weighted = weight_pair * x
        faded = fade_pair * grad
        for_level[:, lanes] = weighted * leave - faded * entering[:, lanes]
        sums[0:1, lanes] = jnp.sum(weighted * leave, axis=0, keepdims=True)
        dskip_ref[:, lanes] += jnp.sum(x * grad, axis=0, keepdims=True)
        faded_low = faded.astype(BF16)
        d_b += mm(weighted.astype(BF16), old_back[:, lanes], ((1,), (1,)))
        d_c += mm(faded_low, kept[:, lanes], ((1,), (1,)))
        back[:, lanes] = back[:, lanes] * pair_of(last, first, low_half) + mm(by_state, faded_low)
    all_pairs = mixed_grads[...]
    db_ref[...] = d_b + mm(all_pairs.T.astype(BF16), rows_c)
    dc_ref[...] = d_c + mm(all_pairs.astype(BF16), rows_b)
    width = x_ref.shape[1]
    chooser = (iota2((width, LANES), 0) // HEAD == iota2((width, LANES), 1)).astype(BF16)
    dstep_ref[...] = head_sums(for_step[...], chooser)
    sums[1:2, :] = at_last
    whole = head_sums(sums[...], chooser)
    d_level = head_sums(for_level[...], chooser) - left[...] + right[...].T
    final = -whole[0:1, :] - last * whole[1:2, :]
    d_level = d_level + jnp.where(iota2((BLOCK, 1), 0) == BLOCK - 1, final, 0.0)
    tri = (at_row <= at_col).astype(F32)
    dlam_ref[...] = mm_exact(tri, d_level)


def scan_backward(x, rows_b, rows_c, lam, step, skip, grad, kept):
    tokens, width = x.shape
    heads = width // HEAD
    count = tokens // BLOCK
    by_block = lambda i: (count - 1 - i, 0)
    return pl.pallas_call(
        functools.partial(backward_kernel, heads),
        grid=(count,),
        in_specs=[
            pl.BlockSpec((BLOCK, width), by_block),
            pl.BlockSpec((BLOCK, STATE), by_block),
            pl.BlockSpec((BLOCK, STATE), by_block),
            pl.BlockSpec((BLOCK, LANES), by_block),
            pl.BlockSpec((BLOCK, LANES), by_block),
            pl.BlockSpec((1, width), lambda i: (0, 0)),
            pl.BlockSpec((BLOCK, width), by_block),
            pl.BlockSpec((1, STATE, width), lambda i: (count - 1 - i, 0, 0)),
        ],
        out_specs=[
            pl.BlockSpec((BLOCK, width), by_block),
            pl.BlockSpec((BLOCK, STATE), by_block),
            pl.BlockSpec((BLOCK, STATE), by_block),
            pl.BlockSpec((BLOCK, LANES), by_block),
            pl.BlockSpec((BLOCK, LANES), by_block),
            pl.BlockSpec((1, width), lambda i: (0, 0)),
        ],
        out_shape=[
            jax.ShapeDtypeStruct((tokens, width), F32),
            jax.ShapeDtypeStruct((tokens, STATE), F32),
            jax.ShapeDtypeStruct((tokens, STATE), F32),
            jax.ShapeDtypeStruct((tokens, LANES), F32),
            jax.ShapeDtypeStruct((tokens, LANES), F32),
            jax.ShapeDtypeStruct((1, width), F32),
        ],
        scratch_shapes=[
            pltpu.VMEM((STATE, width), F32),
            pltpu.VMEM((BLOCK, BLOCK), F32),
            pltpu.VMEM((BLOCK, width), F32),
            pltpu.VMEM((BLOCK, width), F32),
            pltpu.VMEM((BLOCK, LANES), F32),
            pltpu.VMEM((LANES, BLOCK), F32),
            pltpu.VMEM((8, width), F32),
        ],
        compiler_params=pltpu.CompilerParams(vmem_limit_bytes=32 * 1024 * 1024),
        cost_estimate=pl.CostEstimate(
            flops=2 * tokens * width * (4 * BLOCK + 5 * STATE),
            bytes_accessed=tokens * width * 10,
            transcendentals=tokens * heads * BLOCK,
        ),
        name="scan_backward",
    )(x, rows_b, rows_c, lam, step, skip, grad, kept)


def conv_taps(array, taps, weight):
    tokens = array.shape[0]
    padded = jnp.pad(array, ((taps - 1, 0), (0, 0)))
    return sum(weight[k] * padded[k : k + tokens] for k in range(taps))


def silu_slope(v):
    s = jax.nn.sigmoid(v)
    return s * (1.0 + v * (1.0 - s))


def on_device(
    hidden,
    cotangent,
    seq_lens,
    norm_gain,
    in_weight,
    conv_weight,
    conv_bias,
    dt_bias,
    a_log,
    d_skip,
    gate_gain,
    out_weight,
):
    n_ctx, n_fsdp = lax.axis_size("ctx"), lax.axis_size("fsdp")
    me, shard = lax.axis_index("ctx"), lax.axis_index("fsdp")
    taps = conv_weight.shape[0]
    heads_all = dt_bias.shape[0] * n_fsdp
    inner = out_weight.shape[0] * n_fsdp
    heads, width = heads_all // n_ctx, inner // n_ctx
    model = hidden.shape[2]
    conv_width = width + 2 * STATE
    columns = width + conv_width + LANES
    x_at, bc_at, dt_at = inner, 2 * inner, 2 * inner + 2 * STATE

    small = (norm_gain, conv_weight.reshape(-1), conv_bias, dt_bias, a_log, d_skip, gate_gain)
    cuts = [0]
    for part in small:
        cuts.append(cuts[-1] + part.shape[0])
    packed = lax.all_gather(jnp.concatenate(small), "fsdp", axis=0)
    parts = [packed[:, cuts[i] : cuts[i + 1]] for i in range(len(small))]
    gain_norm = parts[0].reshape(-1).astype(F32)
    taps_all = jnp.moveaxis(parts[1].reshape(n_fsdp, taps, -1), 0, 1).reshape(taps, -1)
    bias_all = parts[2].reshape(-1)

    def own(vector, size):
        return lax.dynamic_slice_in_dim(vector, me * size, size, axis=-1)

    def own_channels(vector):
        return jnp.concatenate(
            [own(vector[..., :inner], width), vector[..., inner:]], axis=-1
        ).astype(F32)

    weight_conv, bias_conv = own_channels(taps_all), own_channels(bias_all)
    bias_step = own(parts[3].reshape(-1), heads).astype(F32)
    rate = jnp.exp(own(parts[4].reshape(-1), heads).astype(F32))
    skip = own(parts[5].reshape(-1), heads).astype(F32)
    gain_gate = own(parts[6].reshape(-1), width).astype(F32)

    resid_low = lax.all_gather(hidden[0], "ctx", axis=0, tiled=True)
    own_columns = jnp.concatenate(
        [
            lax.dynamic_slice_in_dim(in_weight, me * width, width, axis=1),
            lax.dynamic_slice_in_dim(in_weight, x_at + me * width, width, axis=1),
            in_weight[:, bc_at:dt_at],
            lax.dynamic_slice_in_dim(in_weight, dt_at + me * heads, heads, axis=1),
            jnp.zeros((in_weight.shape[0], LANES - heads), BF16),
        ],
        axis=1,
    )
    weight_in = lax.all_gather(own_columns, "fsdp", axis=0, tiled=True)
    upstream = lax.all_gather(cotangent[0], "ctx", axis=0, tiled=True)
    piece = out_weight.shape[0] // n_ctx
    there = [(c * n_fsdp + f, f * n_ctx + c) for c in range(n_ctx) for f in range(n_fsdp)]
    back_again = [(b, a) for a, b in there]
    own_rows = lax.ppermute(
        lax.dynamic_slice_in_dim(out_weight, me * piece, piece, axis=0), ("ctx", "fsdp"), there
    )
    weight_out = lax.all_gather(own_rows, "fsdp", axis=0, tiled=True)

    tokens = resid_low.shape[0]
    valid = (jnp.arange(tokens, dtype=jnp.int32) < seq_lens[0]).astype(F32)[:, None]
    resid = resid_low.astype(F32)
    scale_in = lax.rsqrt(jnp.mean(resid * resid, axis=1, keepdims=True) + EPS)
    normed = (resid * scale_in * gain_norm).astype(BF16)
    projected = mm(normed, weight_in).astype(BF16)
    gate_raw = projected[:, :width].astype(F32)
    conv_in = projected[:, width : width + conv_width].astype(F32)
    step_raw = projected[:, width + conv_width : width + conv_width + heads].astype(F32)

    convolved = bias_conv + conv_taps(conv_in, taps, weight_conv)
    activated = jax.nn.silu(convolved).astype(BF16)
    values = activated[:, :width]
    rows_b = activated[:, width : width + STATE]
    rows_c = activated[:, width + STATE :]
    step = jax.nn.softplus(step_raw + bias_step) * valid
    lam = step * rate
    in_lanes = lambda a: jnp.pad(a, ((0, 0), (0, LANES - heads)))
    step_lanes, lam_lanes = in_lanes(step), in_lanes(lam)
    skip_wide = jnp.repeat(skip, HEAD)[None, :]
    mixed_ssd, kept = scan_forward(values, rows_b, rows_c, lam_lanes, step_lanes, skip_wide)

    gate = jax.nn.silu(gate_raw)
    gated = mixed_ssd * gate
    d_mixed = upstream * valid.astype(BF16)
    d_yn = mm(d_mixed, weight_out, ((1,), (1,)))
    d_gain = gain_gate * d_yn
    stats = jnp.stack([jnp.sum(gated * gated, axis=1), jnp.sum(gated * d_gain, axis=1)])
    stats = lax.psum(stats, "ctx") / inner
    scale_gate = lax.rsqrt(stats[0] + EPS)[:, None]
    normed_gate = (gated * scale_gate * gain_gate).astype(BF16)
    mixed = lax.psum_scatter(
        mm(normed_gate, weight_out).astype(BF16), "ctx", scatter_dimension=0, tiled=True
    )
    own_tokens = lambda a: lax.dynamic_slice_in_dim(a, me * hidden.shape[1], hidden.shape[1], axis=0)
    layer_out = (hidden[0].astype(F32) + own_tokens(valid) * mixed.astype(F32)).astype(BF16)

    grad_out = mm(normed_gate, d_mixed, ((0,), (0,))).astype(BF16)
    grad_out = lax.psum_scatter(grad_out, "fsdp", scatter_dimension=0, tiled=True)
    grad_gain_gate = jnp.sum(d_yn * gated * scale_gate, axis=0)
    d_gated = scale_gate * d_gain - gated * (scale_gate**3 * stats[1][:, None])
    d_ssd = (d_gated * gate).astype(BF16)
    d_gate_raw = d_gated * mixed_ssd * silu_slope(gate_raw)

    d_x, d_b, d_c, d_step, d_lam, d_skip_lanes = scan_backward(
        values, rows_b, rows_c, lam_lanes, step_lanes, skip_wide, d_ssd, kept
    )
    d_step, d_lam = d_step[:, :heads], d_lam[:, :heads]
    grad_skip = jnp.sum(d_skip_lanes.reshape(heads, HEAD), axis=1)
    d_raw = valid * (d_step + d_lam * rate) * jax.nn.sigmoid(step_raw + bias_step)
    grad_bias_step = jnp.sum(d_raw, axis=0)
    grad_log = jnp.sum(d_lam * lam, axis=0)
    d_conv = jnp.concatenate([d_x, d_b, d_c], axis=1) * silu_slope(convolved)
    grad_bias_conv = jnp.sum(d_conv, axis=0)
    padded_in = jnp.pad(conv_in, ((taps - 1, 0), (0, 0)))
    grad_taps = jnp.stack(
        [jnp.sum(d_conv * padded_in[k : k + tokens], axis=0) for k in range(taps)]
    )
    padded_back = jnp.pad(d_conv, ((0, taps - 1), (0, 0)))
    d_conv_in = sum(
        weight_conv[k] * padded_back[taps - 1 - k : taps - 1 - k + tokens] for k in range(taps)
    )
    d_projected = jnp.concatenate([d_gate_raw, d_conv_in, in_lanes(d_raw)], axis=1).astype(BF16)
    grad_in = mm(normed, d_projected, ((0,), (0,))).astype(BF16)
    grad_in = lax.psum_scatter(grad_in, "fsdp", scatter_dimension=0, tiled=True)
    d_normed = mm(d_projected, weight_in, ((1,), (1,))).astype(BF16)
    d_normed = lax.psum_scatter(d_normed, "ctx", scatter_dimension=0, tiled=True).astype(F32)

    resid_own = hidden[0].astype(F32)
    scale_own = own_tokens(scale_in)
    f = gain_norm * d_normed
    d_resid = scale_own * f - resid_own * scale_own**3 * jnp.mean(
        resid_own * f, axis=1, keepdims=True
    )
    hidden_grad = (cotangent[0].astype(F32) + d_resid).astype(BF16)
    grad_gain_norm = jnp.sum(d_normed * resid_own * scale_own, axis=0)

    def placed(value, total):
        start = me * value.shape[-1]
        return lax.dynamic_update_slice_in_dim(
            jnp.zeros(value.shape[:-1] + (total,), F32), value, start, axis=-1
        )

    def placed_channels(value):
        return jnp.concatenate([placed(value[..., :width], inner), value[..., width:]], axis=-1)

    small_grads = (
        grad_gain_norm,
        placed_channels(grad_taps).reshape(-1),
        placed_channels(grad_bias_conv),
        placed(grad_bias_step, heads_all),
        placed(grad_log, heads_all),
        placed(grad_skip, heads_all),
        placed(grad_gain_gate, inner),
    )
    flat = lax.psum(jnp.concatenate(small_grads), ("ctx", "fsdp"))
    outs, at = [], 0
    for value in small_grads:
        outs.append(flat[at : at + value.shape[0]])
        at += value.shape[0]

    def own_shard(vector):
        size = vector.shape[-1] // n_fsdp
        return lax.dynamic_slice_in_dim(vector, shard * size, size, axis=-1)

    conv_total = inner + 2 * STATE
    pieces = lax.all_gather(grad_in, "ctx", axis=0).astype(F32)
    in_order = lambda a: jnp.moveaxis(a, 0, 1).reshape(a.shape[1], -1)
    grad_in_weight = jnp.concatenate(
        [
            in_order(pieces[:, :, :width]),
            in_order(pieces[:, :, width : 2 * width]),
            jnp.sum(pieces[:, :, 2 * width : width + conv_width], axis=0),
            in_order(pieces[:, :, width + conv_width : width + conv_width + heads]),
        ],
        axis=1,
    )
    grad_out = lax.ppermute(grad_out, ("ctx", "fsdp"), back_again)
    grad_out_weight = lax.all_gather(grad_out, "ctx", axis=0, tiled=True).astype(F32)
    return (
        layer_out[None],
        hidden_grad[None],
        own_shard(outs[0]),
        grad_in_weight,
        own_shard(outs[1].reshape(taps, conv_total)),
        own_shard(outs[2]),
        own_shard(outs[3]),
        own_shard(outs[4]),
        own_shard(outs[5]),
        own_shard(outs[6]),
        grad_out_weight,
    )


def solution(mesh):
    tokens, rows, flat = P("fsdp", "ctx", None), P("fsdp", None), P("fsdp")
    taps = P(None, "fsdp")
    return jax.shard_map(
        on_device,
        mesh=mesh,
        in_specs=(tokens, tokens, flat, flat, rows, taps, flat, flat, flat, flat, flat, rows),
        out_specs=(tokens, tokens, flat, rows, taps, flat, flat, flat, flat, flat, rows),
        check_vma=False,
    )
```

time: 2930 us -> 946 us (0.32)
  waiting for transfers between devices: 2290 us -> 636 us
  blocking collectives: 214 us -> 55.1 us
  matrix products: 236 us -> 80.2 us
  other arithmetic: 99.8 us -> 52.2 us
  Pallas kernels: 0 us -> 45.7 us
    reduce_scatter x2 -> x4, waiting for transfers between devices: 1460 us -> 257 us  [the longest x1 169 us: on_device(): grad_in = lax.psum_scatter(grad_in, 'fsdp', scatter_dimension=0, tiled=True)]
    all_gather x4 -> x6, waiting for transfers between devices: 690 us -> 253 us  [the longest x1 127 us: on_device(): weight_in = lax.all_gather(own_columns, 'fsdp', axis=0, tiled=True)]
    dot_general x21 -> x6, matrix products: 236 us -> 80.2 us  [mm(): lax.dot_general(a, b, (contract, ((), ())), preferred_element_type=F32)]
    all_gather x3 -> x0, blocking collectives: 100 us -> none  [the longest x1 67.9 us: on_device(): lax.all_gather(conv_weight, 'fsdp', axis=1, tiled=True)]
    unnamed x3 -> x1, blocking collectives: 103 us -> 48.9 us
    pallas_call x0 -> x2, Pallas kernels: none -> 45.7 us  [the longest x1 32.3 us: scan_backward(): pl.pallas_call(functools.partial(backward_kernel, heads), grid=(count,),...]
  transfers between devices with their start and end apart: 10 -> 13, of which waited for: 7 -> 8; matrix products, arithmetic and copies ran while one was open for 10% -> 12% of each run, Pallas kernels for 0% -> 5%
where the time goes in v1:
time: 946 us; the launch traced here: 935 us
  waiting for transfers between devices  636 us (67%)
  matrix products  80.2 us (8%)
  blocking collectives  55.1 us (6%)
  other arithmetic  52.2 us (6%)
  Pallas kernels  45.7 us (5%)
  local copies, waits for them, and re-layouts  41.6 us (4%)
  between operations  16.4 us (2%)
    reduce_scatter x1, waiting for transfers between devices, on_device(): grad_in = lax.psum_scatter(grad_in, 'fsdp', scatter_dimension=0, tiled=True)  169 us
    all_gather x1, waiting for transfers between devices, on_device(): weight_in = lax.all_gather(own_columns, 'fsdp', axis=0, tiled=True)  127 us
    psum x1, waiting for transfers between devices, on_device(): flat = lax.psum(jnp.concatenate(small_grads), ('ctx', 'fsdp'))  124 us
    dot_general x6, matrix products, mm(): lax.dot_general(a, b, (contract, ((), ())), preferred_element_type=F32)  80.2 us
    all_gather x1, waiting for transfers between devices, on_device(): weight_out = lax.all_gather(own_rows, 'fsdp', axis=0, tiled=True)  71.9 us
    unnamed x1, blocking collectives  48.9 us
    reduce_scatter x1, waiting for transfers between devices, on_device(): lax.psum_scatter(mm(normed_gate, weight_out).astype(BF16), 'ctx', scatter...  47.5 us
    reduce_scatter x1, waiting for transfers between devices, on_device(): lax.psum_scatter(d_normed, 'ctx', scatter_dimension=0, tiled=True)  40.5 us
  transfers between devices with their start and end apart: 13, of which 8 were waited for; matrix products, arithmetic and copies ran while one was open for 12% of the time, Pallas kernels for 5%

profile of v1, /device:TPU:17, one launch (start us, length us, event | category | flops | bytes accessed | tf_op | source)
XLA Modules:
  0.0 934.8 jit_solution(12683642223279124311)
XLA Ops:
  8.1 1.1 dynamic-slice_dynamic-update-slice_fusion.1
  9.2 1.1 dynamic-slice_dynamic-update-slice_fusion
  10.2 0.9 slice_dynamic-update-slice_fusion
  11.9 1.0 copy-done.13
  13.8 4.4 collective-permute-start
  20.0 48.9 %all-reduce.5 = bf16[28096]{0:T(1024)(128)(2,1)S(1)} all-reduce(bf16[28096]{0:T(1024)(128)(2,1)S(1)} %dynamic-update-slice), channel_id=2, replica_groups=mesh['ctx'=4,'fsdp'=8] {'fsdp'}, use_global_device_ids=true, to_apply=%add.5 | all-reduce | flops 28096 | bytes 112384
  69.2 0.8 copy-done.16
  72.0 3.1 fusion.1
  75.1 127.1 %all-gather.11.cloned.1.call-done = bf16[2048,2432]{0,1:T(8,128)(2,1)} async-done(((bf16[256,2432]{0,1:T(8,128)(2,1)}), bf16[2048,2432]{0,1:T(8,128)(2,1)}) %all-gather.11.cloned.1.call-update) | async-done | bytes 9961488 | tf_op jit(solution)/shard_map/all_gather | solution.py:341
  202.2 15.1 %convolution_convert_fusion.1 = bf16[1024,2432]{1,0:T(8,128)(2,1)S(1)} fusion(bf16[2048,2432]{0,1:T(8,128)(2,1)} %all-gather.11.cloned.1.call-done, bf16[1,1024,2048]{2,1,0:T(8,128)(2,1)} %all-gather.17.cloned.1.call-done, f32[2048]{0:T(1024)S(1)} %bitcast.66, f32[1024]{0:T(1024)S(1)} %add_rsqrt_fusion), kind=kOutput, calls=%fused_computation.12 | convolution fusion | flops 10211426304 | bytes 19148800 | tf_op jit(solution)/shard_map/dot_general | solution.py:20
  217.6 5.1 multiply_convert_fusion
  223.5 13.4 %scan_forward.1 = (f32[1024,1024]{1,0:T(8,128)S(1)}, bf16[4,128,1024]{2,1,0:T(8,128)(2,1)S(1)}) custom-call(bf16[1024,1024]{1,0:T(8,128)(2,1)S(1)} %slice.210.x_ref, bf16[1024,128]{1,0:T(8,128)(2,1)S(1)} %get-tuple-element.58.b_ref, bf16[1024,128]{1,0:T(8,128)(2,1)S(1)} %get-tuple-element.57.c_ref, f32[1024,128]{1,0:T(8,128)S(1)} %pad.21.lam_ref, ...), custom_call_target="tpu_custom_call" | custom-call | flops 1610612736 | bytes 6291456 | tf_op jit(solution)/shard_map/scan_forward/pallas_call | solution.py:81
  236.9 2.0 copy-done.2
  239.6 1.0 copy-done.5
  240.6 71.9 %all-gather.13.cloned.1.call-done = bf16[1024,2048]{1,0:T(8,128)(2,1)} async-done(((bf16[128,2048]{1,0:T(8,128)(2,1)}), bf16[1024,2048]{1,0:T(8,128)(2,1)}) %all-gather.13.cloned.1.call-update) | async-done | bytes 4194320 | tf_op jit(solution)/shard_map/all_gather | solution.py:349
  312.5 13.5 %multiply_reduce_fusion.6 = (f32[1024]{0:T(1024)S(1)}, f32[1024]{0:T(1024)S(1)}, f32[1024,1024]{1,0:T(8,128)}, f32[1024,1024]{1,0:T(8,128)}) fusion(f32[1024]{0:T(1024)S(1)} %dynamic-slice_convert_fusion, f32[1024,1024]{1,0:T(8,128)} %copy-done.2, bf16[1024,2432]{1,0:T(8,128)(2,1)} %copy-done.8, bf16[1024,2048]{1,0:T(8,128)(2,1)} %all-gather.13.cloned.1.call-done, ...), kind=kOutput, calls=%fused_computation.42 | convolution fusion | flops 4308596736 | bytes 23083008 | tf_op jit(solution)/shard_map/dot_general | solution.py:20
  326.0 6.2 psum.14
  332.3 10.3 %convolution_convert_fusion.3 = bf16[1024,2048]{1,0:T(8,128)(2,1)} fusion(bf16[1,1024,2048]{2,1,0:T(8,128)(2,1)} %all-gather.19.cloned.1.call-done, bf16[1024]{0:T(1024)(128)(2,1)S(1)} %fusion.39, f32[1024,1024]{1,0:T(8,128)} %get-tuple-element.46, f32[1024]{0:T(1024)S(1)} %bitcast.70, f32[1024]{0:T(1024)S(1)} %dynamic-slice_convert_fusion), kind=kOutput, calls=%fused_computation.44 | convolution fusion | flops 4302307328 | bytes 12593152 | tf_op jit(solution)/shard_map/dot_general | solution.py:20
  342.7 7.0 fusion.12
  349.8 32.3 %scan_backward.1 = (f32[1024,1024]{1,0:T(8,128)S(1)}, f32[1024,128]{1,0:T(8,128)S(1)}, f32[1024,128]{1,0:T(8,128)S(1)}, f32[1024,128]{1,0:T(8,128)S(1)}, f32[1024,128]{1,0:T(8,128)S(1)}, /*index=5*/f32[1,1024]{1,0:T(1,128)S(1)}) custom-call(bf16[1024,1024]{1,0:T(8,128)(2,1)S(1)} %slice.210.x_ref, bf16[1024,128]{1,0:T(8,128)(2,1)S(1)} %copy-done.4, ...), custom_call_target="tpu_custom_call" | custom-call | flops 3489660928 | bytes 10485760 | tf_op jit(solution)/shard_map/scan_backward/pallas_call | solution.py:222
  382.0 1.6 fusion.45
  383.6 6.7 fusion.44
  390.3 2.6 add_convert_fusion
  393.0 1.5 copy-done.12
  394.4 14.9 %convolution_convert_fusion.2 = bf16[1024,2048]{1,0:T(8,128)(2,1)} fusion(bf16[2048,2432]{0,1:T(8,128)(2,1)} %all-gather.11.cloned.1.call-done, bf16[1024,16]{1,0:T(8,128)(2,1)S(1)} %get-tuple-element.44, bf16[1024,1280]{1,0:T(8,128)(2,1)S(1)} %add_convert_fusion, bf16[1024,1024]{1,0:T(8,128)(2,1)S(1)} %get-tuple-element.49), kind=kOutput, calls=%fused_computation.43 | convolution fusion | flops 10222567424 | bytes 18907136 | tf_op jit(solution)/shard_map/dot_general | solution.py:20
  409.4 1.7 copy-done.15
  411.1 16.4 %convolution_convert_fusion = bf16[2048,2432]{1,0:T(8,128)(2,1)} fusion(bf16[1,1024,2048]{2,1,0:T(8,128)(2,1)} %all-gather.17.cloned.1.call-done, f32[2048]{0:T(1024)S(1)} %bitcast.67, f32[1024]{0:T(1024)S(1)} %add_rsqrt_fusion, bf16[1024,16]{1,0:T(8,128)(2,1)S(1)} %get-tuple-element.44, bf16[1024,1280]{1,0:T(8,128)(2,1)} %copy-done.12, ...), kind=kOutput, calls=%fused_computation | convolution fusion | flops 10233839616 | bytes 18919424 | tf_op jit(solution)/shard_map/dot_general | solution.py:20
  427.8 10.1 %convolution_convert_fusion.4 = bf16[1024,2048]{1,0:T(8,128)(2,1)} fusion(bf16[1024,2048]{1,0:T(8,128)(2,1)} %all-gather.13.cloned.1.call-done, f32[1024,1024]{1,0:T(8,128)} %get-tuple-element.46, f32[1024]{0:T(1024)S(1)} %bitcast.73, f32[1024]{0:T(1024)S(1)} %dynamic-slice_convert_fusion), kind=kOutput, calls=%fused_computation.45 | convolution fusion | flops 4300210176 | bytes 12591104 | tf_op jit(solution)/shard_map/dot_general | solution.py:20
  438.8 0.8 reduce.11
  440.7 2.6 collective-permute-start.1
  443.3 40.5 %reduce-scatter.7.cloned.1.call-done = bf16[256,2048]{1,0:T(8,128)(2,1)} async-done(((bf16[1024,2048]{1,0:T(8,128)(2,1)}), bf16[256,2048]{1,0:T(8,128)(2,1)}) %reduce-scatter.7.cloned.1.call-update) | async-done | bytes 1048592 | tf_op jit(solution)/shard_map/reduce_scatter | solution.py:417
  483.9 2.0 fusion.22
  487.2 169.3 %reduce-scatter.9.cloned.1.call-done = bf16[256,2432]{1,0:T(8,128)(2,1)} async-done(((bf16[2048,2432]{1,0:T(8,128)(2,1)}), bf16[256,2432]{1,0:T(8,128)(2,1)}) %reduce-scatter.9.cloned.1.call-update) | async-done | bytes 1245200 | tf_op jit(solution)/shard_map/reduce_scatter | solution.py:415
  656.6 47.5 %reduce-scatter.5.cloned.1.call-done = bf16[256,2048]{1,0:T(8,128)(2,1)} async-done(((bf16[1024,2048]{1,0:T(8,128)(2,1)}), bf16[256,2048]{1,0:T(8,128)(2,1)}) %reduce-scatter.5.cloned.1.call-update) | async-done | bytes 1048592 | tf_op jit(solution)/shard_map/reduce_scatter | solution.py:382
  704.1 3.5 fusion.29
  707.6 123.8 %all-reduce.8.cloned.1.call-done = f32[28096]{0:T(1024)} async-done(((f32[28096]{0:T(1024)}), f32[28096]{0:T(1024)}) %all-reduce.8.cloned.1.call-update) | async-done | bytes 112400 | tf_op jit(solution)/shard_map/psum | solution.py:446
  831.4 0.9 slice.229
  832.3 0.9 fusion.48
  834.9 0.7 slice.230
  836.3 0.8 slice.234
  839.8 17.4 %all-gather.15.cloned.1.call-done = bf16[512,2048]{1,0:T(8,128)(2,1)} async-done(((bf16[128,2048]{1,0:T(8,128)(2,1)}), bf16[512,2048]{1,0:T(8,128)(2,1)}) %all-gather.15.cloned.1.call-update) | async-done | bytes 2097168 | tf_op jit(solution)/shard_map/all_gather | solution.py:469
  857.1 4.1 convert_element_type.154
  861.2 36.5 %all-gather.21.cloned.1.call-done = bf16[1024,2432]{1,0:T(8,128)(2,1)} async-done(((bf16[256,2432]{1,0:T(8,128)(2,1)}), bf16[1024,2432]{1,0:T(8,128)(2,1)}) %all-gather.21.cloned.1.call-update) | async-done | bytes 4980752 | tf_op jit(solution)/shard_map/all_gather | solution.py:457
  897.7 3.1 bitcast_convert_fusion
  900.8 4.5 slice_bitcast_fusion.1
  905.4 5.4 copy.44
  910.8 5.4 copy.45
  916.5 11.3 %pad_maximum_fusion = f32[256,8512]{0,1:T(8,128)} fusion(f32[256,64]{0,1:T(8,128)S(1)} %bitcast.64, f32[256,256]{0,1:T(8,128)S(1)} %copy.47, f32[256,4096]{0,1:T(8,128)} %bitcast.63, f32[256,4096]{0,1:T(8,128)} %bitcast.62), kind=kLoop, calls=%fused_computation.5 | loop fusion | flops 6537216 | bytes 17432576 | tf_op jit(solution)/shard_map/concatenate | solution.py:459
  (168 shorter events, 16.0 us)
Async XLA Ops:
  7.2 6.5 copy-start
  7.2 11.1 %copy-start.24 = (u32[32]{0:T(128)S(1)}, u32[32]{0:T(128)}, u32[]{:S(2)}) copy-start(u32[32]{0:T(128)} %constant.85) | copy-start | bytes 388
  7.2 11.0 %copy-start.17 = (bf16[4,544]{1,0:T(4,128)(2,1)S(1)}, bf16[4,544]{1,0:T(4,128)(2,1)}, u32[]{:S(2)}) copy-start(bf16[4,544]{1,0:T(4,128)(2,1)} %param.17) | copy-start | bytes 13060
  7.2 12.3 %copy-start.20 = (bf16[256]{0:T(256)(128)(2,1)S(1)}, bf16[256]{0:T(256)(128)(2,1)}, u32[]{:S(2)}) copy-start(bf16[256]{0:T(256)(128)(2,1)} %param.15) | copy-start | bytes 1540
  7.2 12.3 %copy-start.18 = (bf16[544]{0:T(1024)(128)(2,1)S(1)}, bf16[544]{0:T(1024)(128)(2,1)}, u32[]{:S(2)}) copy-start(bf16[544]{0:T(1024)(128)(2,1)} %param.18) | copy-start | bytes 3268
  7.2 12.3 %copy-start.21 = (bf16[8]{0:T(256)(128)(2,1)S(1)}, bf16[8]{0:T(256)(128)(2,1)}, u32[]{:S(2)}) copy-start(bf16[8]{0:T(256)(128)(2,1)} %param.19) | copy-start | bytes 52
  7.2 12.3 %copy-start.22 = (bf16[8]{0:T(256)(128)(2,1)S(1)}, bf16[8]{0:T(256)(128)(2,1)}, u32[]{:S(2)}) copy-start(bf16[8]{0:T(256)(128)(2,1)} %param.20) | copy-start | bytes 52
  7.3 12.3 %copy-start.23 = (bf16[8]{0:T(256)(128)(2,1)S(1)}, bf16[8]{0:T(256)(128)(2,1)}, u32[]{:S(2)}) copy-start(bf16[8]{0:T(256)(128)(2,1)} %param.21) | copy-start | bytes 52
  7.3 12.3 %copy-start.19 = (bf16[512]{0:T(512)(128)(2,1)S(1)}, bf16[512]{0:T(512)(128)(2,1)}, u32[]{:S(2)}) copy-start(bf16[512]{0:T(512)(128)(2,1)} %param.22) | copy-start | bytes 3076
  7.3 64.7 %all-gather.17.cloned.1.call-start = ((), (), s32[]{:S(2)}) async-start(), calls=%async_computation.12 | async-start | bytes 5242880 | tf_op jit(solution)/shard_map/all_gather | solution.py:330
  8.0 194.1 %all-gather.11.cloned.1.call-start = ((), (), s32[]{:S(2)}) async-start(), calls=%async_computation.4 | async-start | bytes 11206656 | tf_op jit(solution)/shard_map/all_gather | solution.py:341
  11.9 1.0 copy-start.13
  12.9 227.7 %all-gather.19.cloned.1.call-start = ((), (), s32[]{:S(2)}) async-start(), calls=%async_computation.13 | async-start | bytes 5242880 | tf_op jit(solution)/shard_map/all_gather | solution.py:342
  13.7 298.8 %all-gather.13.cloned.1.call-start = ((), (), s32[]{:S(2)}) async-start(), calls=%async_computation.5 | async-start | bytes 4718592 | tf_op jit(solution)/shard_map/all_gather | solution.py:349
  13.8 55.4 %collective-permute-start = (bf16[128,2048]{1,0:T(8,128)(2,1)S(1)}, bf16[128,2048]{1,0:T(8,128)(2,1)S(1)}, u32[]{:S(2)}, u32[]{:S(2)}) collective-permute-start(bf16[128,2048]{1,0:T(8,128)(2,1)S(1)} %constant_dynamic-slice_fusion.1), channel_id=1, source_target_pairs={{0,0},{1,4},{2,8},{3,12},{4,16},{5,20},{6,24},{7,28},{8,1},{9,5},{... | collective-permute-start | bytes 1572872 | tf_op jit(solution)/shard_map/ppermute | solution.py:346
  69.2 0.8 copy-start.16
  70.0 370.7 %reduce-scatter.11.cloned.1.call-start = ((), (), s32[]{:S(2)}) async-start(), calls=%async_computation.10 | async-start | bytes 4718592 | tf_op jit(solution)/shard_map/reduce_scatter | solution.py:389
  217.2 5.8 copy-start.8
  217.6 5.1 copy-start.7
  236.9 2.0 copy-start.2
  238.9 0.7 copy-start.3
  239.6 1.0 copy-start.5
  342.6 141.3 %reduce-scatter.7.cloned.1.call-start = ((), (), s32[]{:S(2)}) async-start(), calls=%async_computation.7 | async-start | bytes 5242880 | tf_op jit(solution)/shard_map/reduce_scatter | solution.py:417
  342.6 7.1 copy-start.4
  342.6 7.1 copy-start.6
  349.7 43.2 %copy-start.14 = (bf16[1024,1024]{1,0:T(8,128)(2,1)}, bf16[1024,1024]{1,0:T(8,128)(2,1)S(1)}, u32[]{:S(2)}) copy-start(bf16[1024,1024]{1,0:T(8,128)(2,1)S(1)} %get-tuple-element.49) | copy-start | bytes 6291460
  349.7 33.9 %slice-start = ((s8[5242880]{0:T(1024)(128)(4,1)}), s8[4194304]{0:T(1024)(128)(4,1)S(1)}, s32[]{:S(2)}) async-start(s8[5242880]{0:T(1024)(128)(4,1)} %bitcast.60), calls=%async_computation.15 | async-start | bytes 8388608
  349.8 33.8 %slice-start.1 = ((s8[5242880]{0:T(1024)(128)(4,1)}), s8[1048576]{0:T(1024)(128)(4,1)S(1)}, s32[]{:S(2)}) async-start(s8[5242880]{0:T(1024)(128)(4,1)} %bitcast.60), calls=%async_computation.16 | async-start | bytes 2097152
  392.9 1.5 copy-start.12
  409.4 1.8 copy-start.15
  409.4 247.1 %reduce-scatter.9.cloned.1.call-start = ((), (), s32[]{:S(2)}) async-start(), calls=%async_computation.9 | async-start | bytes 11206656 | tf_op jit(solution)/shard_map/reduce_scatter | solution.py:415
  427.5 276.5 %reduce-scatter.5.cloned.1.call-start = ((), (), s32[]{:S(2)}) async-start(), calls=%async_computation.6 | async-start | bytes 5242880 | tf_op jit(solution)/shard_map/reduce_scatter | solution.py:382
  437.9 46.0 %copy-start.9 = (bf16[1,256,2048]{2,1,0:T(8,128)(2,1)S(1)}, bf16[1,256,2048]{2,1,0:T(8,128)(2,1)}, u32[]{:S(2)}) copy-start(bf16[1,256,2048]{2,1,0:T(8,128)(2,1)} %param.12) | copy-start | bytes 3145732
  437.9 266.1 %copy-start.11 = (bf16[1,256,2048]{2,1,0:T(8,128)(2,1)S(1)}, bf16[1,256,2048]{2,1,0:T(8,128)(2,1)}, u32[]{:S(2)}) copy-start(bf16[1,256,2048]{2,1,0:T(8,128)(2,1)} %param.13) | copy-start | bytes 3145732
  437.9 393.4 %all-reduce.8.cloned.1.call-start = ((), (), s32[]{:S(2)}) async-start(), calls=%async_computation.8 | async-start | bytes 229376 | tf_op jit(solution)/shard_map/psum | solution.py:446
  440.7 45.9 %collective-permute-start.1 = (bf16[128,2048]{1,0:T(8,128)(2,1)}, bf16[128,2048]{1,0:T(8,128)(2,1)}, u32[]{:S(2)}, u32[]{:S(2)}) collective-permute-start(bf16[128,2048]{1,0:T(8,128)(2,1)} %reduce-scatter.11.cloned.1.call-done), channel_id=1, source_target_pairs={{0,0},{4,1},{8,2},{12,3},{16,4},{20,5},{24,6},{28,7},{1,8},{5,9},{... | collective-permute-start | bytes 1572872 | tf_op jit(solution)/shard_map/ppermute | solution.py:468
  483.9 220.2 %copy-start.10 = (bf16[256,2048]{1,0:T(8,128)(2,1)S(1)}, bf16[256,2048]{1,0:T(8,128)(2,1)}, u32[]{:S(2)}) copy-start(bf16[256,2048]{1,0:T(8,128)(2,1)} %reduce-scatter.7.cloned.1.call-done) | copy-start | bytes 3145732
  486.6 370.5 %all-gather.15.cloned.1.call-start = ((), (), s32[]{:S(2)}) async-start(), calls=%async_computation.11 | async-start | bytes 2621440 | tf_op jit(solution)/shard_map/all_gather | solution.py:469
  487.2 410.6 %all-gather.21.cloned.1.call-start = ((), (), s32[]{:S(2)}) async-start(), calls=%async_computation.14 | async-start | bytes 6225920 | tf_op jit(solution)/shard_map/all_gather | solution.py:457
  916.5 11.3 %copy-start.1 = (bf16[512,2048]{1,0:T(8,128)(2,1)S(1)}, bf16[512,2048]{1,0:T(8,128)(2,1)}, u32[]{:S(2)}) copy-start(bf16[512,2048]{1,0:T(8,128)(2,1)} %param.23) | copy-start | bytes 6291460
Sparse Core Ops, SparseCore 0:
  9.7 43.5 all-gather.16
  55.9 146.2 all-gather.10
  203.7 34.3 all-gather.18
  240.7 71.7 all-gather.12
  342.7 87.2 reduce-scatter.10
  433.1 50.7 reduce-scatter.6
  487.5 168.9 reduce-scatter.8
  659.6 44.4 reduce-scatter.4
  711.1 120.2 all-reduce.7
  832.9 24.2 all-gather.14
  858.8 38.9 all-gather.20

commit v2 on v1

--- a/solution.py
+++ b/solution.py
@@ -267,6 +267,268 @@
     )(x, rows_b, rows_c, lam, step, skip, grad, kept)
 
 
+MESH = pl.DeviceIdType.MESH
+
+
+def ring_place(index, half):
+    a, b = index // 2, index % 2
+    return a + b * (2 * half - 1 - 2 * a)
+
+
+def ring_index(place, half):
+    b = place // half
+    return 2 * (place + b * (2 * half - 1 - 2 * place)) + b
+
+
+class Ring:
+    def __init__(self, n):
+        self.n, self.half = n, n // 2
+        self.me, self.shard = lax.axis_index("ctx"), lax.axis_index("fsdp")
+        self.place = ring_place(self.shard, self.half)
+
+    def at(self, steps):
+        return ring_index(lax.rem(self.place + steps + 2 * self.n, self.n), self.half)
+
+    def neighbour(self, way):
+        return (self.me, self.at(1 if way == 0 else -1))
+
+
+def gather_kernel(
+    n,
+    n_ctx,
+    hidden,
+    cotangent,
+    in_weight,
+    shared,
+    out_weight,
+    hidden_all,
+    cotangent_all,
+    w_x,
+    w_s,
+    w_z,
+    w_o,
+    local_sem,
+    ring_send,
+    ring_recv,
+    ctx_send,
+    ctx_recv,
+    piece_send,
+    piece_recv,
+):
+    ring = Ring(n)
+    me, shard = ring.me, ring.shard
+    width = w_x.shape[2]
+    inner = width * n_ctx
+    row = me // 2
+    other_core = (me + 1 - 2 * (me % 2), shard)
+    other_row = (me + 2 - 4 * row, shard)
+    piece = w_o.shape[1]
+    sent_as = shard * n_ctx + me
+    piece_to = (sent_as // n, sent_as % n)
+    held_as = me * n + shard
+    piece_from = (held_as % n_ctx, held_as // n_ctx)
+    moves = sent_as != held_as
+
+    barrier = pltpu.get_barrier_semaphore()
+    for device in (other_core, other_row, ring.neighbour(0), ring.neighbour(1)):
+        pl.semaphore_signal(barrier, inc=1, device_id=device, device_id_type=MESH)
+
+    @pl.when(moves)
+    def _():
+        for device in (piece_to, piece_from):
+            pl.semaphore_signal(barrier, inc=1, device_id=device, device_id_type=MESH)
+        pl.semaphore_wait(barrier, 6)
+
+    @pl.when(jnp.logical_not(moves))
+    def _():
+        pl.semaphore_wait(barrier, 4)
+
+    def remote(source, target, send, recv, device):
+        return pltpu.make_async_remote_copy(
+            src_ref=source,
+            dst_ref=target,
+            send_sem=send,
+            recv_sem=recv,
+            device_id=device,
+            device_id_type=MESH,
+        )
+
+    own_x = in_weight.at[:, pl.ds(pl.multiple_of(inner + me * width, LANES), width)]
+    own_z = in_weight.at[:, pl.ds(pl.multiple_of(me * width, LANES), width)]
+    half = width // 2
+    quarter = w_o.shape[2] // 4
+    rows, more = w_x.shape[1] // 2, w_s.shape[1] // 2
+    by_rows = lambda a, way, count, first, size: a.at[
+        pl.ds(way * count, count), pl.ds(first, size)
+    ]
+    x_part = lambda sub: lambda a, way: by_rows(a, way, rows, sub * half, half)
+    s_part = lambda a, way: by_rows(a, way, more, 0, a.shape[1])
+    o_part = lambda sub: lambda a, way: a.at[:, pl.ds((2 * way + sub) * quarter, quarter)]
+    phases = (
+        ((w_s, shared, s_part), (w_x, own_x, x_part(0)), (w_x, own_x, x_part(1))),
+        ((w_z, own_z, x_part(0)), (w_z, own_z, x_part(1))),
+        ((w_o, None, o_part(0)), (w_o, None, o_part(1))),
+    )
+    numbered, count = [], 0
+    for phase in phases:
+        numbered.append([(count + i,) + stream for i, stream in enumerate(phase)])
+        count += len(phase)
+
+    def hop(stream, way, step):
+        number, whole, own, part = stream
+        index = ring.at(-step if way == 0 else step)
+        source = whole.at[index]
+        if own is not None and isinstance(step, int) and step == 0:
+            source = own
+        return remote(
+            part(source, way),
+            part(whole.at[index], way),
+            ring_send.at[number, way],
+            ring_recv.at[number, way, step],
+            ring.neighbour(way),
+        )
+
+    def arrives(stream, way, step):
+        number, whole, own, part = stream
+        index = ring.at(-step - 1 if way == 0 else step + 1)
+        landed = part(whole.at[index], way)
+        return remote(
+            landed, landed, ring_send.at[number, way], ring_recv.at[number, way, step],
+            ring.neighbour(way),
+        )
+
+    def start_phase(number):
+        for stream in numbered[number]:
+            for way in (0, 1):
+                hop(stream, way, 0).start()
+
+    to_row = lambda i, a, whole: remote(
+        a, whole.at[me], ctx_send.at[i, 0], ctx_recv.at[i, 0], other_row
+    )
+    to_core = lambda i, a, whole: remote(
+        a, whole.at[me], ctx_send.at[i, 1], ctx_recv.at[i, 1], other_core
+    )
+    beyond = other_row[0]
+    pass_on = lambda i, whole: remote(
+        whole.at[beyond], whole.at[beyond], ctx_send.at[i, 2], ctx_recv.at[i, 2], other_core
+    )
+
+    to_row(0, hidden, hidden_all).start()
+    start_phase(0)
+    to_core(0, hidden, hidden_all).start()
+    own_piece = out_weight.at[pl.ds(me * piece, piece)]
+    send_piece = remote(own_piece, w_o.at[piece_to[1]], piece_send, piece_recv, piece_to)
+    keep_piece = pltpu.make_async_copy(own_piece, w_o.at[shard], local_sem.at[5])
+
+    @pl.when(moves)
+    def _():
+        send_piece.start()
+
+    @pl.when(jnp.logical_not(moves))
+    def _():
+        keep_piece.start()
+
+    locals_ = [
+        pltpu.make_async_copy(source, target, local_sem.at[i])
+        for i, (source, target) in enumerate(
+            (
+                (hidden, hidden_all.at[me]),
+                (cotangent, cotangent_all.at[me]),
+                (own_x, w_x.at[shard]),
+                (own_z, w_z.at[shard]),
+                (shared, w_s.at[shard]),
+            )
+        )
+    ]
+    for copy in locals_:
+        copy.start()
+
+    def finish_ctx(i, a, whole):
+        to_row(i, a, whole).wait_recv()
+        pass_on(i, whole).start()
+
+    def close_ctx(i, a, whole):
+        to_row(i, a, whole).wait_send()
+        to_core(i, a, whole).wait()
+        pass_on(i, whole).wait()
+
+    def run_phase(number, after):
+        def body(step, carry):
+            for stream in numbered[number]:
+                for way in (0, 1):
+                    arrives(stream, way, step).wait_recv()
+                    hop(stream, way, step).wait_send()
+                    hop(stream, way, step + 1).start()
+            return carry
+
+        lax.fori_loop(0, n - 2, body, 0)
+        after()
+        for stream in numbered[number]:
+            for way in (0, 1):
+                arrives(stream, way, n - 2).wait_recv()
+                hop(stream, way, n - 2).wait_send()
+
+    def after_first():
+        finish_ctx(0, hidden, hidden_all)
+        to_row(1, cotangent, cotangent_all).start()
+        to_core(1, cotangent, cotangent_all).start()
+        start_phase(1)
+
+    def after_second():
+        @pl.when(moves)
+        def _():
+            send_piece.wait()
+
+        @pl.when(jnp.logical_not(moves))
+        def _():
+            keep_piece.wait()
+
+        finish_ctx(1, cotangent, cotangent_all)
+        start_phase(2)
+
+    def after_third():
+        close_ctx(0, hidden, hidden_all)
+        close_ctx(1, cotangent, cotangent_all)
+        for copy in locals_:
+            copy.wait()
+
+    run_phase(0, after_first)
+    run_phase(1, after_second)
+    run_phase(2, after_third)
+
+
+def gather_all(n, n_ctx, hidden, cotangent, in_weight, shared, out_weight):
+    tokens, model = hidden.shape
+    width = out_weight.shape[0] * n // n_ctx
+    rows = in_weight.shape[0]
+    any_space = pl.BlockSpec(memory_space=pl.ANY)
+    low = lambda *shape: jax.ShapeDtypeStruct(shape, BF16)
+    return pl.pallas_call(
+        functools.partial(gather_kernel, n, n_ctx),
+        in_specs=[any_space] * 5,
+        out_specs=[any_space] * 6,
+        out_shape=[
+            low(n_ctx, tokens, model),
+            low(n_ctx, tokens, model),
+            low(n, rows, width),
+            low(n, shared.shape[0], shared.shape[1]),
+            low(n, rows, width),
+            low(n, width // n, model),
+        ],
+        scratch_shapes=[
+            pltpu.SemaphoreType.DMA((6,)),
+            pltpu.SemaphoreType.DMA((7, 2)),
+            pltpu.SemaphoreType.DMA((7, 2, n - 1)),
+            pltpu.SemaphoreType.DMA((2, 3)),
+            pltpu.SemaphoreType.DMA((2, 3)),
+            pltpu.SemaphoreType.DMA,
+            pltpu.SemaphoreType.DMA,
+        ],
+        compiler_params=pltpu.CompilerParams(collective_id=0, has_side_effects=True),
+        name="gather_all",
+    )(hidden, cotangent, in_weight, shared, out_weight)
+
+
 def conv_taps(array, taps, weight):
     tokens = array.shape[0]
     padded = jnp.pad(array, ((taps - 1, 0), (0, 0)))
@@ -298,71 +560,61 @@
     heads_all = dt_bias.shape[0] * n_fsdp
     inner = out_weight.shape[0] * n_fsdp
     heads, width = heads_all // n_ctx, inner // n_ctx
-    model = hidden.shape[2]
-    conv_width = width + 2 * STATE
-    columns = width + conv_width + LANES
-    x_at, bc_at, dt_at = inner, 2 * inner, 2 * inner + 2 * STATE
+    model, rows = hidden.shape[2], in_weight.shape[0]
+    both = 2 * STATE
+    shared_width = -(-(both + heads_all) // LANES) * LANES
 
     small = (norm_gain, conv_weight.reshape(-1), conv_bias, dt_bias, a_log, d_skip, gate_gain)
     cuts = [0]
     for part in small:
         cuts.append(cuts[-1] + part.shape[0])
-    packed = lax.all_gather(jnp.concatenate(small), "fsdp", axis=0)
+    small_rows = -(-cuts[-1] // (32 * shared_width)) * 32
+    fill = small_rows * shared_width - cuts[-1]
+    shared = jnp.concatenate(
+        [
+            jnp.pad(in_weight[:, 2 * inner :], ((0, 0), (0, shared_width - both - heads_all))),
+            jnp.concatenate(small + (jnp.zeros((fill,), BF16),)).reshape(small_rows, shared_width),
+        ],
+        axis=0,
+    )
+    resid_low, upstream, w_x, w_s, w_z, w_o = gather_all(
+        n_fsdp, n_ctx, hidden[0], cotangent[0], in_weight, shared, out_weight
+    )
+    resid_low, upstream = resid_low.reshape(-1, model), upstream.reshape(-1, model)
+    w_x, w_z, w_o = w_x.reshape(-1, width), w_z.reshape(-1, width), w_o.reshape(-1, model)
+    packed = w_s[:, rows:, :].reshape(n_fsdp, -1)
+    w_s = w_s[:, :rows, :].reshape(-1, shared_width)
     parts = [packed[:, cuts[i] : cuts[i + 1]] for i in range(len(small))]
     gain_norm = parts[0].reshape(-1).astype(F32)
-    taps_all = jnp.moveaxis(parts[1].reshape(n_fsdp, taps, -1), 0, 1).reshape(taps, -1)
-    bias_all = parts[2].reshape(-1)
+    taps_all = jnp.moveaxis(parts[1].reshape(n_fsdp, taps, -1), 0, 1).reshape(taps, -1).astype(F32)
+    bias_all = parts[2].reshape(-1).astype(F32)
 
     def own(vector, size):
         return lax.dynamic_slice_in_dim(vector, me * size, size, axis=-1)
 
-    def own_channels(vector):
-        return jnp.concatenate(
-            [own(vector[..., :inner], width), vector[..., inner:]], axis=-1
-        ).astype(F32)
-
-    weight_conv, bias_conv = own_channels(taps_all), own_channels(bias_all)
+    taps_x, taps_s = own(taps_all[:, :inner], width), taps_all[:, inner:]
+    bias_x, bias_s = own(bias_all[:inner], width), bias_all[inner:]
     bias_step = own(parts[3].reshape(-1), heads).astype(F32)
     rate = jnp.exp(own(parts[4].reshape(-1), heads).astype(F32))
     skip = own(parts[5].reshape(-1), heads).astype(F32)
     gain_gate = own(parts[6].reshape(-1), width).astype(F32)
-
-    resid_low = lax.all_gather(hidden[0], "ctx", axis=0, tiled=True)
-    own_columns = jnp.concatenate(
-        [
-            lax.dynamic_slice_in_dim(in_weight, me * width, width, axis=1),
-            lax.dynamic_slice_in_dim(in_weight, x_at + me * width, width, axis=1),
-            in_weight[:, bc_at:dt_at],
-            lax.dynamic_slice_in_dim(in_weight, dt_at + me * heads, heads, axis=1),
-            jnp.zeros((in_weight.shape[0], LANES - heads), BF16),
-        ],
-        axis=1,
-    )
-    weight_in = lax.all_gather(own_columns, "fsdp", axis=0, tiled=True)
-    upstream = lax.all_gather(cotangent[0], "ctx", axis=0, tiled=True)
-    piece = out_weight.shape[0] // n_ctx
-    there = [(c * n_fsdp + f, f * n_ctx + c) for c in range(n_ctx) for f in range(n_fsdp)]
-    back_again = [(b, a) for a, b in there]
-    own_rows = lax.ppermute(
-        lax.dynamic_slice_in_dim(out_weight, me * piece, piece, axis=0), ("ctx", "fsdp"), there
-    )
-    weight_out = lax.all_gather(own_rows, "fsdp", axis=0, tiled=True)
 
     tokens = resid_low.shape[0]
     valid = (jnp.arange(tokens, dtype=jnp.int32) < seq_lens[0]).astype(F32)[:, None]
     resid = resid_low.astype(F32)
     scale_in = lax.rsqrt(jnp.mean(resid * resid, axis=1, keepdims=True) + EPS)
     normed = (resid * scale_in * gain_norm).astype(BF16)
-    projected = mm(normed, weight_in).astype(BF16)
-    gate_raw = projected[:, :width].astype(F32)
-    conv_in = projected[:, width : width + conv_width].astype(F32)
-    step_raw = projected[:, width + conv_width : width + conv_width + heads].astype(F32)
-
-    convolved = bias_conv + conv_taps(conv_in, taps, weight_conv)
-    activated = jax.nn.silu(convolved).astype(BF16)
-    values = activated[:, :width]
-    rows_b = activated[:, width : width + STATE]
-    rows_c = activated[:, width + STATE :]
+    gate_raw = mm(normed, w_z).astype(BF16).astype(F32)
+    conv_in_x = mm(normed, w_x).astype(BF16).astype(F32)
+    projected_s = mm(normed, w_s).astype(BF16).astype(F32)
+    conv_in_s = projected_s[:, :both]
+    step_raw = own(projected_s[:, both : both + heads_all], heads)
+
+    convolved_x = bias_x + conv_taps(conv_in_x, taps, taps_x)
+    convolved_s = bias_s + conv_taps(conv_in_s, taps, taps_s)
+    values = jax.nn.silu(convolved_x).astype(BF16)
+    activated_s = jax.nn.silu(convolved_s).astype(BF16)
+    rows_b, rows_c = activated_s[:, :STATE], activated_s[:, STATE:]
     step = jax.nn.softplus(step_raw + bias_step) * valid
     lam = step * rate
     in_lanes = lambda a: jnp.pad(a, ((0, 0), (0, LANES - heads)))
@@ -373,14 +625,14 @@
     gate = jax.nn.silu(gate_raw)
     gated = mixed_ssd * gate
     d_mixed = upstream * valid.astype(BF16)
-    d_yn = mm(d_mixed, weight_out, ((1,), (1,)))
+    d_yn = mm(d_mixed, w_o, ((1,), (1,)))
     d_gain = gain_gate * d_yn
     stats = jnp.stack([jnp.sum(gated * gated, axis=1), jnp.sum(gated * d_gain, axis=1)])
     stats = lax.psum(stats, "ctx") / inner
     scale_gate = lax.rsqrt(stats[0] + EPS)[:, None]
     normed_gate = (gated * scale_gate * gain_gate).astype(BF16)
     mixed = lax.psum_scatter(
-        mm(normed_gate, weight_out).astype(BF16), "ctx", scatter_dimension=0, tiled=True
+        mm(normed_gate, w_o).astype(BF16), "ctx", scatter_dimension=0, tiled=True
     )
     own_tokens = lambda a: lax.dynamic_slice_in_dim(a, me * hidden.shape[1], hidden.shape[1], axis=0)
     layer_out = (hidden[0].astype(F32) + own_tokens(valid) * mixed.astype(F32)).astype(BF16)
@@ -400,20 +652,34 @@
     d_raw = valid * (d_step + d_lam * rate) * jax.nn.sigmoid(step_raw + bias_step)
     grad_bias_step = jnp.sum(d_raw, axis=0)
     grad_log = jnp.sum(d_lam * lam, axis=0)
-    d_conv = jnp.concatenate([d_x, d_b, d_c], axis=1) * silu_slope(convolved)
-    grad_bias_conv = jnp.sum(d_conv, axis=0)
-    padded_in = jnp.pad(conv_in, ((taps - 1, 0), (0, 0)))
-    grad_taps = jnp.stack(
-        [jnp.sum(d_conv * padded_in[k : k + tokens], axis=0) for k in range(taps)]
-    )
-    padded_back = jnp.pad(d_conv, ((0, taps - 1), (0, 0)))
-    d_conv_in = sum(
-        weight_conv[k] * padded_back[taps - 1 - k : taps - 1 - k + tokens] for k in range(taps)
-    )
-    d_projected = jnp.concatenate([d_gate_raw, d_conv_in, in_lanes(d_raw)], axis=1).astype(BF16)
-    grad_in = mm(normed, d_projected, ((0,), (0,))).astype(BF16)
+    def conv_back(d_active, convolved, conv_in, weight):
+        d_conv = d_active * silu_slope(convolved)
+        padded_in = jnp.pad(conv_in, ((taps - 1, 0), (0, 0)))
+        grad_taps = jnp.stack(
+            [jnp.sum(d_conv * padded_in[k : k + tokens], axis=0) for k in range(taps)]
+        )
+        padded = jnp.pad(d_conv, ((0, taps - 1), (0, 0)))
+        d_in = sum(weight[k] * padded[taps - 1 - k : taps - 1 - k + tokens] for k in range(taps))
+        return d_in.astype(BF16), grad_taps, jnp.sum(d_conv, axis=0)
+
+    d_in_x, grad_taps_x, grad_bias_x = conv_back(d_x, convolved_x, conv_in_x, taps_x)
+    d_in_s, grad_taps_s, grad_bias_s = conv_back(
+        jnp.concatenate([d_b, d_c], axis=1), convolved_s, conv_in_s, taps_s
+    )
+    d_raw_all = lax.dynamic_update_slice_in_dim(
+        jnp.zeros((tokens, shared_width - both), BF16), d_raw.astype(BF16), me * heads, axis=1
+    )
+    d_in_s = jnp.concatenate([d_in_s, d_raw_all], axis=1)
+    d_in_z = d_gate_raw.astype(BF16)
+    grad_in = jnp.concatenate(
+        [mm(normed, d, ((0,), (0,))).astype(BF16) for d in (d_in_z, d_in_x, d_in_s)], axis=1
+    )
     grad_in = lax.psum_scatter(grad_in, "fsdp", scatter_dimension=0, tiled=True)
-    d_normed = mm(d_projected, weight_in, ((1,), (1,))).astype(BF16)
+    d_normed = (
+        mm(d_in_z, w_z, ((1,), (1,)))
+        + mm(d_in_x, w_x, ((1,), (1,)))
+        + mm(d_in_s, w_s, ((1,), (1,)))
+    ).astype(BF16)
     d_normed = lax.psum_scatter(d_normed, "ctx", scatter_dimension=0, tiled=True).astype(F32)
 
     resid_own = hidden[0].astype(F32)
@@ -431,13 +697,10 @@
             jnp.zeros(value.shape[:-1] + (total,), F32), value, start, axis=-1
         )
 
-    def placed_channels(value):
-        return jnp.concatenate([placed(value[..., :width], inner), value[..., width:]], axis=-1)
-
     small_grads = (
         grad_gain_norm,
-        placed_channels(grad_taps).reshape(-1),
-        placed_channels(grad_bias_conv),
+        jnp.concatenate([placed(grad_taps_x, inner), grad_taps_s], axis=1).reshape(-1),
+        jnp.concatenate([placed(grad_bias_x, inner), grad_bias_s]),
         placed(grad_bias_step, heads_all),
         placed(grad_log, heads_all),
         placed(grad_skip, heads_all),
@@ -453,18 +716,18 @@
         size = vector.shape[-1] // n_fsdp
         return lax.dynamic_slice_in_dim(vector, shard * size, size, axis=-1)
 
-    conv_total = inner + 2 * STATE
+    conv_total = inner + both
     pieces = lax.all_gather(grad_in, "ctx", axis=0).astype(F32)
     in_order = lambda a: jnp.moveaxis(a, 0, 1).reshape(a.shape[1], -1)
     grad_in_weight = jnp.concatenate(
         [
             in_order(pieces[:, :, :width]),
             in_order(pieces[:, :, width : 2 * width]),
-            jnp.sum(pieces[:, :, 2 * width : width + conv_width], axis=0),
-            in_order(pieces[:, :, width + conv_width : width + conv_width + heads]),
+            jnp.sum(pieces[:, :, 2 * width : 2 * width + both + heads_all], axis=0),
         ],
         axis=1,
     )
+    back_again = [(f * n_ctx + c, c * n_fsdp + f) for c in range(n_ctx) for f in range(n_fsdp)]
     grad_out = lax.ppermute(grad_out, ("ctx", "fsdp"), back_again)
     grad_out_weight = lax.all_gather(grad_out, "ctx", axis=0, tiled=True).astype(F32)
     return (

time: 946 us -> 883 us (0.933)
  waiting for transfers between devices: 636 us -> 421 us
  Pallas kernels: 45.7 us -> 213 us
  blocking collectives: 55.1 us -> 10.3 us
  other arithmetic: 52.2 us -> 80.6 us
  local copies, waits for them, and re-layouts: 41.6 us -> 54.8 us
    all_gather x4 -> x0, waiting for transfers between devices: 199 us -> none  [the longest x1 127 us: on_device(): weight_in = lax.all_gather(own_columns, 'fsdp', axis=0, tiled=True)]
    pallas_call x0 -> x1, Pallas kernels: none -> 168 us  [gather_all(): pl.pallas_call(functools.partial(gather_kernel, n, n_ctx), in_specs=[any_...]
    unnamed x1 -> x0, blocking collectives: 48.9 us -> none
    concatenate x1 -> x3, other arithmetic: 0.02 us -> 17.3 us  [the longest x1 16.6 us: on_device(): jnp.concatenate([mm(normed, d, ((0,), (0,))).astype(BF16) for d in (d_in_...]
    reduce_scatter x1, waiting for transfers between devices: 40.5 us -> 24.7 us  [on_device(): lax.psum_scatter(d_normed, 'ctx', scatter_dimension=0, tiled=True)]
    convert_element_type x0 -> x5, local copies, waits for them, and re-layouts: none -> 11.2 us  [the longest x1 10.9 us: on_device(): pieces = lax.all_gather(grad_in, 'ctx', axis=0).astype(F32)]
    convert_element_type x6 -> x9, other arithmetic: 8.61 us -> 19.2 us  [the longest x1 6.98 us: on_device(): d_ssd = (d_gated * gate).astype(BF16)]
    another operation x3 -> x0, other arithmetic: 9.69 us -> none
  transfers between devices with their start and end apart: 13 -> 8, of which waited for: 8 -> 6; matrix products, arithmetic and copies ran while one was open for 12% -> 12% of each run, Pallas kernels for 5% -> 4%
where the time goes in v2:
time: 883 us; the launch traced here: 876 us
  waiting for transfers between devices  421 us (48%)
  Pallas kernels  213 us (24%)
  other arithmetic  80.6 us (9%)
  matrix products  76.2 us (9%)
  local copies, waits for them, and re-layouts  54.8 us (6%)
  between operations  15.9 us (2%)
  blocking collectives  10.3 us (1%)
    reduce_scatter x1, waiting for transfers between devices, on_device(): grad_in = lax.psum_scatter(grad_in, 'fsdp', scatter_dimension=0, tiled=True)  170 us
    pallas_call x1, Pallas kernels, gather_all(): pl.pallas_call(functools.partial(gather_kernel, n, n_ctx), in_specs=[any_...  168 us
    psum x1, waiting for transfers between devices, on_device(): flat = lax.psum(jnp.concatenate(small_grads), ('ctx', 'fsdp'))  124 us
    dot_general x12, matrix products, mm(): lax.dot_general(a, b, (contract, ((), ())), preferred_element_type=F32)  76.2 us
    reduce_scatter x1, waiting for transfers between devices, on_device(): lax.psum_scatter(mm(normed_gate, w_o).astype(BF16), 'ctx', scatter_dimens...  47.3 us
    all_gather x1, waiting for transfers between devices, on_device(): pieces = lax.all_gather(grad_in, 'ctx', axis=0).astype(F32)  37.1 us
    pallas_call x1, Pallas kernels, scan_backward(): pl.pallas_call(functools.partial(backward_kernel, heads), grid=(count,),...  32.5 us
    reduce_scatter x1, waiting for transfers between devices, on_device(): lax.psum_scatter(d_normed, 'ctx', scatter_dimension=0, tiled=True)  24.7 us
  transfers between devices with their start and end apart: 8, of which 6 were waited for; matrix products, arithmetic and copies ran while one was open for 12% of the time, Pallas kernels for 4%

profile of v2, /device:TPU:17, one launch (start us, length us, event | category | flops | bytes accessed | tf_op | source)
XLA Modules:
  0.0 876.0 jit_solution(17353025408138894930)
XLA Ops:
  8.0 4.1 concatenate.24
  12.2 6.4 copy.35.in_weight
  20.2 167.7 %gather_all.1 = (bf16[4,256,2048]{2,1,0:T(8,128)(2,1)}, bf16[4,256,2048]{2,1,0:T(8,128)(2,1)}, bf16[8,256,1024]{2,1,0:T(8,128)(2,1)}, bf16[8,288,384]{2,1,0:T(8,...) custom-call(bf16[256,2048]{1,0:T(8,128)(2,1)} %bitcast.100, bf16[256,2048]{1,0:T(8,128)(2,1)} %bitcast.107, ...), custom_call_target="tpu_custom_call" | custom-call | tf_op jit(solution)/shard_map/gather_all/pallas_call | solution.py:506
  189.0 1.6 slice.194
  191.2 3.2 multiply_reduce_fusion
  196.1 2.3 fusion.20
  201.1 1.6 multiply_convert_fusion.4
  202.7 4.6 bitcast_multiply_fusion.1
  207.7 1.8 copy-done.24
  209.6 1.3 copy-done.37
  210.9 4.5 convert_convert_fusion
  216.0 14.4 %fusion.45 = f32[1024,1024]{1,0:T(8,128)S(1)} fusion(bf16[1024,2048]{1,0:T(8,128)(2,1)S(1)} %bitcast.103, bf16[1024,2048]{1,0:T(8,128)(2,1)S(1)} %bitcast.156), kind=kOutput, calls=%fused_computation.131 | convolution fusion | flops 4294967296 | bytes 12582912 | tf_op jit(solution)/shard_map/dot_general | solution.py:20
  230.6 4.0 multiply_convert_fusion.3
  234.6 13.1 %scan_forward.1 = (f32[1024,1024]{1,0:T(8,128)S(1)}, bf16[4,128,1024]{2,1,0:T(8,128)(2,1)S(1)}) custom-call(bf16[1024,1024]{1,0:T(8,128)(2,1)S(1)} %get-tuple-element.66.x_ref, bf16[1024,128]{1,0:T(8,128)(2,1)S(1)} %get-tuple-element.77.b_ref, bf16[1024,128]{1,0:T(8,128)(2,1)S(1)} %get-tuple-element.76.c_ref, f32[1024,128]{1,0:T(8,128)S(1)} %pad.32.lam_ref, ...), custom_call_target="tpu_custom_call" | custom-call | flops 1610612736 | bytes 6291456 | tf_op jit(solution)/shard_map/scan_forward/pallas_call | solution.py:81
  247.7 7.1 multiply_reduce_fusion.7
  254.9 10.3 %psum.14 = f32[2,1024]{1,0:T(2,128)S(1)} all-reduce(f32[2,1024]{1,0:T(2,128)S(1)} %pad_maximum_fusion.5), channel_id=1, replica_groups=mesh['ctx'=4,'fsdp'=8] {'ctx'}, use_global_device_ids=true, to_apply=%region_3.4 | all-reduce | flops 2048 | bytes 16384 | tf_op jit(solution)/shard_map/psum | solution.py:631
  265.2 11.3 %convolution_convert_fusion = bf16[1024,2048]{1,0:T(8,128)(2,1)} fusion(bf16[1024,2048]{1,0:T(8,128)(2,1)} %bitcast_multiply_fusion.1, f32[1024]{0:T(1024)S(1)} %bitcast.126, f32[1024]{0:T(1024)S(1)} %dynamic-slice_convert_fusion, f32[1024,1024]{1,0:T(8,128)} %copy-done, bf16[1024,1024]{1,0:T(8,128)(2,1)} %get-tuple-element.97), kind=kOutput, calls=%fused_computation.40 | convolution fusion | flops 4306501632 | bytes 14688256 | tf_op jit(solution)/shard_map/dot_general | solution.py:20
  277.1 7.0 multiply_convert_fusion.1
  284.1 32.5 %scan_backward.1 = (f32[1024,1024]{1,0:T(8,128)S(1)}, f32[1024,128]{1,0:T(8,128)S(1)}, f32[1024,128]{1,0:T(8,128)S(1)}, f32[1024,128]{1,0:T(8,128)S(1)}, f32[1024,128]{1,0:T(8,128)S(1)}, /*index=5*/f32[1,1024]{1,0:T(1,128)S(1)}) custom-call(bf16[1024,1024]{1,0:T(8,128)(2,1)S(1)} %get-tuple-element.66.x_ref, bf16[1024,128]{1,0:T(8,128)(2,1)S(1)} %copy-done.8, ...), custom_call_target="tpu_custom_call" | custom-call | flops 3489660928 | bytes 10485760 | tf_op jit(solution)/shard_map/scan_backward/pallas_call | solution.py:222
  316.6 2.0 copy-done.1
  319.0 1.8 dynamic_update_slice.21
  320.8 3.6 fusion.37
  324.9 9.5 %multiply_reduce_fusion.5 = (f32[1024]{0:T(1024)S(1)}, f32[1024]{0:T(1024)S(1)}, f32[1024]{0:T(1024)S(1)}, f32[1024]{0:T(1024)S(1)}, f32[1024]{0:T(1024)S(1)}, /*index=5*/f32[1024,1024]{1,0:T(8,128)S(1)}) fusion(f32[1024,1024]{1,0:T(8,128)} %copy-done.13, f32[1024,1024]{1,0:T(8,128)S(1)} %copy-done.2, f32[1024,1024]{1,0:T(8,128)} %get-tuple-element.67), kind=kLoop, calls=%fused_computation.25 | loop fusion | flops 17820672 | bytes 16797696 | tf_op jit(solution)/shard_map/reduce_sum | solution.py:659
  334.4 1.9 add_convert_fusion.1
  337.2 4.5 fusion.46
  341.8 4.5 fusion.47
  346.4 4.5 add_convert_fusion
  351.2 3.2 fusion.1
  354.4 1.9 convolution_convert_fusion.4
  356.3 5.0 convolution_convert_fusion.1
  361.4 5.1 convolution_convert_fusion.2
  366.5 16.6 %pad_maximum_fusion = bf16[2048,2432]{0,1:T(8,128)(2,1)} fusion(bf16[2048,384]{0,1:T(8,128)(2,1)S(1)} %convolution_convert_fusion.4, bf16[2048,1024]{0,1:T(8,128)(2,1)S(1)} %convolution_convert_fusion.1, bf16[2048,1024]{0,1:T(8,128)(2,1)S(1)} %convolution_convert_fusion.2), kind=kLoop, calls=%fused_computation | loop fusion | flops 29884416 | bytes 19922944 | tf_op jit(solution)/shard_map/concatenate | solution.py:674
  383.5 1.1 copy-done.30
  384.6 10.9 %convolution_convert_fusion.3 = bf16[1024,2048]{1,0:T(8,128)(2,1)} fusion(bf16[1024,2048]{1,0:T(8,128)(2,1)} %bitcast.155, f32[1024]{0:T(1024)S(1)} %bitcast.129, f32[1024]{0:T(1024)S(1)} %dynamic-slice_convert_fusion, f32[1024,1024]{1,0:T(8,128)} %copy-done, bf16[1024,1024]{1,0:T(8,128)(2,1)S(1)} %copy-done.30), kind=kOutput, calls=%fused_computation.43 | convolution fusion | flops 4306501632 | bytes 14688256 | tf_op jit(solution)/shard_map/dot_general | solution.py:20
  395.7 2.1 collective-permute-start
  400.5 24.7 %reduce-scatter.7.cloned.1.call-done = bf16[256,2048]{1,0:T(8,128)(2,1)} async-done(((bf16[1024,2048]{1,0:T(8,128)(2,1)}), bf16[256,2048]{1,0:T(8,128)(2,1)}) %reduce-scatter.7.cloned.1.call-update) | async-done | bytes 1048592 | tf_op jit(solution)/shard_map/reduce_scatter | solution.py:683
  425.3 2.0 fusion.18
  428.8 170.5 %reduce-scatter.9.cloned.1.call-done = bf16[256,2432]{0,1:T(8,128)(2,1)} async-done(((bf16[2048,2432]{0,1:T(8,128)(2,1)}), bf16[256,2432]{0,1:T(8,128)(2,1)}) %reduce-scatter.9.cloned.1.call-update) | async-done | bytes 1245200 | tf_op jit(solution)/shard_map/reduce_scatter | solution.py:677
  599.4 47.3 %reduce-scatter.5.cloned.1.call-done = bf16[256,2048]{1,0:T(8,128)(2,1)} async-done(((bf16[1024,2048]{1,0:T(8,128)(2,1)}), bf16[256,2048]{1,0:T(8,128)(2,1)}) %reduce-scatter.5.cloned.1.call-update) | async-done | bytes 1048592 | tf_op jit(solution)/shard_map/reduce_scatter | solution.py:634
  646.7 3.6 fusion.22
  650.3 123.6 %all-reduce.9.cloned.1.call-done = f32[28096]{0:T(1024)} async-done(((f32[28096]{0:T(1024)}), f32[28096]{0:T(1024)}) %all-reduce.9.cloned.1.call-update) | async-done | bytes 112400 | tf_op jit(solution)/shard_map/psum | solution.py:709
  782.3 17.4 %all-gather.4.cloned.1.call-done = bf16[512,2048]{1,0:T(8,128)(2,1)} async-done(((bf16[128,2048]{1,0:T(8,128)(2,1)}), bf16[512,2048]{1,0:T(8,128)(2,1)}) %all-gather.4.cloned.1.call-update) | async-done | bytes 2097168 | tf_op jit(solution)/shard_map/all_gather | solution.py:732
  799.6 4.1 convert_element_type.235
  803.8 37.1 %all-gather.6.cloned.1.call-done = bf16[1024,2432]{0,1:T(8,128)(2,1)} async-done(((bf16[256,2432]{0,1:T(8,128)(2,1)}), bf16[1024,2432]{0,1:T(8,128)(2,1)}) %all-gather.6.cloned.1.call-update) | async-done | bytes 4980752 | tf_op jit(solution)/shard_map/all_gather | solution.py:720
  840.9 10.9 %reshape.231 = f32[4,256,2432]{1,0,2:T(4,128)} reshape(bf16[1024,2432]{0,1:T(8,128)(2,1)} %all-gather.6.cloned.1.call-done) | data formatting | bytes 14942208 | tf_op jit(solution)/shard_map/convert_element_type | solution.py:720
  851.8 1.9 slice_reduce_fusion
  853.7 4.9 slice_bitcast_fusion.1
  860.2 8.7 pad_maximum_fusion.1
  (186 shorter events, 25.9 us)
Async XLA Ops:
  7.2 388.5 %reduce-scatter.11.cloned.1.call-start = ((), (), s32[]{:S(2)}) async-start(), calls=%async_computation.8 | async-start | bytes 4718592 | tf_op jit(solution)/shard_map/reduce_scatter | solution.py:641
  190.6 5.5 copy-start.16
  190.9 5.2 copy-start.34
  191.1 4.9 copy-start.33
  191.1 3.9 copy-start.11
  196.1 2.4 copy-start.23
  196.1 4.9 slice-start.2
  196.1 4.9 slice-start.1
  199.6 15.8 %copy-start.18 = (f32[1024,64]{1,0:T(8,128)}, f32[1024,64]{1,0:T(8,128)S(1)}, u32[]{:S(2)}) copy-start(f32[1024,64]{1,0:T(8,128)S(1)} %slice.243) | copy-start | bytes 786436
  199.7 3.0 copy-start.15
  202.7 31.9 %copy-start.7 = (bf16[1024,128]{1,0:T(8,128)(2,1)}, bf16[1024,128]{1,0:T(8,128)(2,1)S(1)}, u32[]{:S(2)}) copy-start(bf16[1024,128]{1,0:T(8,128)(2,1)S(1)} %get-tuple-element.77.b_ref) | copy-start | bytes 786436
  202.7 4.7 copy-start.12
  207.4 2.2 copy-start.24
  207.4 3.5 copy-start.37
  210.9 5.1 copy-start.36
  215.4 15.2 %copy-start.13 = (f32[1024,1024]{1,0:T(8,128)}, f32[1024,1024]{1,0:T(8,128)S(1)}, u32[]{:S(2)}) copy-start(f32[1024,1024]{1,0:T(8,128)S(1)} %convert_convert_fusion) | copy-start | bytes 12582916
  215.8 14.6 %copy-start.20 = (f32[1024,16]{1,0:T(8,128)}, f32[1024,16]{1,0:T(8,128)S(1)}, u32[]{:S(2)}) copy-start(f32[1024,16]{1,0:T(8,128)S(1)} %get-tuple-element.62) | copy-start | bytes 196612
  215.9 18.7 %copy-start.3 = (f32[1024,128]{1,0:T(8,128)}, f32[1024,128]{1,0:T(8,128)S(1)}, u32[]{:S(2)}) copy-start(f32[1024,128]{1,0:T(8,128)S(1)} %pad.33.step_ref) | copy-start | bytes 1572868
  215.9 18.7 %copy-start.5 = (f32[1024,128]{1,0:T(8,128)}, f32[1024,128]{1,0:T(8,128)S(1)}, u32[]{:S(2)}) copy-start(f32[1024,128]{1,0:T(8,128)S(1)} %pad.32.lam_ref) | copy-start | bytes 1572868
  215.9 14.5 %slice-start = ((f32[4,4352]{1,0:T(4,128)}), f32[4,4096]{1,0:T(4,128)S(1)}, s32[]{:S(2)}) async-start(f32[4,4352]{1,0:T(4,128)} %copy-done.33), calls=%async_computation.11 | async-start | bytes 131072 | tf_op jit(solution)/shard_map/slice | solution.py:595
  230.4 17.3 %copy-start.27 = (f32[1024,1024]{1,0:T(8,128)}, f32[1024,1024]{1,0:T(8,128)S(1)}, u32[]{:S(2)}) copy-start(f32[1024,1024]{1,0:T(8,128)S(1)} %fusion.45) | copy-start | bytes 12582916
  234.6 13.1 %copy-start.39 = (bf16[8,256,1024]{2,1,0:T(8,128)(2,1)S(1)}, bf16[8,256,1024]{2,1,0:T(8,128)(2,1)}, u32[]{:S(2)}) copy-start(bf16[8,256,1024]{2,1,0:T(8,128)(2,1)} %get-tuple-element.29) | copy-start | bytes 12582916
  247.7 7.2 copy-start
  247.7 7.2 copy-start.9
  276.5 148.7 %reduce-scatter.7.cloned.1.call-start = ((), (), s32[]{:S(2)}) async-start(), calls=%async_computation.5 | async-start | bytes 5242880 | tf_op jit(solution)/shard_map/reduce_scatter | solution.py:683
  277.0 7.0 copy-start.4
  277.0 7.0 copy-start.6
  277.0 7.0 copy-start.8
  277.0 7.0 copy-start.10
  284.0 34.5 %copy-start.19 = (f32[1024,64]{1,0:T(8,128)S(1)}, f32[1024,64]{1,0:T(8,128)}, u32[]{:S(2)}) copy-start(f32[1024,64]{1,0:T(8,128)} %copy-done.18) | copy-start | bytes 786436
  284.1 34.5 %copy-start.21 = (f32[1024,16]{1,0:T(8,128)S(1)}, f32[1024,16]{1,0:T(8,128)}, u32[]{:S(2)}) copy-start(f32[1024,16]{1,0:T(8,128)} %copy-done.20) | copy-start | bytes 196612
  316.6 2.0 copy-start.1
  320.8 4.1 copy-start.2
  334.4 2.8 copy-start.40
  336.3 5.5 copy-start.28
  337.2 4.6 copy-start.38
  341.8 4.6 copy-start.17
  350.9 248.4 %reduce-scatter.9.cloned.1.call-start = ((), (), s32[]{:S(2)}) async-start(), calls=%async_computation.7 | async-start | bytes 11206656 | tf_op jit(solution)/shard_map/reduce_scatter | solution.py:677
  356.3 5.1 copy-start.32
  383.1 263.6 %reduce-scatter.5.cloned.1.call-start = ((), (), s32[]{:S(2)}) async-start(), calls=%async_computation.4 | async-start | bytes 5242880 | tf_op jit(solution)/shard_map/reduce_scatter | solution.py:634
  395.6 2.3 copy-start.35
  395.6 29.7 %copy-start.14 = (bf16[1,256,2048]{2,1,0:T(8,128)(2,1)S(1)}, bf16[1,256,2048]{2,1,0:T(8,128)(2,1)}, u32[]{:S(2)}) copy-start(bf16[1,256,2048]{2,1,0:T(8,128)(2,1)} %param.12) | copy-start | bytes 3145732
  395.6 251.2 %copy-start.25 = (bf16[1,256,2048]{2,1,0:T(8,128)(2,1)S(1)}, bf16[1,256,2048]{2,1,0:T(8,128)(2,1)}, u32[]{:S(2)}) copy-start(bf16[1,256,2048]{2,1,0:T(8,128)(2,1)} %param.13) | copy-start | bytes 3145732
  395.6 378.3 %all-reduce.9.cloned.1.call-start = ((), (), s32[]{:S(2)}) async-start(), calls=%async_computation.6 | async-start | bytes 229376 | tf_op jit(solution)/shard_map/psum | solution.py:709
  395.7 32.3 %collective-permute-start = (bf16[128,2048]{1,0:T(8,128)(2,1)}, bf16[128,2048]{1,0:T(8,128)(2,1)}, u32[]{:S(2)}, u32[]{:S(2)}) collective-permute-start(bf16[128,2048]{1,0:T(8,128)(2,1)} %reduce-scatter.11.cloned.1.call-done), channel_id=1, source_target_pairs={{0,0},{4,1},{8,2},{12,3},{16,4},{20,5},{24,6},{28,7},{1,8},{5,9},{... | collective-permute-start | bytes 1572872 | tf_op jit(solution)/shard_map/ppermute | solution.py:731
  425.3 221.5 %copy-start.26 = (bf16[256,2048]{1,0:T(8,128)(2,1)S(1)}, bf16[256,2048]{1,0:T(8,128)(2,1)}, u32[]{:S(2)}) copy-start(bf16[256,2048]{1,0:T(8,128)(2,1)} %reduce-scatter.7.cloned.1.call-done) | copy-start | bytes 3145732
  428.0 371.6 %all-gather.4.cloned.1.call-start = ((), (), s32[]{:S(2)}) async-start(), calls=%async_computation.9 | async-start | bytes 2621440 | tf_op jit(solution)/shard_map/all_gather | solution.py:732
  428.6 412.3 %all-gather.6.cloned.1.call-start = ((), (), s32[]{:S(2)}) async-start(), calls=%async_computation.10 | async-start | bytes 6225920 | tf_op jit(solution)/shard_map/all_gather | solution.py:720
  (4 other events, 6.6 us)
Sparse Core Ops, SparseCore 0:
  276.7 89.5 reduce-scatter.10
  369.6 55.6 reduce-scatter.6
  428.9 170.3 reduce-scatter.8
  602.2 44.4 reduce-scatter.4
  653.6 120.2 all-reduce.8
  775.4 24.1 all-gather.3
  801.2 39.6 all-gather.5

commit v3 on v2

--- a/solution.py
+++ b/solution.py
@@ -529,6 +529,505 @@
     )(hidden, cotangent, in_weight, shared, out_weight)
 
 
+def reduce_kernel(
+    n,
+    n_ctx,
+    normed_t,
+    gate_t,
+    d_mixed,
+    d_z,
+    d_x,
+    d_s,
+    mixed_parts,
+    normed_parts,
+    small,
+    hidden,
+    cotangent,
+    gain,
+    g_z,
+    g_x,
+    g_s,
+    g_o,
+    layer_out,
+    hidden_grad,
+    small_out,
+    v_normed_t,
+    v_gate_t,
+    v_d_mixed,
+    v_d_z,
+    v_d_x,
+    v_d_s,
+    slot_o,
+    slot_z,
+    slot_x,
+    slot_s,
+    first_o,
+    first_z,
+    first_x,
+    first_s,
+    done_o,
+    done_z,
+    done_x,
+    done_s,
+    moved,
+    mine,
+    from_core,
+    from_row,
+    v_hidden,
+    v_cotangent,
+    v_gain,
+    v_out,
+    v_grad,
+    small_all,
+    small_ctx,
+    load_sem,
+    store_sem,
+    ring_send,
+    ring_recv,
+    ctx_send,
+    ctx_recv,
+    own_sem,
+    piece_send,
+    piece_recv,
+    part_send,
+    part_recv,
+    small_send,
+    small_recv,
+    small_ctx_send,
+    small_ctx_recv,
+):
+    ring = Ring(n)
+    me, shard = ring.me, ring.shard
+    row = me // 2
+    core = me % 2
+    core_at = me + 1 - 2 * core
+    row_at = me + 2 - 4 * row
+    both_at = row_at + 1 - 2 * core
+    other_core, other_row, other_both = (core_at, shard), (row_at, shard), (both_at, shard)
+    held_as = me * n + shard
+    piece_to = (held_as % n_ctx, held_as // n_ctx)
+    sent_as = shard * n_ctx + me
+    piece_from = (sent_as // n, sent_as % n)
+    moves = sent_as != held_as
+
+    barrier = pltpu.get_barrier_semaphore()
+
+    def greet(device):
+        pl.semaphore_signal(barrier, inc=1, device_id=device, device_id_type=MESH)
+
+    def peer(offset):
+        return (me, lax.rem(shard + offset, n))
+
+    for device in (other_core, other_row, other_both):
+        greet(device)
+    lax.fori_loop(1, n, lambda j, carry: (greet(peer(j)), carry)[1], 0)
+
+    loads = [
+        pltpu.make_async_copy(source, target, load_sem.at[i])
+        for i, (source, target) in enumerate(
+            (
+                (gate_t, v_gate_t),
+                (d_mixed, v_d_mixed),
+                (mixed_parts.at[row_at], mine.at[0, 1]),
+                (normed_parts.at[row_at], mine.at[1, 1]),
+                (normed_t, v_normed_t),
+                (d_z, v_d_z),
+                (mixed_parts.at[me], mine.at[0, 0]),
+                (normed_parts.at[me], mine.at[1, 0]),
+                (hidden, v_hidden),
+                (cotangent, v_cotangent),
+                (gain, v_gain),
+                (small, small_all.at[shard, pl.ds(0, small.shape[0])]),
+                (d_x, v_d_x),
+                (d_s, v_d_s),
+            )
+        )
+    ]
+    for copy in loads:
+        copy.start()
+
+    @pl.when(moves)
+    def _():
+        greet(piece_to)
+        greet(piece_from)
+        pl.semaphore_wait(barrier, n + 4)
+
+    @pl.when(jnp.logical_not(moves))
+    def _():
+        pl.semaphore_wait(barrier, n + 2)
+
+    def remote(source, target, send, recv, device):
+        return pltpu.make_async_remote_copy(
+            src_ref=source,
+            dst_ref=target,
+            send_sem=send,
+            recv_sem=recv,
+            device_id=device,
+            device_id_type=MESH,
+        )
+
+    def to_core(i, which):
+        source = (mixed_parts, normed_parts)[i].at[(core_at, both_at)[which]]
+        return remote(
+            source, from_core.at[i, which], part_send.at[i, which], part_recv.at[i, which], other_core
+        )
+
+    def to_row(i):
+        return remote(
+            mine.at[i, 1], from_row.at[i], part_send.at[i, 2], part_recv.at[i, 2], other_row
+        )
+
+    for which in (1, 0):
+        for i in (0, 1):
+            to_core(i, which).start()
+
+    rows, piece = v_normed_t.shape[0] // (2 * n), done_o.shape[0]
+    half = v_d_z.shape[1] // 2
+    quarter = v_d_mixed.shape[1] // 4
+
+    def in_stream(number, right, first, size, slots, stage, done):
+        def own(index, way):
+            left = v_normed_t[pl.ds(pl.multiple_of((2 * index + way) * rows, 16), rows), :]
+            return mm(left, right[:, first : first + size])
+
+        return (
+            number,
+            own,
+            lambda way, step: slots.at[step, way, :, pl.ds(first, size)],
+            lambda way: stage.at[way, :, pl.ds(first, size)],
+            lambda way: done.at[pl.ds(way * rows, rows), pl.ds(first, size)],
+        )
+
+    def out_stream(number, sub):
+        def own(index, way):
+            left = v_gate_t[pl.ds(pl.multiple_of(index * piece, 16), piece), :]
+            at = (2 * way + sub) * quarter
+            return mm(left, v_d_mixed[:, at : at + quarter])
+
+        return (
+            number,
+            own,
+            lambda way, step: slot_o.at[step, way, :, pl.ds(sub * quarter, quarter)],
+            lambda way: first_o.at[way, :, pl.ds(sub * quarter, quarter)],
+            lambda way: done_o.at[:, pl.ds((2 * way + sub) * quarter, quarter)],
+        )
+
+    phases = (
+        (out_stream(0, 0), out_stream(1, 1)),
+        (
+            in_stream(2, v_d_z, 0, half, slot_z, first_z, done_z),
+            in_stream(3, v_d_z, half, half, slot_z, first_z, done_z),
+        ),
+        (
+            in_stream(4, v_d_s, 0, v_d_s.shape[1], slot_s, first_s, done_s),
+            in_stream(5, v_d_x, 0, half, slot_x, first_x, done_x),
+            in_stream(6, v_d_x, half, half, slot_x, first_x, done_x),
+        ),
+    )
+
+    def hop(stream, way, step, source):
+        number, own, slot, stage, done = stream
+        return remote(
+            source,
+            slot(way, step),
+            ring_send.at[number, way],
+            ring_recv.at[number, way, step],
+            ring.neighbour(way),
+        )
+
+    def start_phase(number):
+        for stream in phases[number]:
+            for way in (0, 1):
+                stage = stream[3](way)
+                stage[...] = stream[1](ring.at(-1 if way == 0 else 1), way).astype(BF16)
+                hop(stream, way, 0, stage).start()
+
+    def arrived(stream, way, step):
+        number, own, slot, stage, done = stream
+        partial = own(ring.at(-step - 2 if way == 0 else step + 2), way)
+        hop(stream, way, step, stage(way)).wait()
+        return slot(way, step)[...].astype(F32) + partial
+
+    def run_phase(number, after):
+        def body(step, carry):
+            for stream in phases[number]:
+                for way in (0, 1):
+                    total = arrived(stream, way, step)
+                    place = stream[2](way, step)
+                    place[...] = total.astype(BF16)
+                    hop(stream, way, step + 1, place).start()
+            return carry
+
+        lax.fori_loop(0, n - 2, body, 0)
+        after()
+        for stream in phases[number]:
+            for way in (0, 1):
+                done = stream[4](way)
+                done[...] = arrived(stream, way, n - 2).astype(BF16)
+
+    ctx_pairs = ((moved, g_o), (done_z, g_z), (done_x, g_x), (done_s, g_s))
+
+    def share(i, kind):
+        source, whole = ctx_pairs[i]
+        if kind == 2:
+            source, at = whole.at[row_at], row_at
+        else:
+            at = me
+        device = other_row if kind == 0 else other_core
+        return remote(source, whole.at[at], ctx_send.at[i, kind], ctx_recv.at[i, kind], device)
+
+    def keep(i):
+        source, whole = ctx_pairs[i]
+        return pltpu.make_async_copy(source, whole.at[me], own_sem.at[i])
+
+    def start_share(i):
+        share(i, 0).start()
+        share(i, 1).start()
+        keep(i).start()
+
+    def pass_share(i):
+        share(i, 0).wait_recv()
+        share(i, 2).start()
+
+    def close_share(i):
+        share(i, 0).wait_send()
+        share(i, 1).wait()
+        share(i, 2).wait()
+        keep(i).wait()
+
+    send_piece = remote(done_o, moved, piece_send, piece_recv, piece_to)
+    keep_piece = pltpu.make_async_copy(done_o, moved, piece_send)
+
+    def move_piece(wait):
+        @pl.when(moves)
+        def _():
+            send_piece.wait() if wait else send_piece.start()
+
+        @pl.when(jnp.logical_not(moves))
+        def _():
+            keep_piece.wait() if wait else keep_piece.start()
+
+    def small_to(offset):
+        return remote(
+            small_all.at[shard],
+            small_all.at[shard],
+            small_send.at[offset - 1],
+            small_recv.at[offset - 1],
+            peer(offset),
+        )
+
+    def small_share(i):
+        return remote(
+            small_ctx.at[me],
+            small_ctx.at[me],
+            small_ctx_send.at[i],
+            small_ctx_recv.at[i],
+            (other_core, other_row, other_both)[i],
+        )
+
+    store_layer = pltpu.make_async_copy(v_out, layer_out, store_sem.at[0])
+    store_grad = pltpu.make_async_copy(v_grad, hidden_grad, store_sem.at[1])
+    store_small = pltpu.make_async_copy(small_ctx, small_out, store_sem.at[2])
+
+    def sum_rows():
+        for i in (0, 1):
+            to_core(i, 1).wait()
+            mine[i, 1] = (mine[i, 1].astype(F32) + from_core[i, 1].astype(F32)).astype(BF16)
+            to_row(i).start()
+
+    def whole_sum(i):
+        to_core(i, 0).wait()
+        to_row(i).wait()
+        return (
+            mine[i, 0].astype(F32) + from_core[i, 0].astype(F32) + from_row[i].astype(F32)
+        )
+
+    def finish_tokens():
+        resid = v_hidden[...].astype(F32)
+        v_out[...] = (resid + whole_sum(0)).astype(BF16)
+        store_layer.start()
+        scale = lax.rsqrt(jnp.mean(resid * resid, axis=1, keepdims=True) + EPS)
+        d_normed = whole_sum(1)
+        f = v_gain[...] * d_normed
+        slope = scale**3 * jnp.mean(resid * f, axis=1, keepdims=True)
+        v_grad[...] = (v_cotangent[...].astype(F32) + scale * f - resid * slope).astype(BF16)
+        store_grad.start()
+        by_model = jnp.sum(d_normed * resid * scale, axis=0, keepdims=True)
+        base = small.shape[0]
+        for j in range(by_model.shape[1] // LANES):
+            small_all[shard, base + j : base + j + 1, :] = by_model[
+                :, j * LANES : (j + 1) * LANES
+            ]
+        lax.fori_loop(1, n, lambda j, carry: (small_to(j).start(), carry)[1], 0)
+
+    def sum_small():
+        lax.fori_loop(1, n, lambda j, carry: (small_to(j).wait(), carry)[1], 0)
+        small_ctx[me] = jnp.sum(small_all[...], axis=0)
+        for i in range(3):
+            small_share(i).start()
+
+    loads[0].wait()
+    loads[1].wait()
+    start_phase(0)
+    for copy in loads[2:]:
+        copy.wait()
+    sum_rows()
+
+    def after_first():
+        start_phase(1)
+
+    def after_second():
+        start_phase(2)
+        move_piece(True)
+        start_share(0)
+        finish_tokens()
+
+    def after_third():
+        pass_share(0)
+        pass_share(1)
+        sum_small()
+
+    run_phase(0, after_first)
+    move_piece(False)
+    run_phase(1, after_second)
+    start_share(1)
+    run_phase(2, after_third)
+    start_share(2)
+    start_share(3)
+    for i in range(3):
+        small_share(i).wait()
+    store_small.start()
+    pass_share(2)
+    pass_share(3)
+    for i in range(4):
+        close_share(i)
+    store_layer.wait()
+    store_grad.wait()
+    store_small.wait()
+
+
+def reduce_all(
+    n, n_ctx, normed_t, gate_t, d_mixed, d_z, d_x, d_s, mixed_parts, normed_parts, small, hidden, cotangent, gain
+):
+    model, tokens = normed_t.shape
+    width, shared_width = d_z.shape[1], d_s.shape[1]
+    rows, piece, own = model // n, width // n, hidden.shape[0]
+    small_rows = small.shape[0] + model // LANES
+    any_space = pl.BlockSpec(memory_space=pl.ANY)
+    dma = pltpu.SemaphoreType.DMA
+    low = lambda *shape: jax.ShapeDtypeStruct(shape, BF16)
+    v_low = lambda *shape: pltpu.VMEM(shape, BF16)
+    v_full = lambda *shape: pltpu.VMEM(shape, F32)
+    return pl.pallas_call(
+        functools.partial(reduce_kernel, n, n_ctx),
+        in_specs=[any_space] * 12,
+        out_specs=[any_space] * 7,
+        out_shape=[
+            low(n_ctx, rows, width),
+            low(n_ctx, rows, width),
+            low(n_ctx, rows, shared_width),
+            low(n_ctx, piece, model),
+            low(own, model),
+            low(own, model),
+            jax.ShapeDtypeStruct((n_ctx, small_rows, LANES), F32),
+        ],
+        scratch_shapes=[
+            v_low(model, tokens),
+            v_low(width, tokens),
+            v_low(tokens, model),
+            v_low(tokens, width),
+            v_low(tokens, width),
+            v_low(tokens, shared_width),
+            v_low(n - 1, 2, piece, model // 2),
+            v_low(n - 1, 2, rows // 2, width),
+            v_low(n - 1, 2, rows // 2, width),
+            v_low(n - 1, 2, rows // 2, shared_width),
+            v_low(2, piece, model // 2),
+            v_low(2, rows // 2, width),
+            v_low(2, rows // 2, width),
+            v_low(2, rows // 2, shared_width),
+            v_low(piece, model),
+            v_low(rows, width),
+            v_low(rows, width),
+            v_low(rows, shared_width),
+            v_low(piece, model),
+            v_low(2, 2, own, model),
+            v_low(2, 2, own, model),
+            v_low(2, own, model),
+            v_low(own, model),
+            v_low(own, model),
+            v_full(1, model),
+            v_low(own, model),
+            v_low(own, model),
+            v_full(n, small_rows, LANES),
+            v_full(n_ctx, small_rows, LANES),
+            dma((14,)),
+            dma((3,)),
+            dma((7, 2)),
+            dma((7, 2, n - 1)),
+            dma((4, 3)),
+            dma((4, 3)),
+            dma((4,)),
+            dma,
+            dma,
+            dma((2, 3)),
+            dma((2, 3)),
+            dma((n - 1,)),
+            dma((n - 1,)),
+            dma((3,)),
+            dma((3,)),
+        ],
+        compiler_params=pltpu.CompilerParams(
+            collective_id=1, has_side_effects=True, vmem_limit_bytes=58 * 1024 * 1024
+        ),
+        name="reduce_all",
+    )(
+        normed_t, gate_t, d_mixed, d_z, d_x, d_s, mixed_parts, normed_parts, small, hidden, cotangent, gain
+    )
+
+
+def assemble_kernel(width, both_heads, z_ref, x_ref, s_ref, o_ref, in_ref, out_ref):
+    n_ctx = z_ref.shape[0]
+    for c in range(n_ctx):
+        in_ref[:, c * width : (c + 1) * width] = z_ref[c].astype(F32)
+        in_ref[:, (n_ctx + c) * width : (n_ctx + c + 1) * width] = x_ref[c].astype(F32)
+    total = s_ref[0].astype(F32)
+    for c in range(1, n_ctx):
+        total += s_ref[c].astype(F32)
+    in_ref[:, 2 * n_ctx * width :] = total[:, :both_heads]
+    out_ref[...] = o_ref[...].astype(F32)
+
+
+def assemble(g_z, g_x, g_s, g_o, both_heads):
+    n_ctx, rows, width = g_z.shape
+    shared_width, model = g_s.shape[2], g_o.shape[2]
+    g_o = g_o.reshape(-1, model)
+    steps = 4 if rows >= 64 and g_o.shape[0] >= 64 else 1
+    tile, tile_o = rows // steps, g_o.shape[0] // steps
+    columns = 2 * n_ctx * width + both_heads
+    part = lambda size: pl.BlockSpec((n_ctx, tile, size), lambda i: (0, i, 0))
+    return pl.pallas_call(
+        functools.partial(assemble_kernel, width, both_heads),
+        grid=(steps,),
+        in_specs=[
+            part(width),
+            part(width),
+            part(shared_width),
+            pl.BlockSpec((tile_o, model), lambda i: (i, 0)),
+        ],
+        out_specs=[
+            pl.BlockSpec((tile, columns), lambda i: (i, 0)),
+            pl.BlockSpec((tile_o, model), lambda i: (i, 0)),
+        ],
+        out_shape=[
+            jax.ShapeDtypeStruct((rows, columns), F32),
+            jax.ShapeDtypeStruct(g_o.shape, F32),
+        ],
+        compiler_params=pltpu.CompilerParams(vmem_limit_bytes=32 * 1024 * 1024),
+        name="assemble",
+    )(g_z, g_x, g_s, g_o)
+
+
 def conv_taps(array, taps, weight):
     tokens = array.shape[0]
     padded = jnp.pad(array, ((taps - 1, 0), (0, 0)))
@@ -631,14 +1130,7 @@
     stats = lax.psum(stats, "ctx") / inner
     scale_gate = lax.rsqrt(stats[0] + EPS)[:, None]
     normed_gate = (gated * scale_gate * gain_gate).astype(BF16)
-    mixed = lax.psum_scatter(
-        mm(normed_gate, w_o).astype(BF16), "ctx", scatter_dimension=0, tiled=True
-    )
-    own_tokens = lambda a: lax.dynamic_slice_in_dim(a, me * hidden.shape[1], hidden.shape[1], axis=0)
-    layer_out = (hidden[0].astype(F32) + own_tokens(valid) * mixed.astype(F32)).astype(BF16)
-
-    grad_out = mm(normed_gate, d_mixed, ((0,), (0,))).astype(BF16)
-    grad_out = lax.psum_scatter(grad_out, "fsdp", scatter_dimension=0, tiled=True)
+    mixed = (valid * mm(normed_gate, w_o)).astype(BF16)
     grad_gain_gate = jnp.sum(d_yn * gated * scale_gate, axis=0)
     d_gated = scale_gate * d_gain - gated * (scale_gate**3 * stats[1][:, None])
     d_ssd = (d_gated * gate).astype(BF16)
@@ -671,76 +1163,63 @@
     )
     d_in_s = jnp.concatenate([d_in_s, d_raw_all], axis=1)
     d_in_z = d_gate_raw.astype(BF16)
-    grad_in = jnp.concatenate(
-        [mm(normed, d, ((0,), (0,))).astype(BF16) for d in (d_in_z, d_in_x, d_in_s)], axis=1
-    )
-    grad_in = lax.psum_scatter(grad_in, "fsdp", scatter_dimension=0, tiled=True)
     d_normed = (
         mm(d_in_z, w_z, ((1,), (1,)))
         + mm(d_in_x, w_x, ((1,), (1,)))
         + mm(d_in_s, w_s, ((1,), (1,)))
     ).astype(BF16)
-    d_normed = lax.psum_scatter(d_normed, "ctx", scatter_dimension=0, tiled=True).astype(F32)
-
-    resid_own = hidden[0].astype(F32)
-    scale_own = own_tokens(scale_in)
-    f = gain_norm * d_normed
-    d_resid = scale_own * f - resid_own * scale_own**3 * jnp.mean(
-        resid_own * f, axis=1, keepdims=True
-    )
-    hidden_grad = (cotangent[0].astype(F32) + d_resid).astype(BF16)
-    grad_gain_norm = jnp.sum(d_normed * resid_own * scale_own, axis=0)
-
-    def placed(value, total):
-        start = me * value.shape[-1]
-        return lax.dynamic_update_slice_in_dim(
-            jnp.zeros(value.shape[:-1] + (total,), F32), value, start, axis=-1
-        )
-
-    small_grads = (
-        grad_gain_norm,
-        jnp.concatenate([placed(grad_taps_x, inner), grad_taps_s], axis=1).reshape(-1),
-        jnp.concatenate([placed(grad_bias_x, inner), grad_bias_s]),
-        placed(grad_bias_step, heads_all),
-        placed(grad_log, heads_all),
-        placed(grad_skip, heads_all),
-        placed(grad_gain_gate, inner),
-    )
-    flat = lax.psum(jnp.concatenate(small_grads), ("ctx", "fsdp"))
-    outs, at = [], 0
-    for value in small_grads:
-        outs.append(flat[at : at + value.shape[0]])
-        at += value.shape[0]
+    small_grads = [grad_taps_x, grad_taps_s, grad_bias_x, grad_bias_s, grad_gain_gate]
+    small_grads += [grad_bias_step, grad_log, grad_skip]
+    sizes = [a.size for a in small_grads]
+    small_count = -(-sum(sizes) // (8 * LANES)) * 8 * LANES
+    flat = jnp.concatenate(
+        [a.reshape(-1) for a in small_grads] + [jnp.zeros((small_count - sum(sizes),), F32)]
+    )
+    own = hidden.shape[1]
+    g_z, g_x, g_s, g_o, layer_out, hidden_grad, small_sums = reduce_all(
+        n_fsdp,
+        n_ctx,
+        normed.T,
+        normed_gate.T,
+        d_mixed,
+        d_in_z,
+        d_in_x,
+        d_in_s,
+        mixed.reshape(n_ctx, own, model),
+        d_normed.reshape(n_ctx, own, model),
+        flat.reshape(-1, LANES),
+        hidden[0],
+        cotangent[0],
+        gain_norm[None, :],
+    )
+    grad_in_weight, grad_out_weight = assemble(g_z, g_x, g_s, g_o, both + heads_all)
+    small_sums = small_sums.reshape(n_ctx, -1)
+    ends = [sum(sizes[:i]) for i in range(len(sizes) + 1)]
+    taps_x_sum, taps_s_sum, bias_x_sum, bias_s_sum, gate_sum, step_sum, log_sum, skip_sum = [
+        small_sums[:, ends[i] : ends[i + 1]] for i in range(len(sizes))
+    ]
+    grad_gain_norm = jnp.sum(small_sums[:, small_count:], axis=0)
+    by_tap = lambda a: jnp.moveaxis(a.reshape(n_ctx, taps, -1), 0, 1)
 
     def own_shard(vector):
         size = vector.shape[-1] // n_fsdp
         return lax.dynamic_slice_in_dim(vector, shard * size, size, axis=-1)
 
-    conv_total = inner + both
-    pieces = lax.all_gather(grad_in, "ctx", axis=0).astype(F32)
-    in_order = lambda a: jnp.moveaxis(a, 0, 1).reshape(a.shape[1], -1)
-    grad_in_weight = jnp.concatenate(
-        [
-            in_order(pieces[:, :, :width]),
-            in_order(pieces[:, :, width : 2 * width]),
-            jnp.sum(pieces[:, :, 2 * width : 2 * width + both + heads_all], axis=0),
-        ],
-        axis=1,
-    )
-    back_again = [(f * n_ctx + c, c * n_fsdp + f) for c in range(n_ctx) for f in range(n_fsdp)]
-    grad_out = lax.ppermute(grad_out, ("ctx", "fsdp"), back_again)
-    grad_out_weight = lax.all_gather(grad_out, "ctx", axis=0, tiled=True).astype(F32)
     return (
         layer_out[None],
         hidden_grad[None],
-        own_shard(outs[0]),
+        own_shard(grad_gain_norm),
         grad_in_weight,
-        own_shard(outs[1].reshape(taps, conv_total)),
-        own_shard(outs[2]),
-        own_shard(outs[3]),
-        own_shard(outs[4]),
-        own_shard(outs[5]),
-        own_shard(outs[6]),
+        own_shard(
+            jnp.concatenate(
+                [by_tap(taps_x_sum).reshape(taps, -1), jnp.sum(by_tap(taps_s_sum), axis=1)], axis=1
+            )
+        ),
+        own_shard(jnp.concatenate([bias_x_sum.reshape(-1), jnp.sum(bias_s_sum, axis=0)])),
+        own_shard(step_sum.reshape(-1)),
+        own_shard(log_sum.reshape(-1)),
+        own_shard(skip_sum.reshape(-1)),
+        own_shard(gate_sum.reshape(-1)),
         grad_out_weight,
     )
 

time: 883 us -> 581 us (0.66)
  waiting for transfers between devices: 421 us -> 0 us
  Pallas kernels: 213 us -> 405 us
  matrix products: 76.2 us -> 44.9 us
  other arithmetic: 80.6 us -> 51.1 us
  between operations: 15.9 us -> 2.39 us
    reduce_scatter x4 -> x0, waiting for transfers between devices: 243 us -> none  [the longest x1 170 us: on_device(): grad_in = lax.psum_scatter(grad_in, 'fsdp', scatter_dimension=0, tiled=True)]
    pallas_call x0 -> x2, Pallas kernels: none -> 192 us  [the longest x1 189 us: reduce_all(): pl.pallas_call(functools.partial(reduce_kernel, n, n_ctx), in_specs=[any_...]
    psum x1 -> x0, waiting for transfers between devices: 124 us -> none  [on_device(): flat = lax.psum(jnp.concatenate(small_grads), ('ctx', 'fsdp'))]
    all_gather x2 -> x0, waiting for transfers between devices: 54.5 us -> none  [the longest x1 37.1 us: on_device(): pieces = lax.all_gather(grad_in, 'ctx', axis=0).astype(F32)]
    dot_general x12 -> x8, matrix products: 76.2 us -> 44.9 us  [mm(): lax.dot_general(a, b, (contract, ((), ())), preferred_element_type=F32)]
    concatenate x3, other arithmetic: 25.3 us -> 2.33 us  [the longest x1 0.96 us: on_device(): d_in_s = jnp.concatenate([d_in_s, d_raw_all], axis=1)]
    unnamed x90 -> x115, local copies, waits for them, and re-layouts: 15.9 us -> 35.6 us
  transfers between devices with their start and end apart: 8 -> 0, of which waited for: 6 -> 0; matrix products, arithmetic and copies ran while one was open for 12% -> 0% of each run, Pallas kernels for 4% -> 0%
where the time goes in v3:
time: 581 us; the launch traced here: 572 us
  Pallas kernels  405 us (70%)
  local copies, waits for them, and re-layouts  58.4 us (10%)
  other arithmetic  51.1 us (9%)
  matrix products  44.9 us (8%)
  blocking collectives  10.3 us (2%)
    pallas_call x1, Pallas kernels, reduce_all(): pl.pallas_call(functools.partial(reduce_kernel, n, n_ctx), in_specs=[any_...  189 us
    pallas_call x1, Pallas kernels, gather_all(): pl.pallas_call(functools.partial(gather_kernel, n, n_ctx), in_specs=[any_...  168 us
    dot_general x8, matrix products, mm(): lax.dot_general(a, b, (contract, ((), ())), preferred_element_type=F32)  44.9 us
    unnamed x115, local copies, waits for them, and re-layouts  35.6 us
    pallas_call x1, Pallas kernels, scan_backward(): pl.pallas_call(functools.partial(backward_kernel, heads), grid=(count,),...  32.5 us
    pallas_call x1, Pallas kernels, scan_forward(): pl.pallas_call(functools.partial(forward_kernel, heads), grid=(count,), i...  13.3 us

profile of v3, /device:TPU:17, one launch (start us, length us, event | category | flops | bytes accessed | tf_op | source)
XLA Modules:
  0.0 572.1 jit_solution(7613840223527939281)
XLA Ops:
  0.7 6.4 %copy.39.in_weight = bf16[256,8512]{1,0:T(8,128)(2,1)} copy(bf16[256,8512]{0,1:T(8,128)(2,1)} %param.16) | data formatting | bytes 8716288 | tf_op args[4]
  7.1 0.9 slice.225
  9.1 167.7 %gather_all.1 = (bf16[4,256,2048]{2,1,0:T(8,128)(2,1)}, bf16[4,256,2048]{2,1,0:T(8,128)(2,1)}, bf16[8,256,1024]{2,1,0:T(8,128)(2,1)}, bf16[8,288,384]{2,1,0:T(8,...) custom-call(bf16[256,2048]{1,0:T(8,128)(2,1)} %bitcast.110, bf16[256,2048]{1,0:T(8,128)(2,1)} %bitcast.112, ...), custom_call_target="tpu_custom_call" | custom-call | tf_op jit(solution)/shard_map/gather_all/pallas_call | solution.py:506
  176.9 6.9 %copy.48 = f32[1024,2048]{0,1:T(8,128)} copy(bf16[1024,2048]{1,0:T(8,128)(2,1)} %bitcast.106) | data formatting | bytes 12582912 | tf_op jit(solution)/shard_map/convert_element_type | solution.py:1103
  183.7 0.9 slice_bitcast_fusion
  184.8 3.1 multiply_reduce_fusion
  187.9 5.2 fusion.7.normed_t
  193.2 3.3 multiply_convert_fusion.1
  196.6 6.0 %convert_convert_fusion = f32[1024,1024]{1,0:T(8,128)} fusion(bf16[1024,2048]{1,0:T(8,128)(2,1)S(1)} %bitcast.115, bf16[2048,1024]{1,0:T(8,128)(2,1)S(1)} %bitcast.175), kind=kOutput, calls=%fused_computation.37 | convolution fusion | flops 4297064448 | bytes 12582912 | tf_op jit(solution)/shard_map/dot_general | solution.py:20
  203.1 8.9 %multiply_convert_fusion.5 = (bf16[1024,1024]{1,0:T(8,128)(2,1)S(1)}, f32[1024,1024]{1,0:T(8,128)}) fusion(f32[1024,1024]{1,0:T(8,128)} %convert_convert_fusion, f32[1024]{0:T(1024)S(1)} %bitcast.146, f32[1024]{0:T(1024)S(1)} %bitcast.142, f32[1024]{0:T(1024)S(1)} %bitcast.144, f32[1024]{0:T(1024)S(1)} %bitcast.140, f32[1024]{0:T(1024)S(1)} %dynamic_slice.42), kind=kLoop, calls=%fused_computation.31 | loop fusion | flops 13631488 | bytes 10506240 | tf_op jit(solution)/shard_map/convert_element_type | solution.py:1114
  212.2 2.3 fusion.10
  214.7 1.0 copy-done.28
  215.7 1.6 multiply_convert_fusion.6
  217.4 0.7 fusion.27
  219.3 1.1 slice.239
  220.9 0.7 copy-done.26
  221.8 1.1 copy-done.11
  222.9 13.3 %scan_forward.1 = (f32[1024,1024]{1,0:T(8,128)S(1)}, bf16[4,128,1024]{2,1,0:T(8,128)(2,1)S(1)}) custom-call(bf16[1024,1024]{1,0:T(8,128)(2,1)S(1)} %get-tuple-element.114.x_ref, bf16[1024,128]{1,0:T(8,128)(2,1)S(1)} %copy-done.11, bf16[1024,128]{1,0:T(8,128)(2,1)S(1)} %get-tuple-element.121.c_ref, f32[1024,128]{1,0:T(8,128)S(1)} %pad.32.lam_ref, ...), custom_call_target="tpu_custom_call" | custom-call | flops 1610612736 | bytes 6291456 | tf_op jit(solution)/shard_map/scan_forward/pallas_call | solution.py:81
  236.3 8.9 %convolution_convert_fusion = bf16[1024,1024]{1,0:T(8,128)(2,1)S(1)} fusion(bf16[1024,2048]{1,0:T(8,128)(2,1)S(1)} %bitcast.117, bf16[2048,1024]{1,0:T(8,128)(2,1)} %bitcast.177), kind=kOutput, calls=%fused_computation.38 | convolution fusion | flops 4296015872 | bytes 10485760 | tf_op jit(solution)/shard_map/dot_general | solution.py:20
  245.6 0.9 copy-done.33
  246.5 1.7 copy-done.47
  248.1 7.7 %multiply_reduce_fusion.7 = (f32[1024]{0:T(1024)S(1)}, f32[1024]{0:T(1024)S(1)}, f32[1024,1024]{1,0:T(8,128)}, f32[1024,1024]{1,0:T(8,128)}) fusion(f32[1024]{0:T(1024)S(1)} %dynamic-slice_convert_fusion, f32[1024,1024]{1,0:T(8,128)S(1)} %get-tuple-element.37, bf16[1024,1024]{1,0:T(8,128)(2,1)S(1)} %convolution_convert_fusion, ...), kind=kOutput, calls=%fused_computation.30 | convolution fusion | flops 4306499584 | bytes 23080960 | tf_op jit(solution)/shard_map/dot_general | solution.py:20
  255.9 10.3 %psum.7 = f32[2,1024]{1,0:T(2,128)S(1)} all-reduce(f32[2,1024]{1,0:T(2,128)S(1)} %pad_maximum_fusion.1), channel_id=1, replica_groups=mesh['ctx'=4,'fsdp'=8] {'ctx'}, use_global_device_ids=true, to_apply=%region_3.4 | all-reduce | flops 2048 | bytes 16384 | tf_op jit(solution)/shard_map/psum | solution.py:1130
  266.2 9.0 %multiply_convert_fusion.3 = (bf16[1024,1024]{1,0:T(8,128)(2,1)}, bf16[1024,1024]{1,0:T(8,128)(2,1)}, f32[1024]{0:T(1024)S(1)}, bf16[1024,1024]{0,1:T(8,128)(2,1)}) fusion(f32[1024,1024]{1,0:T(8,128)} %get-tuple-element.109, f32[1024]{0:T(1024)S(1)} %fusion.16, f32[1024,1024]{1,0:T(8,128)} %get-tuple-element.146, f32[1024]{0:T(1024)S(1)} %bitcast.149, ...), kind=kLoop, calls=%fused_computation.26 | loop fusion | flops 25164800 | bytes 20987904 | tf_op jit(solution)/shard_map/convert_element_type | solution.py:1136
  275.2 3.9 copy.44.gate_t
  279.1 4.7 bitcast_multiply_fusion.d_mixed
  283.9 32.5 %scan_backward.1 = (f32[1024,1024]{1,0:T(8,128)S(1)}, f32[1024,128]{1,0:T(8,128)S(1)}, f32[1024,128]{1,0:T(8,128)S(1)}, f32[1024,128]{1,0:T(8,128)S(1)}, f32[1024,128]{1,0:T(8,128)S(1)}, /*index=5*/f32[1,1024]{1,0:T(1,128)S(1)}) custom-call(bf16[1024,1024]{1,0:T(8,128)(2,1)S(1)} %get-tuple-element.114.x_ref, bf16[1024,128]{1,0:T(8,128)(2,1)S(1)} %copy-done.12, ...), custom_call_target="tpu_custom_call" | custom-call | flops 3489660928 | bytes 10485760 | tf_op jit(solution)/shard_map/scan_backward/pallas_call | solution.py:222
  316.3 3.5 multiply_reduce_fusion.5
  319.9 2.8 add_convert_fusion.1.d_x
  322.7 1.1 fusion.24
  323.8 3.1 dynamic_update_slice.3
  326.9 2.5 fusion.23
  329.9 1.0 pad_maximum_fusion.d_s
  331.0 6.5 %multiply_convert_fusion = bf16[1024,2048]{1,0:T(8,128)(2,1)} fusion(bf16[1024,2048]{1,0:T(8,128)(2,1)S(1)} %bitcast.180, f32[1024]{0:T(1024)S(1)} %get-tuple-element.149, f32[1024,1024]{1,0:T(8,128)S(1)} %copy-done.32, f32[1024]{0:T(1024)S(1)} %bitcast.150, f32[1024]{0:T(1024)S(1)} %dynamic-slice_convert_fusion), kind=kOutput, calls=%fused_computation.1 | convolution fusion | flops 4302307328 | bytes 12595200 | tf_op jit(solution)/shard_map/dot_general | solution.py:20
  337.6 4.6 fusion.32
  342.2 4.6 fusion.33
  346.8 4.4 add_convert_fusion
  353.9 188.6 %reduce_all.1 = (bf16[4,256,1024]{2,1,0:T(8,128)(2,1)}, bf16[4,256,1024]{2,1,0:T(8,128)(2,1)}, bf16[4,256,384]{2,1,0:T(8,128)(2,1)}, bf16[4,128,2048]{2,1,0:T(8,...) custom-call(bf16[2048,1024]{1,0:T(8,128)(2,1)} %fusion.7.normed_t, ...), custom_call_target="tpu_custom_call" | custom-call | tf_op jit(solution)/shard_map/reduce_all/pallas_call | solution.py:921
  542.5 1.0 copy.65
  544.2 1.6 copy-done.2
  545.8 1.6 copy-done.3
  547.4 1.6 copy-done.4
  549.0 1.1 copy-done.6
  550.1 2.9 assemble.1
  553.0 3.4 copy-done
  556.4 9.4 %copy.46 = f32[256,8512]{0,1:T(8,128)} copy(f32[256,8512]{1,0:T(8,128)} %copy-done) | data formatting | bytes 17432576
  570.0 1.0 copy.74
  570.9 1.0 copy.75
  (165 shorter events, 11.7 us)
Async XLA Ops:
  0.6 7.5 %copy-start.37 = (bf16[4,544]{1,0:T(4,128)(2,1)S(1)}, bf16[4,544]{1,0:T(4,128)(2,1)}, u32[]{:S(2)}) copy-start(bf16[4,544]{1,0:T(4,128)(2,1)} %param.17) | copy-start | bytes 13060
  0.7 7.5 %copy-start.38 = (bf16[544]{0:T(1024)(128)(2,1)S(1)}, bf16[544]{0:T(1024)(128)(2,1)}, u32[]{:S(2)}) copy-start(bf16[544]{0:T(1024)(128)(2,1)} %param.18) | copy-start | bytes 3268
  0.7 7.5 %copy-start.39 = (bf16[512]{0:T(512)(128)(2,1)S(1)}, bf16[512]{0:T(512)(128)(2,1)}, u32[]{:S(2)}) copy-start(bf16[512]{0:T(512)(128)(2,1)} %param.22) | copy-start | bytes 3076
  0.7 7.5 %copy-start.40 = (bf16[256]{0:T(256)(128)(2,1)S(1)}, bf16[256]{0:T(256)(128)(2,1)}, u32[]{:S(2)}) copy-start(bf16[256]{0:T(256)(128)(2,1)} %param.15) | copy-start | bytes 1540
  0.7 7.5 %copy-start.41 = (bf16[8]{0:T(256)(128)(2,1)S(1)}, bf16[8]{0:T(256)(128)(2,1)}, u32[]{:S(2)}) copy-start(bf16[8]{0:T(256)(128)(2,1)} %param.19) | copy-start | bytes 52
  0.7 7.5 %copy-start.42 = (bf16[8]{0:T(256)(128)(2,1)S(1)}, bf16[8]{0:T(256)(128)(2,1)}, u32[]{:S(2)}) copy-start(bf16[8]{0:T(256)(128)(2,1)} %param.20) | copy-start | bytes 52
  0.7 7.5 %copy-start.43 = (bf16[8]{0:T(256)(128)(2,1)S(1)}, bf16[8]{0:T(256)(128)(2,1)}, u32[]{:S(2)}) copy-start(bf16[8]{0:T(256)(128)(2,1)} %param.21) | copy-start | bytes 52
  193.2 3.5 copy-start.44
  196.5 6.1 %copy-start.29 = (bf16[4,256,2048]{2,1,0:T(8,128)(2,1)}, bf16[4,256,2048]{2,1,0:T(8,128)(2,1)S(1)}, u32[]{:S(2)}) copy-start(bf16[4,256,2048]{2,1,0:T(8,128)(2,1)S(1)} %multiply_convert_fusion.1) | copy-start | bytes 12582916
  203.1 8.9 %copy-start.34 = (bf16[8,288,384]{2,1,0:T(8,128)(2,1)S(1)}, bf16[8,288,384]{2,1,0:T(8,128)(2,1)}, u32[]{:S(2)}) copy-start(bf16[8,288,384]{2,1,0:T(8,128)(2,1)} %get-tuple-element.35) | copy-start | bytes 5308420
  203.1 9.1 %copy-start.30 = (bf16[4,256,2048]{2,1,0:T(8,128)(2,1)S(1)}, bf16[4,256,2048]{2,1,0:T(8,128)(2,1)}, u32[]{:S(2)}) copy-start(bf16[4,256,2048]{2,1,0:T(8,128)(2,1)} %copy-done.29) | copy-start | bytes 12582916
  212.2 2.4 copy-start.22
  214.6 1.1 copy-start.28
  215.7 1.6 copy-start.18
  220.4 1.3 copy-start.24
  221.6 14.6 %copy-start.7 = (f32[1024,128]{1,0:T(8,128)}, f32[1024,128]{1,0:T(8,128)S(1)}, u32[]{:S(2)}) copy-start(f32[1024,128]{1,0:T(8,128)S(1)} %pad.32.lam_ref) | copy-start | bytes 1572868
  221.6 23.5 %copy-start.9 = (f32[1024,128]{1,0:T(8,128)}, f32[1024,128]{1,0:T(8,128)S(1)}, u32[]{:S(2)}) copy-start(f32[1024,128]{1,0:T(8,128)S(1)} %pad.33.step_ref) | copy-start | bytes 1572868
  221.8 1.1 copy-start.11
  222.9 13.3 %copy-start.31 = (bf16[4,256,2048]{2,1,0:T(8,128)(2,1)S(1)}, bf16[4,256,2048]{2,1,0:T(8,128)(2,1)}, u32[]{:S(2)}) copy-start(bf16[4,256,2048]{2,1,0:T(8,128)(2,1)} %copy-done.29) | copy-start | bytes 12582916
  236.2 8.9 %copy-start.13 = (bf16[4,128,1024]{2,1,0:T(8,128)(2,1)}, bf16[4,128,1024]{2,1,0:T(8,128)(2,1)S(1)}, u32[]{:S(2)}) copy-start(bf16[4,128,1024]{2,1,0:T(8,128)(2,1)S(1)} %get-tuple-element.41.kept_ref) | copy-start | bytes 3145732
  236.2 9.3 %copy-start.1 = (f32[1024,1024]{1,0:T(8,128)}, f32[1024,1024]{1,0:T(8,128)S(1)}, u32[]{:S(2)}) copy-start(f32[1024,1024]{1,0:T(8,128)S(1)} %get-tuple-element.37) | copy-start | bytes 12582916
  236.3 8.9 %copy-start.15 = (bf16[4,256,2048]{2,1,0:T(8,128)(2,1)S(1)}, bf16[4,256,2048]{2,1,0:T(8,128)(2,1)}, u32[]{:S(2)}) copy-start(bf16[4,256,2048]{2,1,0:T(8,128)(2,1)} %get-tuple-element.39) | copy-start | bytes 12582916
  245.2 1.3 copy-start.33
  245.2 2.9 copy-start.47
  279.1 4.7 copy-start.5
  279.1 4.7 copy-start.8
  279.1 4.7 copy-start.10
  279.1 4.7 copy-start.12
  279.1 4.7 copy-start.14
  283.8 32.5 %copy-start.16 = (f32[1024,1024]{1,0:T(8,128)S(1)}, f32[1024,1024]{1,0:T(8,128)}, u32[]{:S(2)}) copy-start(f32[1024,1024]{1,0:T(8,128)} %convert_convert_fusion) | copy-start | bytes 12582916
  283.8 32.5 %copy-start.17 = (f32[1024,1024]{1,0:T(8,128)S(1)}, f32[1024,1024]{1,0:T(8,128)}, u32[]{:S(2)}) copy-start(f32[1024,1024]{1,0:T(8,128)} %get-tuple-element.115) | copy-start | bytes 12582916
  319.8 2.9 copy-start.25
  319.8 2.9 copy-start.27
  319.9 7.0 %copy-start.19 = (f32[1024,256]{1,0:T(8,128)S(1)}, f32[1024,256]{1,0:T(8,128)}, u32[]{:S(2)}) copy-start(f32[1024,256]{1,0:T(8,128)} %copy-done.18) | copy-start | bytes 3145732
  326.9 4.0 copy-start.32
  326.9 4.1 copy-start.48
  331.0 6.5 %copy-start.20 = (bf16[1024,1024]{1,0:T(8,128)(2,1)S(1)}, bf16[1024,1024]{1,0:T(8,128)(2,1)}, u32[]{:S(2)}) copy-start(bf16[1024,1024]{1,0:T(8,128)(2,1)} %get-tuple-element.117.d_z) | copy-start | bytes 6291460
  331.0 6.6 %copy-start.46 = (bf16[8,256,1024]{2,1,0:T(8,128)(2,1)S(1)}, bf16[8,256,1024]{2,1,0:T(8,128)(2,1)}, u32[]{:S(2)}) copy-start(bf16[8,256,1024]{2,1,0:T(8,128)(2,1)} %get-tuple-element.38) | copy-start | bytes 12582916
  337.6 4.6 copy-start.21
  337.6 4.6 copy-start.45
  342.2 4.6 copy-start.23
  544.2 1.6 copy-start.2
  545.8 1.6 copy-start.3
  547.4 1.6 copy-start.4
  549.0 1.1 copy-start.6
  553.0 3.4 copy-start
  556.4 13.6 %copy-start.36 = (bf16[256,2048]{1,0:T(8,128)(2,1)S(1)}, bf16[256,2048]{1,0:T(8,128)(2,1)}, u32[]{:S(2)}) copy-start(bf16[256,2048]{1,0:T(8,128)(2,1)} %get-tuple-element.48) | copy-start | bytes 3145732
  556.4 14.6 %copy-start.35 = (bf16[256,2048]{1,0:T(8,128)(2,1)S(1)}, bf16[256,2048]{1,0:T(8,128)(2,1)}, u32[]{:S(2)}) copy-start(bf16[256,2048]{1,0:T(8,128)(2,1)} %get-tuple-element.49) | copy-start | bytes 3145732
  (1 other events, 0.8 us)

commit v4 on v3

v4 whole, which is shorter than its diff:
```python
import functools

import jax
import jax.numpy as jnp
from jax import lax
from jax.experimental import pallas as pl
from jax.experimental.pallas import tpu as pltpu
from jax.sharding import PartitionSpec as P

HEAD = 64
STATE = 128
BLOCK = 256
LANES = 128
EPS = 1e-05
F32 = jnp.float32
BF16 = jnp.bfloat16


def mm(a, b, contract=((1,), (0,))):
    return lax.dot_general(a, b, (contract, ((), ())), preferred_element_type=F32)


def mm_exact(a, b, contract=((1,), (0,))):
    return lax.dot_general(
        a, b, (contract, ((), ())), precision=lax.Precision.HIGHEST, preferred_element_type=F32
    )


def iota2(shape, axis):
    return lax.broadcasted_iota(jnp.int32, shape, axis)


def levels(lam, step):
    tri = (iota2((BLOCK, BLOCK), 0) >= iota2((BLOCK, BLOCK), 1)).astype(F32)
    level = mm_exact(tri, lam)
    across = level.T
    last = level[BLOCK - 1 : BLOCK, :]
    weight = jnp.exp(level - last) * step
    return level, across, jnp.exp(-last), weight, jnp.exp(-level)


def pair_of(array, first, low_half):
    return jnp.where(low_half, array[:, first : first + 1], array[:, first + 1 : first + 2])


def spread(level, across, head):
    return jnp.exp(-jnp.abs(level[:, head : head + 1] - across[head : head + 1, :]))


def silu_and_slope(v):
    s = jax.nn.sigmoid(v)
    return v * s, s * (1.0 + v * (1.0 - s))


def own_lanes(array, me, heads, back=False):
    shift = me * heads if back else lax.rem(LANES - me * heads, LANES)
    return pltpu.roll(array, shift, 1)


def column_valid(length_ref, block):
    at = iota2((BLOCK, 1), 0) + block * BLOCK
    return (at < length_ref[0]).astype(F32)


def forward_kernel(
    heads,
    length_ref,
    px_ref,
    ps_ref,
    pz_ref,
    up_ref,
    w_o,
    taps_x_ref,
    taps_s_ref,
    gate_gain_ref,
    skip_ref,
    head_ref,
    x_ref,
    b_ref,
    c_ref,
    slope_x_ref,
    slope_s_ref,
    lam_ref,
    step_ref,
    chain_ref,
    kept_ref,
    y_ref,
    dyn_ref,
    stat_ref,
    state,
    before_x,
    before_s,
    v_o,
    load_sem,
):
    block = pl.program_id(0)
    load = pltpu.make_async_copy(w_o, v_o, load_sem)

    @pl.when(block == 0)
    def _():
        load.start()
        state[...] = jnp.zeros_like(state)
        before_x[...] = jnp.zeros_like(before_x)
        before_s[...] = jnp.zeros_like(before_s)

    valid = column_valid(length_ref, block)
    low_half = iota2((1, LANES), 1) < HEAD
    taps = taps_x_ref.shape[0] - 1

    def conv(current, before, weight):
        padded = jnp.concatenate([before, current], axis=0)
        total = weight[taps : taps + 1]
        for k in range(taps):
            first = 8 - (taps - 1) + k
            total = total + weight[k : k + 1] * padded[first : first + BLOCK]
        return silu_and_slope(total)

    shared = ps_ref[...].astype(F32)
    both = shared[:, : 2 * STATE]
    active, slope = conv(both, before_s[...], taps_s_ref[...])
    before_s[...] = both[BLOCK - 8 :]
    slope_s_ref[...] = slope.astype(BF16)
    rows_b, rows_c = active[:, :STATE].astype(BF16), active[:, STATE:].astype(BF16)
    b_ref[...] = rows_b
    c_ref[...] = rows_c
    raw = own_lanes(shared[:, 2 * STATE :], lax.axis_index("ctx"), heads)
    raw = raw + head_ref[0:1]
    own = iota2((1, LANES), 1) < heads
    step = jnp.where(own, valid * jax.nn.softplus(raw), 0.0)
    lam = step * head_ref[1:2]
    step_ref[...] = step
    lam_ref[...] = lam
    chain_ref[...] = jnp.where(own, valid * jax.nn.sigmoid(raw), 0.0)

    gram = mm(rows_c, rows_b, ((1,), (1,)))
    level, across, last, weight, fade = levels(lam, step)
    kept_ref[0] = state[...].astype(BF16)
    entering = mm(rows_c, state[...].astype(BF16))
    by_state = rows_b.T
    squares = jnp.zeros((BLOCK, LANES), F32)
    for first in range(0, heads, 2):
        lanes = slice(first * HEAD, (first + 2) * HEAD)
        current = px_ref[:, lanes].astype(F32)
        active, slope = conv(current, before_x[:, lanes], taps_x_ref[:, lanes])
        before_x[:, lanes] = current[BLOCK - 8 :]
        slope_x_ref[:, lanes] = slope.astype(BF16)
        x_low = active.astype(BF16)
        x_ref[:, lanes] = x_low
        x = x_low.astype(F32)
        scaled = x * pair_of(step, first, low_half)
        total = pair_of(fade, first, low_half) * entering[:, lanes] + skip_ref[:, lanes] * x
        for head, keep in ((first, low_half), (first + 1, jnp.logical_not(low_half))):
            mixing = (gram * spread(level, across, head)).astype(BF16)
            total += mm(mixing, jnp.where(keep, scaled, 0.0).astype(BF16))
        y_ref[:, lanes] = total
        update = mm(by_state, (x * pair_of(weight, first, low_half)).astype(BF16))
        state[:, lanes] = state[:, lanes] * pair_of(last, first, low_half) + update
        gated = total * jax.nn.silu(pz_ref[:, lanes].astype(F32))
        squares += gated * gated

    @pl.when(block == 0)
    def _():
        load.wait()

    d_yn = valid * mm(up_ref[0], v_o[...], ((1,), (1,)))
    dyn_ref[...] = d_yn
    gated = y_ref[...] * jax.nn.silu(pz_ref[...].astype(F32))
    terms = gate_gain_ref[...] * d_yn * gated
    square = jnp.sum(squares, axis=1, keepdims=True)
    along = jnp.sum(terms, axis=1, keepdims=True)
    lane = iota2((1, LANES), 1)
    both_sums = jnp.where(lane == 0, square, 0.0) + jnp.where(lane == 1, along, 0.0)
    stat_ref[...] = both_sums.T[0:8]


def scan_forward(length, px, ps, pz, upstream, w_o, taps_x, taps_s, gate_gain, skip, head):
    tokens, width = px.shape
    heads = width // HEAD
    count = tokens // BLOCK
    model = w_o.shape[1]
    by_block = lambda i: (i, 0)
    at_block = lambda size: pl.BlockSpec((BLOCK, size), by_block)
    whole = lambda a: pl.BlockSpec(a.shape, lambda i: (0, 0))
    low = lambda *shape: jax.ShapeDtypeStruct(shape, BF16)
    full = lambda *shape: jax.ShapeDtypeStruct(shape, F32)
    return pl.pallas_call(
        functools.partial(forward_kernel, heads),
        grid=(count,),
        in_specs=[
            pl.BlockSpec(memory_space=pltpu.SMEM),
            at_block(width),
            at_block(ps.shape[1]),
            at_block(width),
            pl.BlockSpec((1, BLOCK, model), lambda i: (i, 0, 0)),
            pl.BlockSpec(memory_space=pl.ANY),
            whole(taps_x),
            whole(taps_s),
            whole(gate_gain),
            whole(skip),
            whole(head),
        ],
        out_specs=[
            at_block(width),
            at_block(STATE),
            at_block(STATE),
            at_block(width),
            at_block(2 * STATE),
            at_block(LANES),
            at_block(LANES),
            at_block(LANES),
            pl.BlockSpec((1, STATE, width), lambda i: (i, 0, 0)),
            at_block(width),
            at_block(width),
            pl.BlockSpec((8, BLOCK), lambda i: (0, i)),
        ],
        out_shape=[
            low(tokens, width),
            low(tokens, STATE),
            low(tokens, STATE),
            low(tokens, width),
            low(tokens, 2 * STATE),
            full(tokens, LANES),
            full(tokens, LANES),
            full(tokens, LANES),
            low(count, STATE, width),
            full(tokens, width),
            full(tokens, width),
            full(8, tokens),
        ],
        scratch_shapes=[
            pltpu.VMEM((STATE, width), F32),
            pltpu.VMEM((8, width), F32),
            pltpu.VMEM((8, 2 * STATE), F32),
            pltpu.VMEM(w_o.shape, BF16),
            pltpu.SemaphoreType.DMA,
        ],
        compiler_params=pltpu.CompilerParams(vmem_limit_bytes=56 * 1024 * 1024),
        cost_estimate=pl.CostEstimate(
            flops=2 * tokens * width * (2 * BLOCK + 2 * STATE + model),
            bytes_accessed=tokens * width * 24,
            transcendentals=tokens * heads * BLOCK,
        ),
        name="scan_forward",
    )(length, px, ps, pz, upstream, w_o, taps_x, taps_s, gate_gain, skip, head)


def head_sums(product, chooser):
    high = product.astype(BF16)
    rest = (product - high.astype(F32)).astype(BF16)
    return mm(high, chooser) + mm(rest, chooser)


def backward_kernel(
    heads,
    channels,
    length_ref,
    px_ref,
    ps_ref,
    pz_ref,
    x_ref,
    b_ref,
    c_ref,
    slope_x_ref,
    slope_s_ref,
    lam_ref,
    step_ref,
    chain_ref,
    kept_ref,
    y_ref,
    dyn_ref,
    stat_ref,
    w_o,
    w_z,
    w_x,
    w_s,
    taps_x_ref,
    taps_s_ref,
    gate_gain_ref,
    skip_ref,
    head_ref,
    ynt_ref,
    mixed_ref,
    normed_ref,
    dz_ref,
    dx_ref,
    ds_ref,
    small_ref,
    back,
    mixed_grads,
    for_step,
    for_level,
    left,
    right,
    sums,
    after_x,
    after_s,
    v_y,
    v_o,
    v_z,
    v_x,
    v_s,
    load_sem,
):
    turn = pl.program_id(0)
    block = pl.num_programs(0) - 1 - turn
    loads = [
        pltpu.make_async_copy(source, target, load_sem.at[i])
        for i, (source, target) in enumerate(((w_o, v_o), (w_z, v_z), (w_x, v_x), (w_s, v_s)))
    ]

    @pl.when(turn == 0)
    def _():
        for copy in loads:
            copy.start()
        back[...] = jnp.zeros_like(back)
        small_ref[...] = jnp.zeros_like(small_ref)
        after_x[...] = jnp.zeros_like(after_x)
        after_s[...] = jnp.zeros_like(after_s)

    width = x_ref.shape[1]
    valid = column_valid(length_ref, block)
    columns = stat_ref[...].T
    scale = lax.rsqrt(columns[:, 0:1] / channels + EPS)
    slant = scale * scale * scale * columns[:, 1:2] / channels
    taps = taps_x_ref.shape[0] - 1

    rows_b, rows_c = b_ref[...], c_ref[...]
    step = step_ref[...]
    lam = lam_ref[...]
    gram = mm(rows_c, rows_b, ((1,), (1,)))
    gram_t = mm(rows_b, rows_c, ((1,), (1,)))
    level, across, last, weight, fade = levels(lam, step)
    out_decay = jnp.exp(level - level[BLOCK - 1 : BLOCK, :])
    step_across = step.T
    at_row, at_col = iota2((BLOCK, BLOCK), 0), iota2((BLOCK, BLOCK), 1)
    order = (at_row > at_col).astype(F32) - (at_row < at_col).astype(F32)
    low_half = iota2((1, LANES), 1) < HEAD
    lane = iota2((1, LANES), 1)
    by_state = rows_c.T
    kept = kept_ref[0]
    old_back = back[...].astype(BF16)
    entering = mm(rows_c, kept)
    leaving = mm(rows_b, old_back)
    at_last = jnp.sum(kept.astype(F32) * back[...], axis=0, keepdims=True)
    mixed_grads[...] = jnp.zeros_like(mixed_grads)
    left[...] = jnp.zeros_like(left)
    right[...] = jnp.zeros_like(right)
    sums[...] = jnp.zeros_like(sums)
    d_b = jnp.zeros((BLOCK, STATE), F32)
    d_c = jnp.zeros((BLOCK, STATE), F32)

    def conv_back(d_conv, after, current, weight):
        padded = jnp.concatenate([d_conv, after], axis=0)
        d_in = jnp.zeros_like(d_conv)
        grads = []
        for k in range(taps):
            moved = padded[taps - 1 - k : taps - 1 - k + BLOCK]
            d_in += weight[k : k + 1] * moved
            grads.append(jnp.sum(current * moved, axis=0, keepdims=True))
        grads.append(jnp.sum(d_conv, axis=0, keepdims=True))
        return d_in, jnp.concatenate(grads, axis=0)

    for first in range(0, heads, 2):
        lanes = slice(first * HEAD, (first + 2) * HEAD)
        x_low = x_ref[:, lanes]
        x = x_low.astype(F32)
        raw = pz_ref[:, lanes].astype(F32)
        gate, gate_slope = silu_and_slope(raw)
        mixed = y_ref[:, lanes]
        d_yn = dyn_ref[:, lanes]
        gain = gate_gain_ref[:, lanes]
        gated = mixed * gate
        v_y[:, lanes] = (valid * (gated * scale * gain)).astype(BF16)
        small_ref[taps + 1 : taps + 2, lanes] += jnp.sum(
            d_yn * (gated * scale), axis=0, keepdims=True
        )
        d_gated = scale * (gain * d_yn) - gated * slant
        dz_ref[:, lanes] = (d_gated * mixed * gate_slope).astype(BF16)
        grad_low = (d_gated * gate).astype(BF16)
        grad = grad_low.astype(F32)
        through = jnp.zeros((BLOCK, LANES), F32)
        for head, keep in ((first, low_half), (first + 1, jnp.logical_not(low_half))):
            decay = spread(level, across, head)
            grad_own = jnp.where(keep, grad, 0.0).astype(BF16)
            pairs = mm(grad_own, x_low, ((1,), (1,)))
            through += mm((gram_t * decay).astype(BF16), grad_own)
            scaled = decay * pairs * step_across[head : head + 1, :]
            mixed_grads[...] += scaled
            ordered = gram * scaled * order
            left[...] = jnp.where(
                lane == head, jnp.sum(ordered, axis=1, keepdims=True), left[...]
            )
            right[head : head + 1, :] = jnp.sum(ordered, axis=0, keepdims=True)
        weight_pair = pair_of(weight, first, low_half)
        step_pair = pair_of(step, first, low_half)
        fade_pair = pair_of(fade, first, low_half)
        out_pair = pair_of(out_decay, first, low_half)
        leave = leaving[:, lanes]
        d_x = step_pair * through + weight_pair * leave + skip_ref[:, lanes] * grad
        for_step[:, lanes] = x * (through + out_pair * leave)
        weighted = weight_pair * x
        faded = fade_pair * grad
        for_level[:, lanes] = weighted * leave - faded * entering[:, lanes]
        sums[0:1, lanes] = jnp.sum(weighted * leave, axis=0, keepdims=True)
        sums[2:3, lanes] = jnp.sum(x * grad, axis=0, keepdims=True)
        faded_low = faded.astype(BF16)
        d_b += mm(weighted.astype(BF16), old_back[:, lanes], ((1,), (1,)))
        d_c += mm(faded_low, kept[:, lanes], ((1,), (1,)))
        back[:, lanes] = back[:, lanes] * pair_of(last, first, low_half) + mm(by_state, faded_low)
        d_conv = d_x * slope_x_ref[:, lanes].astype(F32)
        d_in, grads = conv_back(
            d_conv, after_x[:, lanes], px_ref[:, lanes].astype(F32), taps_x_ref[:, lanes]
        )
        after_x[:, lanes] = d_conv[0:8]
        dx_ref[:, lanes] = d_in.astype(BF16)
        small_ref[0 : taps + 1, lanes] += grads

    all_pairs = mixed_grads[...]
    d_b = d_b + mm(all_pairs.T.astype(BF16), rows_c)
    d_c = d_c + mm(all_pairs.astype(BF16), rows_b)
    d_conv = jnp.concatenate([d_b, d_c], axis=1) * slope_s_ref[...].astype(F32)
    d_in, grads = conv_back(
        d_conv, after_s[...], ps_ref[:, : 2 * STATE].astype(F32), taps_s_ref[...]
    )
    after_s[...] = d_conv[0:8]
    ds_ref[:, : 2 * STATE] = d_in.astype(BF16)
    small_ref[0 : taps + 1, width:] += grads

    chooser = (iota2((width, LANES), 0) // HEAD == iota2((width, LANES), 1)).astype(BF16)
    d_step = head_sums(for_step[...], chooser)
    sums[1:2, :] = at_last
    total = head_sums(sums[...], chooser)
    d_level = head_sums(for_level[...], chooser) - left[...] + right[...].T
    final = -total[0:1, :] - last * total[1:2, :]
    d_level = d_level + jnp.where(iota2((BLOCK, 1), 0) == BLOCK - 1, final, 0.0)
    d_lam = mm_exact((at_row <= at_col).astype(F32), d_level)
    d_raw = (d_step + d_lam * head_ref[1:2]) * chain_ref[...]
    head_row = taps + 2
    small_ref[head_row : head_row + 1, 0:LANES] += jnp.sum(d_raw, axis=0, keepdims=True)
    small_ref[head_row : head_row + 1, LANES : 2 * LANES] += jnp.sum(
        d_lam * lam, axis=0, keepdims=True
    )
    small_ref[head_row : head_row + 1, 2 * LANES : 3 * LANES] += total[2:3, :]
    ds_ref[:, 2 * STATE :] = own_lanes(d_raw, lax.axis_index("ctx"), heads, True).astype(BF16)

    @pl.when(turn == 0)
    def _():
        for copy in loads:
            copy.wait()

    normed_gate = v_y[...]
    ynt_ref[...] = normed_gate.T
    mixed_ref[0] = mm(normed_gate, v_o[...]).astype(BF16)
    normed_ref[0] = (
        mm(dz_ref[...], v_z[...], ((1,), (1,)))
        + mm(dx_ref[...], v_x[...], ((1,), (1,)))
        + mm(ds_ref[...], v_s[...], ((1,), (1,)))
    ).astype(BF16)


def scan_backward(
    channels, length, px, ps, pz, kept_parts, stats, w_o, w_z, w_x, w_s, taps_x, taps_s, gate_gain, skip, head
):
    x, rows_b, rows_c, slope_x, slope_s, lam, step, chain, kept, y, d_yn = kept_parts
    tokens, width = px.shape
    heads = width // HEAD
    count = tokens // BLOCK
    model = w_o.shape[1]
    shared_width = ps.shape[1]
    taps = taps_x.shape[0] - 1
    by_block = lambda i: (count - 1 - i, 0)
    at_block = lambda size: pl.BlockSpec((BLOCK, size), by_block)
    whole = lambda a: pl.BlockSpec(a.shape, lambda i: (0, 0))
    any_space = pl.BlockSpec(memory_space=pl.ANY)
    low = lambda *shape: jax.ShapeDtypeStruct(shape, BF16)
    part = lambda a, b: pl.BlockSpec((1, a, b), lambda i: (count - 1 - i, 0, 0))
    small_shape = (8, width + 2 * STATE)
    return pl.pallas_call(
        functools.partial(backward_kernel, heads, channels),
        grid=(count,),
        in_specs=[
            pl.BlockSpec(memory_space=pltpu.SMEM),
            at_block(width),
            at_block(shared_width),
            at_block(width),
            at_block(width),
            at_block(STATE),
            at_block(STATE),
            at_block(width),
            at_block(2 * STATE),
            at_block(LANES),
            at_block(LANES),
            at_block(LANES),
            part(STATE, width),
            at_block(width),
            at_block(width),
            pl.BlockSpec((8, BLOCK), lambda i: (0, count - 1 - i)),
            any_space,
            any_space,
            any_space,
            any_space,
            whole(taps_x),
            whole(taps_s),
            whole(gate_gain),
            whole(skip),
            whole(head),
        ],
        out_specs=[
            pl.BlockSpec((width, BLOCK), lambda i: (0, count - 1 - i)),
            part(BLOCK, model),
            part(BLOCK, model),
            at_block(width),
            at_block(width),
            at_block(shared_width),
            pl.BlockSpec(small_shape, lambda i: (0, 0)),
        ],
        out_shape=[
            low(width, tokens),
            low(count, BLOCK, model),
            low(count, BLOCK, model),
            low(tokens, width),
            low(tokens, width),
            low(tokens, shared_width),
            jax.ShapeDtypeStruct(small_shape, F32),
        ],
        scratch_shapes=[
            pltpu.VMEM((STATE, width), F32),
            pltpu.VMEM((BLOCK, BLOCK), F32),
            pltpu.VMEM((BLOCK, width), F32),
            pltpu.VMEM((BLOCK, width), F32),
            pltpu.VMEM((BLOCK, LANES), F32),
            pltpu.VMEM((LANES, BLOCK), F32),
            pltpu.VMEM((8, width), F32),
            pltpu.VMEM((8, width), F32),
            pltpu.VMEM((8, 2 * STATE), F32),
            pltpu.VMEM((BLOCK, width), BF16),
            pltpu.VMEM(w_o.shape, BF16),
            pltpu.VMEM(w_z.shape, BF16),
            pltpu.VMEM(w_x.shape, BF16),
            pltpu.VMEM(w_s.shape, BF16),
            pltpu.SemaphoreType.DMA((4,)),
        ],
        compiler_params=pltpu.CompilerParams(vmem_limit_bytes=56 * 1024 * 1024),
        cost_estimate=pl.CostEstimate(
            flops=2 * tokens * width * (4 * BLOCK + 5 * STATE + 3 * model),
            bytes_accessed=tokens * width * 40,
            transcendentals=tokens * heads * BLOCK,
        ),
        name="scan_backward",
    )(
        length, px, ps, pz, x, rows_b, rows_c, slope_x, slope_s, lam, step, chain, kept, y, d_yn, stats, w_o, w_z, w_x, w_s, taps_x, taps_s, gate_gain, skip, head
    )


MESH = pl.DeviceIdType.MESH
SMALL_ROWS = 32


def ring_place(index, half):
    a, b = index // 2, index % 2
    return a + b * (2 * half - 1 - 2 * a)


def ring_index(place, half):
    b = place // half
    return 2 * (place + b * (2 * half - 1 - 2 * place)) + b


class Ring:
    def __init__(self, n):
        self.n, self.half = n, n // 2
        self.me, self.shard = lax.axis_index("ctx"), lax.axis_index("fsdp")
        self.place = ring_place(self.shard, self.half)

    def at(self, steps):
        return ring_index(lax.rem(self.place + steps + 2 * self.n, self.n), self.half)

    def neighbour(self, way):
        return (self.me, self.at(1 if way == 0 else -1))


def remote(source, target, send, recv, device):
    return pltpu.make_async_remote_copy(
        src_ref=source,
        dst_ref=target,
        send_sem=send,
        recv_sem=recv,
        device_id=device,
        device_id_type=MESH,
    )


def gather_kernel(
    n,
    n_ctx,
    hidden,
    cotangent,
    in_weight_t,
    small,
    out_weight,
    cotangent_all,
    w_x,
    w_s,
    w_z,
    w_o,
    small_out,
    proj_x,
    proj_s,
    proj_z,
    normed_t,
    v_hidden,
    v_normed,
    v_x,
    v_s,
    v_z,
    v_small,
    raw_x,
    raw_s,
    raw_z,
    out_x,
    out_s,
    out_z,
    out_t,
    v_gain,
    load_sem,
    local_sem,
    store_sem,
    ring_send,
    ring_recv,
    ctx_send,
    ctx_recv,
    piece_send,
    piece_recv,
):
    ring = Ring(n)
    me, shard = ring.me, ring.shard
    width, model = v_x.shape[1], v_x.shape[0]
    inner = width * n_ctx
    r = model // n
    shared = in_weight_t.shape[0] - 2 * inner
    row = me // 2
    other_core = (me + 1 - 2 * (me % 2), shard)
    other_row = (me + 2 - 4 * row, shard)
    piece = w_o.shape[1]
    sent_as = shard * n_ctx + me
    piece_to = (sent_as // n, sent_as % n)
    held_as = me * n + shard
    piece_from = (held_as % n_ctx, held_as // n_ctx)
    moves = sent_as != held_as

    barrier = pltpu.get_barrier_semaphore()
    for device in (other_core, other_row, ring.neighbour(0), ring.neighbour(1)):
        pl.semaphore_signal(barrier, inc=1, device_id=device, device_id_type=MESH)

    loads = [
        pltpu.make_async_copy(source, target, load_sem.at[i])
        for i, (source, target) in enumerate(
            (
                (in_weight_t.at[pl.ds(pl.multiple_of(inner + me * width, width), width)], raw_x),
                (in_weight_t.at[pl.ds(2 * inner, shared)], raw_s.at[pl.ds(0, shared)]),
                (small, v_small.at[shard]),
                (hidden, v_hidden.at[me]),
                (in_weight_t.at[pl.ds(pl.multiple_of(me * width, width), width)], raw_z),
            )
        )
    ]
    for copy in loads:
        copy.start()

    @pl.when(moves)
    def _():
        for device in (piece_to, piece_from):
            pl.semaphore_signal(barrier, inc=1, device_id=device, device_id_type=MESH)
        pl.semaphore_wait(barrier, 6)

    @pl.when(jnp.logical_not(moves))
    def _():
        pl.semaphore_wait(barrier, 4)

    half, quarter = width // 2, w_o.shape[2] // 4
    rows = r // 2
    both_rows = lambda index, way: pl.ds(pl.multiple_of((2 * index + way) * rows, 16), rows)
    x_part = lambda a, sub: lambda index, way: a.at[both_rows(index, way), pl.ds(sub * half, half)]
    s_part = lambda index, way: v_s.at[both_rows(index, way)]
    small_part = lambda index, way: v_small.at[index, pl.ds(way * SMALL_ROWS // 2, SMALL_ROWS // 2)]
    o_part = lambda sub: lambda index, way: w_o.at[
        index, :, pl.ds((2 * way + sub) * quarter, quarter)
    ]
    phases = (
        ((0, small_part), (1, s_part), (2, x_part(v_x, 0)), (3, x_part(v_x, 1))),
        ((4, x_part(v_z, 0)), (5, x_part(v_z, 1))),
        ((6, o_part(0)), (7, o_part(1))),
    )

    def hop(stream, way, step):
        number, part = stream
        place = part(ring.at(-step if way == 0 else step), way)
        return remote(
            place, place, ring_send.at[number, way], ring_recv.at[number, way, step],
            ring.neighbour(way),
        )

    def arrives(stream, way, step):
        number, part = stream
        landed = part(ring.at(-step - 1 if way == 0 else step + 1), way)
        return remote(
            landed, landed, ring_send.at[number, way], ring_recv.at[number, way, step],
            ring.neighbour(way),
        )

    def start_stream(stream):
        for way in (0, 1):
            hop(stream, way, 0).start()

    def to_row(i, a, whole):
        return remote(a, whole.at[me], ctx_send.at[i, 0], ctx_recv.at[i, 0], other_row)

    def to_core(i, a, whole):
        return remote(a, whole.at[me], ctx_send.at[i, 1], ctx_recv.at[i, 1], other_core)

    def pass_on(i, whole):
        beyond = whole.at[other_row[0]]
        return remote(beyond, beyond, ctx_send.at[i, 2], ctx_recv.at[i, 2], other_core)

    to_row(0, hidden, v_hidden).start()
    to_core(0, hidden, v_hidden).start()
    own_rows = pl.ds(pl.multiple_of(shard * r, 16), r)
    loads[2].wait()
    start_stream(phases[0][0])
    loads[0].wait()
    v_x[own_rows, :] = raw_x[...].T
    start_stream(phases[0][2])
    start_stream(phases[0][3])
    loads[1].wait()
    raw_s[shared:, :] = jnp.zeros((raw_s.shape[0] - shared, r), BF16)
    v_s[own_rows, :] = raw_s[...].T
    start_stream(phases[0][1])
    own_piece = out_weight.at[pl.ds(pl.multiple_of(me * piece, 16), piece)]
    send_piece = remote(own_piece, w_o.at[piece_to[1]], piece_send, piece_recv, piece_to)
    keep_piece = pltpu.make_async_copy(own_piece, w_o.at[shard], piece_send)

    def move_piece(wait):
        @pl.when(moves)
        def _():
            send_piece.wait() if wait else send_piece.start()

        @pl.when(jnp.logical_not(moves))
        def _():
            keep_piece.wait() if wait else keep_piece.start()

    keep_cotangent = pltpu.make_async_copy(cotangent, cotangent_all.at[me], local_sem)
    keep_cotangent.start()
    loads[3].wait()
    loads[4].wait()
    v_z[own_rows, :] = raw_z[...].T

    def run_phase(number, work, after):
        def body(step, carry):
            for stream in phases[number]:
                for way in (0, 1):
                    arrives(stream, way, step).wait_recv()
                    hop(stream, way, step).wait_send()
                    hop(stream, way, step + 1).start()
            if work is not None:

                @pl.when(step < n_ctx)
                def _():
                    work(step)

            return carry

        lax.fori_loop(0, n - 2, body, 0)
        after()
        for stream in phases[number]:
            for way in (0, 1):
                arrives(stream, way, n - 2).wait_recv()
                hop(stream, way, n - 2).wait_send()

    tokens = v_hidden.shape[1]

    def project_first(chunk):
        at = pl.ds(pl.multiple_of(chunk * tokens, tokens), tokens)
        resid = v_hidden[chunk].astype(F32)
        scale = lax.rsqrt(jnp.mean(resid * resid, axis=1, keepdims=True) + EPS)
        normed = (resid * scale * v_gain[...]).astype(BF16)
        v_normed[at, :] = normed
        out_x[at, :] = mm(normed, v_x[...]).astype(BF16)
        out_s[at, :] = mm(normed, v_s[...]).astype(BF16)

    def project_gate(chunk):
        at = pl.ds(pl.multiple_of(chunk * tokens, tokens), tokens)
        normed = v_normed[at, :]
        out_z[at, :] = mm(normed, v_z[...]).astype(BF16)
        out_t[chunk] = normed.T

    stores = [
        pltpu.make_async_copy(source, target, store_sem.at[i])
        for i, (source, target) in enumerate(
            (
                (v_x, w_x),
                (v_s, w_s),
                (v_small, small_out),
                (out_x, proj_x),
                (out_s, proj_s),
                (v_z, w_z),
                (out_z, proj_z),
                (out_t, normed_t),
            )
        )
    ]

    def after_first():
        for stream in phases[1]:
            start_stream(stream)
        to_row(0, hidden, v_hidden).wait_recv()
        pass_on(0, v_hidden).start()
        move_piece(False)
        to_row(1, cotangent, cotangent_all).start()
        to_core(1, cotangent, cotangent_all).start()
        to_row(0, hidden, v_hidden).wait_send()
        to_core(0, hidden, v_hidden).wait()
        pass_on(0, v_hidden).wait()

    def after_second():
        move_piece(True)
        for stream in phases[2]:
            start_stream(stream)
        to_row(1, cotangent, cotangent_all).wait_recv()
        pass_on(1, cotangent_all).start()

    def after_third():
        to_row(1, cotangent, cotangent_all).wait_send()
        to_core(1, cotangent, cotangent_all).wait()
        pass_on(1, cotangent_all).wait()
        keep_cotangent.wait()

    run_phase(0, None, after_first)
    for f in range(n):
        v_gain[:, f * r : (f + 1) * r] = v_small[f, 0:1, 0:r].astype(F32)
    for copy in stores[0:3]:
        copy.start()
    run_phase(1, project_first, after_second)
    for copy in stores[3:6]:
        copy.start()
    run_phase(2, project_gate, after_third)
    for copy in stores[6:]:
        copy.start()
    for copy in stores:
        copy.wait()


def gather_all(n, n_ctx, hidden, cotangent, in_weight_t, small, out_weight, shared_width):
    own, model = hidden.shape
    tokens = own * n_ctx
    width = out_weight.shape[0] * n // n_ctx
    rows = in_weight_t.shape[1]
    any_space = pl.BlockSpec(memory_space=pl.ANY)
    low = lambda *shape: jax.ShapeDtypeStruct(shape, BF16)
    v_low = lambda *shape: pltpu.VMEM(shape, BF16)
    dma = pltpu.SemaphoreType.DMA
    return pl.pallas_call(
        functools.partial(gather_kernel, n, n_ctx),
        in_specs=[any_space] * 5,
        out_specs=[any_space] * 10,
        out_shape=[
            low(n_ctx, own, model),
            low(model, width),
            low(model, shared_width),
            low(model, width),
            low(n, width // n, model),
            low(n, small.shape[0], small.shape[1]),
            low(tokens, width),
            low(tokens, shared_width),
            low(tokens, width),
            low(n_ctx, model, own),
        ],
        scratch_shapes=[
            v_low(n_ctx, own, model),
            v_low(tokens, model),
            v_low(model, width),
            v_low(model, shared_width),
            v_low(model, width),
            v_low(n, small.shape[0], small.shape[1]),
            v_low(width, rows),
            v_low(shared_width, rows),
            v_low(width, rows),
            v_low(tokens, width),
            v_low(tokens, shared_width),
            v_low(tokens, width),
            v_low(n_ctx, model, own),
            pltpu.VMEM((1, model), F32),
            dma((5,)),
            dma,
            dma((8,)),
            dma((8, 2)),
            dma((8, 2, n - 1)),
            dma((2, 3)),
            dma((2, 3)),
            dma,
            dma,
        ],
        compiler_params=pltpu.CompilerParams(
            collective_id=0, has_side_effects=True, vmem_limit_bytes=56 * 1024 * 1024
        ),
        name="gather_all",
    )(hidden, cotangent, in_weight_t, small, out_weight)


def reduce_kernel(
    n,
    n_ctx,
    normed_t,
    gate_t,
    upstream,
    d_z,
    d_x,
    d_s,
    mixed_parts,
    normed_parts,
    small,
    hidden,
    cotangent,
    gain,
    g_z,
    g_x,
    g_s,
    g_o,
    layer_out,
    hidden_grad,
    small_out,
    v_normed_t,
    v_gate_t,
    v_upstream,
    v_d_z,
    v_d_x,
    v_d_s,
    slot_o,
    slot_z,
    slot_x,
    slot_s,
    first_o,
    first_z,
    first_x,
    first_s,
    done_o,
    done_z,
    done_x,
    done_s,
    moved,
    mine,
    from_core,
    from_row,
    v_hidden,
    v_cotangent,
    v_gain,
    v_out,
    v_grad,
    small_all,
    small_ctx,
    load_sem,
    store_sem,
    ring_send,
    ring_recv,
    ctx_send,
    ctx_recv,
    own_sem,
    piece_send,
    piece_recv,
    part_send,
    part_recv,
    small_send,
    small_recv,
    small_ctx_send,
    small_ctx_recv,
):
    ring = Ring(n)
    me, shard = ring.me, ring.shard
    row = me // 2
    core = me % 2
    core_at = me + 1 - 2 * core
    row_at = me + 2 - 4 * row
    both_at = row_at + 1 - 2 * core
    other_core, other_row, other_both = (core_at, shard), (row_at, shard), (both_at, shard)
    held_as = me * n + shard
    piece_to = (held_as % n_ctx, held_as // n_ctx)
    sent_as = shard * n_ctx + me
    piece_from = (sent_as // n, sent_as % n)
    moves = sent_as != held_as

    barrier = pltpu.get_barrier_semaphore()

    def greet(device):
        pl.semaphore_signal(barrier, inc=1, device_id=device, device_id_type=MESH)

    def peer(offset):
        return (me, lax.rem(shard + offset, n))

    for device in (other_core, other_row, other_both):
        greet(device)
    lax.fori_loop(1, n, lambda j, carry: (greet(peer(j)), carry)[1], 0)

    own = hidden.shape[0]
    loads = [
        pltpu.make_async_copy(source, target, load_sem.at[i])
        for i, (source, target) in enumerate(
            (
                (gate_t, v_gate_t),
                *((upstream.at[c], v_upstream.at[pl.ds(c * own, own)]) for c in range(n_ctx)),
                (mixed_parts.at[row_at], mine.at[0, 1]),
                (normed_parts.at[row_at], mine.at[1, 1]),
                *((normed_t.at[c], v_normed_t.at[:, pl.ds(c * own, own)]) for c in range(n_ctx)),
                (d_z, v_d_z),
                (mixed_parts.at[me], mine.at[0, 0]),
                (normed_parts.at[me], mine.at[1, 0]),
                (hidden, v_hidden),
                (cotangent, v_cotangent),
                (gain, v_gain),
                (small, small_all.at[shard, pl.ds(0, small.shape[0])]),
                (d_x, v_d_x),
                (d_s, v_d_s),
            )
        )
    ]
    for copy in loads:
        copy.start()

    @pl.when(moves)
    def _():
        greet(piece_to)
        greet(piece_from)
        pl.semaphore_wait(barrier, n + 4)

    @pl.when(jnp.logical_not(moves))
    def _():
        pl.semaphore_wait(barrier, n + 2)

    def to_core(i, which):
        source = (mixed_parts, normed_parts)[i].at[(core_at, both_at)[which]]
        return remote(
            source, from_core.at[i, which], part_send.at[i, which], part_recv.at[i, which], other_core
        )

    def to_row(i):
        return remote(
            mine.at[i, 1], from_row.at[i], part_send.at[i, 2], part_recv.at[i, 2], other_row
        )

    for which in (1, 0):
        for i in (0, 1):
            to_core(i, which).start()

    rows, piece = v_normed_t.shape[0] // (2 * n), done_o.shape[0]
    half = v_d_z.shape[1] // 2
    quarter = v_upstream.shape[1] // 4

    def in_stream(number, right, first, size, slots, stage, done):
        def own(index, way):
            left = v_normed_t[pl.ds(pl.multiple_of((2 * index + way) * rows, 16), rows), :]
            return mm(left, right[:, first : first + size])

        return (
            number,
            own,
            lambda way, step: slots.at[step, way, :, pl.ds(first, size)],
            lambda way: stage.at[way, :, pl.ds(first, size)],
            lambda way: done.at[pl.ds(first, size), pl.ds(way * rows, rows)],
            True,
        )

    def out_stream(number, sub):
        def own(index, way):
            left = v_gate_t[pl.ds(pl.multiple_of(index * piece, 16), piece), :]
            at = (2 * way + sub) * quarter
            return mm(left, v_upstream[:, at : at + quarter])

        return (
            number,
            own,
            lambda way, step: slot_o.at[step, way, :, pl.ds(sub * quarter, quarter)],
            lambda way: first_o.at[way, :, pl.ds(sub * quarter, quarter)],
            lambda way: done_o.at[:, pl.ds((2 * way + sub) * quarter, quarter)],
            False,
        )

    phases = (
        (out_stream(0, 0), out_stream(1, 1)),
        (
            in_stream(2, v_d_z, 0, half, slot_z, first_z, done_z),
            in_stream(3, v_d_z, half, half, slot_z, first_z, done_z),
        ),
        (
            in_stream(4, v_d_s, 0, v_d_s.shape[1], slot_s, first_s, done_s),
            in_stream(5, v_d_x, 0, half, slot_x, first_x, done_x),
            in_stream(6, v_d_x, half, half, slot_x, first_x, done_x),
        ),
    )

    def hop(stream, way, step, source):
        number, own, slot, stage, done, turned = stream
        return remote(
            source,
            slot(way, step),
            ring_send.at[number, way],
            ring_recv.at[number, way, step],
            ring.neighbour(way),
        )

    def start_phase(number):
        for stream in phases[number]:
            for way in (0, 1):
                stage = stream[3](way)
                stage[...] = stream[1](ring.at(-1 if way == 0 else 1), way).astype(BF16)
                hop(stream, way, 0, stage).start()

    def arrived(stream, way, step):
        number, own, slot, stage, done, turned = stream
        partial = own(ring.at(-step - 2 if way == 0 else step + 2), way)
        hop(stream, way, step, stage(way)).wait()
        return slot(way, step)[...].astype(F32) + partial

    def run_phase(number, after):
        def body(step, carry):
            for stream in phases[number]:
                for way in (0, 1):
                    total = arrived(stream, way, step)
                    place = stream[2](way, step)
                    place[...] = total.astype(BF16)
                    hop(stream, way, step + 1, place).start()
            return carry

        lax.fori_loop(0, n - 2, body, 0)
        after()
        for stream in phases[number]:
            for way in (0, 1):
                done, total = stream[4](way), arrived(stream, way, n - 2)
                done[...] = (total.T if stream[5] else total).astype(BF16)

    ctx_pairs = ((moved, g_o), (done_z, g_z), (done_x, g_x), (done_s, g_s))

    def share(i, kind):
        source, whole = ctx_pairs[i]
        if kind == 2:
            source, at = whole.at[row_at], row_at
        else:
            at = me
        device = other_row if kind == 0 else other_core
        return remote(source, whole.at[at], ctx_send.at[i, kind], ctx_recv.at[i, kind], device)

    def keep(i):
        source, whole = ctx_pairs[i]
        return pltpu.make_async_copy(source, whole.at[me], own_sem.at[i])

    def start_share(i):
        share(i, 0).start()
        share(i, 1).start()
        keep(i).start()

    def pass_share(i):
        share(i, 0).wait_recv()
        share(i, 2).start()

    def close_share(i):
        share(i, 0).wait_send()
        share(i, 1).wait()
        share(i, 2).wait()
        keep(i).wait()

    send_piece = remote(done_o, moved, piece_send, piece_recv, piece_to)
    keep_piece = pltpu.make_async_copy(done_o, moved, piece_send)

    def move_piece(wait):
        @pl.when(moves)
        def _():
            send_piece.wait() if wait else send_piece.start()

        @pl.when(jnp.logical_not(moves))
        def _():
            keep_piece.wait() if wait else keep_piece.start()

    def small_to(offset):
        return remote(
            small_all.at[shard],
            small_all.at[shard],
            small_send.at[offset - 1],
            small_recv.at[offset - 1],
            peer(offset),
        )

    def small_share(i):
        return remote(
            small_ctx.at[me],
            small_ctx.at[me],
            small_ctx_send.at[i],
            small_ctx_recv.at[i],
            (other_core, other_row, other_both)[i],
        )

    store_layer = pltpu.make_async_copy(v_out, layer_out, store_sem.at[0])
    store_grad = pltpu.make_async_copy(v_grad, hidden_grad, store_sem.at[1])
    store_small = pltpu.make_async_copy(small_ctx, small_out, store_sem.at[2])

    def sum_rows():
        for i in (0, 1):
            to_core(i, 1).wait()
            mine[i, 1] = (mine[i, 1].astype(F32) + from_core[i, 1].astype(F32)).astype(BF16)
            to_row(i).start()

    def whole_sum(i):
        to_core(i, 0).wait()
        to_row(i).wait()
        return (
            mine[i, 0].astype(F32) + from_core[i, 0].astype(F32) + from_row[i].astype(F32)
        )

    def finish_tokens():
        resid = v_hidden[...].astype(F32)
        v_out[...] = (resid + whole_sum(0)).astype(BF16)
        store_layer.start()
        scale = lax.rsqrt(jnp.mean(resid * resid, axis=1, keepdims=True) + EPS)
        d_normed = whole_sum(1)
        f = v_gain[...] * d_normed
        slope = scale**3 * jnp.mean(resid * f, axis=1, keepdims=True)
        v_grad[...] = (v_cotangent[...].astype(F32) + scale * f - resid * slope).astype(BF16)
        store_grad.start()
        by_model = jnp.sum(d_normed * resid * scale, axis=0, keepdims=True)
        base, size = small.shape[0], d_z.shape[1]
        small_all[shard, base:, :] = jnp.zeros((small_all.shape[1] - base, small.shape[1]), F32)
        for j in range(by_model.shape[1] // size):
            small_all[shard, base + j : base + j + 1, 0:size] = by_model[
                :, j * size : (j + 1) * size
            ]
        lax.fori_loop(1, n, lambda j, carry: (small_to(j).start(), carry)[1], 0)

    def sum_small():
        lax.fori_loop(1, n, lambda j, carry: (small_to(j).wait(), carry)[1], 0)
        small_ctx[me] = jnp.sum(small_all[...], axis=0)
        for i in range(3):
            small_share(i).start()

    for copy in loads[: 1 + n_ctx]:
        copy.wait()
    start_phase(0)
    for copy in loads[1 + n_ctx :]:
        copy.wait()
    sum_rows()

    def after_first():
        start_phase(1)

    def after_second():
        start_phase(2)
        move_piece(True)
        start_share(0)
        finish_tokens()

    def after_third():
        pass_share(0)
        pass_share(1)
        sum_small()

    run_phase(0, after_first)
    move_piece(False)
    run_phase(1, after_second)
    start_share(1)
    run_phase(2, after_third)
    start_share(2)
    start_share(3)
    for i in range(3):
        small_share(i).wait()
    store_small.start()
    pass_share(2)
    pass_share(3)
    for i in range(4):
        close_share(i)
    store_layer.wait()
    store_grad.wait()
    store_small.wait()


def reduce_all(
    n, n_ctx, normed_t, gate_t, upstream, d_z, d_x, d_s, mixed_parts, normed_parts, small, hidden, cotangent, gain
):
    model, tokens = normed_t.shape[1], d_z.shape[0]
    width, shared_width = d_z.shape[1], d_s.shape[1]
    rows, piece, own = model // n, width // n, hidden.shape[0]
    small_rows, small_width = small.shape[0] + 8, small.shape[1]
    any_space = pl.BlockSpec(memory_space=pl.ANY)
    dma = pltpu.SemaphoreType.DMA
    low = lambda *shape: jax.ShapeDtypeStruct(shape, BF16)
    v_low = lambda *shape: pltpu.VMEM(shape, BF16)
    v_full = lambda *shape: pltpu.VMEM(shape, F32)
    return pl.pallas_call(
        functools.partial(reduce_kernel, n, n_ctx),
        in_specs=[any_space] * 12,
        out_specs=[any_space] * 7,
        out_shape=[
            low(n_ctx, width, rows),
            low(n_ctx, width, rows),
            low(n_ctx, shared_width, rows),
            low(n_ctx, piece, model),
            low(own, model),
            low(own, model),
            jax.ShapeDtypeStruct((n_ctx, small_rows, small_width), F32),
        ],
        scratch_shapes=[
            v_low(model, tokens),
            v_low(width, tokens),
            v_low(tokens, model),
            v_low(tokens, width),
            v_low(tokens, width),
            v_low(tokens, shared_width),
            v_low(n - 1, 2, piece, model // 2),
            v_low(n - 1, 2, rows // 2, width),
            v_low(n - 1, 2, rows // 2, width),
            v_low(n - 1, 2, rows // 2, shared_width),
            v_low(2, piece, model // 2),
            v_low(2, rows // 2, width),
            v_low(2, rows // 2, width),
            v_low(2, rows // 2, shared_width),
            v_low(piece, model),
            v_low(width, rows),
            v_low(width, rows),
            v_low(shared_width, rows),
            v_low(piece, model),
            v_low(2, 2, own, model),
            v_low(2, 2, own, model),
            v_low(2, own, model),
            v_low(own, model),
            v_low(own, model),
            v_full(1, model),
            v_low(own, model),
            v_low(own, model),
            v_full(n, small_rows, small_width),
            v_full(n_ctx, small_rows, small_width),
            dma((12 + 2 * n_ctx,)),
            dma((3,)),
            dma((7, 2)),
            dma((7, 2, n - 1)),
            dma((4, 3)),
            dma((4, 3)),
            dma((4,)),
            dma,
            dma,
            dma((2, 3)),
            dma((2, 3)),
            dma((n - 1,)),
            dma((n - 1,)),
            dma((3,)),
            dma((3,)),
        ],
        compiler_params=pltpu.CompilerParams(
            collective_id=1, has_side_effects=True, vmem_limit_bytes=58 * 1024 * 1024
        ),
        name="reduce_all",
    )(
        normed_t, gate_t, upstream, d_z, d_x, d_s, mixed_parts, normed_parts, small, hidden, cotangent, gain
    )


def assemble_kernel(n_ctx, z_ref, x_ref, s_ref, out_ref):
    place = pl.program_id(0)

    @pl.when(place < n_ctx)
    def _():
        out_ref[...] = z_ref[0].astype(F32)

    @pl.when(jnp.logical_and(place >= n_ctx, place < 2 * n_ctx))
    def _():
        out_ref[...] = x_ref[0].astype(F32)

    @pl.when(place == 2 * n_ctx)
    def _():
        total = s_ref[0].astype(F32)
        for c in range(1, n_ctx):
            total += s_ref[c].astype(F32)
        out_ref[0 : total.shape[0], :] = total


def assemble(g_z, g_x, g_s, columns):
    n_ctx, width, rows = g_z.shape
    return pl.pallas_call(
        functools.partial(assemble_kernel, n_ctx),
        grid=(2 * n_ctx + 1,),
        in_specs=[
            pl.BlockSpec((1, width, rows), lambda i: (jnp.minimum(i, n_ctx - 1), 0, 0)),
            pl.BlockSpec((1, width, rows), lambda i: (jnp.clip(i - n_ctx, 0, n_ctx - 1), 0, 0)),
            pl.BlockSpec(g_s.shape, lambda i: (0, 0, 0)),
        ],
        out_specs=pl.BlockSpec((width, rows), lambda i: (i, 0)),
        out_shape=jax.ShapeDtypeStruct((columns, rows), F32),
        compiler_params=pltpu.CompilerParams(vmem_limit_bytes=58 * 1024 * 1024),
        name="assemble",
    )(g_z, g_x, g_s)


def on_device(
    hidden,
    cotangent,
    seq_lens,
    norm_gain,
    in_weight,
    conv_weight,
    conv_bias,
    dt_bias,
    a_log,
    d_skip,
    gate_gain,
    out_weight,
):
    n_ctx, n_fsdp = lax.axis_size("ctx"), lax.axis_size("fsdp")
    me, shard = lax.axis_index("ctx"), lax.axis_index("fsdp")
    taps = conv_weight.shape[0]
    heads_all = dt_bias.shape[0] * n_fsdp
    inner = out_weight.shape[0] * n_fsdp
    heads, width = heads_all // n_ctx, inner // n_ctx
    model = hidden.shape[2]
    both = 2 * STATE
    shared_width = -(-(both + heads_all) // LANES) * LANES

    per_head = jnp.concatenate([dt_bias, a_log, d_skip])
    lines = [norm_gain[None], conv_weight, conv_bias[None], gate_gain[None], per_head[None]]
    longest = -(-max(a.shape[1] for a in lines) // LANES) * LANES
    small = jnp.concatenate([jnp.pad(a, ((0, 0), (0, longest - a.shape[1]))) for a in lines])
    small = jnp.pad(small, ((0, SMALL_ROWS - small.shape[0]), (0, 0)))
    upstream, w_x, w_s, w_z, w_o, small_all, proj_x, proj_s, proj_z, normed_t = gather_all(
        n_fsdp, n_ctx, hidden[0], cotangent[0], in_weight.T, small, out_weight, shared_width
    )
    w_o = w_o.reshape(-1, model)

    def line(first, count, size):
        rows = small_all[:, first : first + count, :size]
        return jnp.moveaxis(rows, 0, 1).reshape(count, -1).astype(F32)

    def own(lines, size):
        return lax.dynamic_slice_in_dim(lines, me * size, size, axis=1)

    gain_norm = line(0, 1, norm_gain.shape[0])
    conv_lines = line(1, taps + 1, conv_bias.shape[0])
    taps_x, taps_s = own(conv_lines[:, :inner], width), conv_lines[:, inner:]
    gain_gate = own(line(taps + 2, 1, gate_gain.shape[0]), width)
    each = small_all[:, taps + 3, : per_head.shape[0]].reshape(n_fsdp, 3, -1)
    each = own(jnp.moveaxis(each, 0, 1).reshape(3, -1).astype(F32), heads)
    head = jnp.pad(jnp.stack([each[0], jnp.exp(each[1])]), ((0, 0), (0, LANES - heads)))
    skip = jnp.repeat(each[2], HEAD)[None]

    *kept_parts, stats = scan_forward(
        seq_lens, proj_x, proj_s, proj_z, upstream, w_o, taps_x, taps_s, gain_gate, skip, head
    )
    stats = lax.psum(stats, "ctx")
    gate_t, mixed_parts, normed_parts, d_z, d_x, d_s, small_grads = scan_backward(
        inner, seq_lens, proj_x, proj_s, proj_z, kept_parts, stats, w_o, w_z, w_x, w_s, taps_x, taps_s, gain_gate, skip, head
    )
    g_z, g_x, g_s, g_o, layer_out, hidden_grad, sums = reduce_all(
        n_fsdp, n_ctx, normed_t, gate_t, upstream, d_z, d_x, d_s, mixed_parts, normed_parts, small_grads, hidden[0], cotangent[0], gain_norm
    )
    grad_in_weight = assemble(g_z, g_x, g_s, 2 * inner + both + heads_all).T
    grad_out_weight = g_o.reshape(-1, model).astype(F32)

    def shard_of(lines):
        size = lines.shape[1] // n_fsdp
        return lax.dynamic_slice_in_dim(lines, shard * size, size, axis=1)

    in_order = lambda a: jnp.moveaxis(a, 0, 1).reshape(a.shape[1], -1)
    conv_sums = shard_of(
        jnp.concatenate(
            [
                in_order(sums[:, : taps + 1, :width]),
                jnp.sum(sums[:, : taps + 1, width:], axis=0),
            ],
            axis=1,
        )
    )
    gate_sums = shard_of(in_order(sums[:, taps + 1 : taps + 2, :width]))
    head_sums_all = sums[:, taps + 2, : 3 * LANES].reshape(n_ctx, 3, LANES)[:, :, :heads]
    head_grads = shard_of(in_order(head_sums_all))
    norm_sums = jnp.sum(sums[:, 8 : 8 + model // width, :width], axis=0).reshape(1, -1)
    return (
        layer_out[None],
        hidden_grad[None],
        shard_of(norm_sums)[0],
        grad_in_weight,
        conv_sums[:taps],
        conv_sums[taps],
        head_grads[0],
        head_grads[1],
        head_grads[2],
        gate_sums[0],
        grad_out_weight,
    )


def solution(mesh):
    tokens, rows, flat = P("fsdp", "ctx", None), P("fsdp", None), P("fsdp")
    taps = P(None, "fsdp")
    return jax.shard_map(
        on_device,
        mesh=mesh,
        in_specs=(tokens, tokens, flat, flat, rows, taps, flat, flat, flat, flat, flat, rows),
        out_specs=(tokens, tokens, flat, rows, taps, flat, flat, flat, flat, flat, rows),
        check_vma=False,
    )
```

time: 581 us -> 525 us (0.904)
  Pallas kernels: 405 us -> 480 us
  matrix products: 44.9 us -> 0 us
  local copies, waits for them, and re-layouts: 58.4 us -> 15.1 us
  other arithmetic: 51.1 us -> 10.1 us
    dot_general x8 -> x0, matrix products: 44.9 us -> none  [mm(): lax.dot_general(a, b, (contract, ((), ())), preferred_element_type=F32)]
    pallas_call x2, Pallas kernels: 35.3 us -> 79 us  [the longest x1 70.8 us: scan_backward(): pl.pallas_call(functools.partial(backward_kernel, heads, channels), grid=...]
    unnamed x115 -> x7, local copies, waits for them, and re-layouts: 35.6 us -> 1.96 us
    convert_element_type x12 -> x5, other arithmetic: 26.3 us -> 6.99 us  [the longest x1 4.13 us: on_device(): grad_out_weight = g_o.reshape(-1, model).astype(F32)]
    pallas_call x1, Pallas kernels: 13.3 us -> 30.7 us  [scan_forward(): pl.pallas_call(functools.partial(forward_kernel, heads), grid=(count,), i...]
    reduce_sum x7 -> x2, other arithmetic: 10.3 us -> 1.69 us  [the longest x1 0.92 us: on_device(): jnp.sum(sums[:, 8:8 + model // width, :width], axis=0).reshape(1, -1)]
    pallas_call x1, Pallas kernels: 168 us -> 176 us  [gather_all(): pl.pallas_call(functools.partial(gather_kernel, n, n_ctx), in_specs=[any_...]
    convert_element_type x5, local copies, waits for them, and re-layouts: 7.15 us -> 0.29 us  [the longest x3 0.17 us: on_device(): each = own(jnp.moveaxis(each, 0, 1).reshape(3, -1).astype(F32), heads)]
where the time goes in v4:
time: 525 us; the launch traced here: 520 us
  Pallas kernels  480 us (91%)
  local copies, waits for them, and re-layouts  15.1 us (3%)
  blocking collectives  13.9 us (3%)
  other arithmetic  10.1 us (2%)
    pallas_call x1, Pallas kernels, reduce_all(): pl.pallas_call(functools.partial(reduce_kernel, n, n_ctx), in_specs=[any_...  194 us
    pallas_call x1, Pallas kernels, gather_all(): pl.pallas_call(functools.partial(gather_kernel, n, n_ctx), in_specs=[any_...  176 us
    pallas_call x1, Pallas kernels, scan_backward(): pl.pallas_call(functools.partial(backward_kernel, heads, channels), grid=...  70.8 us
    pallas_call x1, Pallas kernels, scan_forward(): pl.pallas_call(functools.partial(forward_kernel, heads), grid=(count,), i...  30.7 us
    psum x1, blocking collectives, on_device(): stats = lax.psum(stats, 'ctx')  13.9 us

profile of v4, /device:TPU:17, one launch (start us, length us, event | category | flops | bytes accessed | tf_op | source)
XLA Modules:
  0.0 520.3 jit_solution(6370291497152938170)
XLA Ops:
  1.3 0.8 maximum_bitcast_fusion
  2.1 0.7 broadcast_in_dim.21
  2.7 0.7 broadcast_in_dim.23
  3.4 0.7 broadcast_in_dim.22
  4.1 0.7 pad.29
  4.9 0.6 pad.33.small
  5.5 176.0 %gather_all.1 = (bf16[4,256,2048]{2,1,0:T(8,128)(2,1)}, bf16[2048,1024]{1,0:T(8,128)(2,1)}, bf16[2048,384]{1,0:T(8,128)(2,1)}, bf16[2048,1024]{1,0:T(8,128)(2,1)...) custom-call(bf16[256,2048]{1,0:T(8,128)(2,1)} %bitcast.43, ...), custom_call_target="tpu_custom_call" | custom-call | tf_op jit(solution)/shard_map/gather_all/pallas_call | solution.py:861
  181.5 0.7 convert_reduce_fusion
  182.2 0.8 slice.68
  183.0 0.6 convert.9.gain
  183.6 0.1 reshape.82
  183.7 0.1 reshape.79
  183.8 0.1 constant_dynamic-slice_fusion.3
  183.9 0.6 select_maximum_fusion.head_ref
  184.5 0.1 broadcast_in_dim.25
  184.5 0.7 broadcast_in_dim_reshape.3.skip_ref
  185.2 0.9 slice.63
  186.1 0.9 convert_bitcast_fusion
  187.0 0.6 dynamic-slice_convert_fusion.gate_gain_ref
  187.6 0.1 reshape.77
  187.7 0.6 slice.81.taps_s_ref
  188.3 0.6 constant_dynamic-slice_fusion.4.taps_x_ref
  188.9 30.7 %scan_forward.1 = (bf16[1024,1024]{1,0:T(8,128)(2,1)}, bf16[1024,128]{1,0:T(8,128)(2,1)}, bf16[1024,128]{1,0:T(8,128)(2,1)}, bf16[1024,1024]{1,0:T(8,128)(2,1)},...) custom-call(s32[1]{0:T(128)S(6)} %copy.34.length_ref, ...), custom_call_target="tpu_custom_call" | custom-call | flops 5905580032 | bytes 25165824 | tf_op jit(solution)/shard_map/scan_forward/pallas_call | solution.py:186
  219.7 13.9 %psum.7.stat_ref = f32[8,1024]{1,0:T(8,128)} all-reduce(f32[8,1024]{1,0:T(8,128)} %get-tuple-element.65), channel_id=1, replica_groups=mesh['ctx'=4,'fsdp'=8] {'ctx'}, use_global_device_ids=true, to_apply=%region_0.1 | all-reduce | flops 8192 | bytes 65536 | tf_op jit(solution)/shard_map/psum | solution.py:1449
  233.5 70.8 %scan_backward.1 = (bf16[1024,1024]{1,0:T(8,128)(2,1)}, bf16[4,256,2048]{2,1,0:T(8,128)(2,1)}, bf16[4,256,2048]{2,1,0:T(8,128)(2,1)}, bf16[1024,1024]{1,0:T(8,12...) custom-call(s32[1]{0:T(128)S(6)} %copy.34.length_ref, ...), custom_call_target="tpu_custom_call" | custom-call | flops 16374562816 | bytes 41943040 | tf_op jit(solution)/shard_map/scan_backward/pallas_call | solution.py:478
  304.3 194.1 %reduce_all.1 = (bf16[4,1024,256]{2,1,0:T(8,128)(2,1)}, bf16[4,1024,256]{2,1,0:T(8,128)(2,1)}, bf16[4,384,256]{2,1,0:T(8,128)(2,1)}, bf16[4,128,2048]{2,1,0:T(8,...) custom-call(bf16[4,2048,256]{2,1,0:T(8,128)(2,1)} %get-tuple-element.47.normed_t, ...), custom_call_target="tpu_custom_call" | custom-call | tf_op jit(solution)/shard_map/reduce_all/pallas_call | solution.py:1292
  498.4 0.8 slice.74
  499.2 0.1 reshape.76
  499.3 0.1 constant_dynamic-slice_fusion.1
  499.4 0.5 slice_bitcast_fusion.1
  499.9 0.8 slice_reduce_fusion
  500.7 0.9 slice_reduce_fusion.1
  501.6 0.6 constant_dynamic-slice_fusion.2
  502.2 0.9 slice.79
  503.1 0.9 slice.70
  504.0 0.1 fusion
  504.1 0.6 constant_dynamic-slice_fusion
  504.7 0.6 slice_reduce_fusion.2
  505.3 0.6 slice.82
  505.9 4.1 bitcast_convert_fusion
  510.1 0.0 copy-start.1
  510.1 0.0 copy-start
  510.1 8.1 %assemble.1 = f32[8512,256]{1,0:T(8,128)} custom-call(bf16[4,1024,256]{2,1,0:T(8,128)(2,1)} %get-tuple-element.79.z_ref, bf16[4,1024,256]{2,1,0:T(8,128)(2,1)} %get-tuple-element.80.x_ref, bf16[4,384,256]{2,1,0:T(8,128)(2,1)} %get-tuple-element.81.s_ref), custom_call_target="tpu_custom_call" | custom-call | tf_op jit(solution)/shard_map/assemble/pallas_call | solution.py:1381
  518.2 0.0 copy-done.1
  518.2 1.0 copy.35
  519.2 0.0 copy-done
  519.2 1.0 copy.36
  (12 shorter events, 0.1 us)
Async XLA Ops:
  510.1 8.1 %copy-start.1 = (bf16[256,2048]{1,0:T(8,128)(2,1)S(1)}, bf16[256,2048]{1,0:T(8,128)(2,1)}, u32[]{:S(2)}) copy-start(bf16[256,2048]{1,0:T(8,128)(2,1)} %get-tuple-element.76) | copy-start | bytes 3145732
  510.1 9.1 %copy-start = (bf16[256,2048]{1,0:T(8,128)(2,1)S(1)}, bf16[256,2048]{1,0:T(8,128)(2,1)}, u32[]{:S(2)}) copy-start(bf16[256,2048]{1,0:T(8,128)(2,1)} %get-tuple-element.77) | copy-start | bytes 3145732

commit v5 on v4

--- a/solution.py
+++ b/solution.py
@@ -52,9 +52,12 @@
     return v * s, s * (1.0 + v * (1.0 - s))
 
 
-def own_lanes(array, me, heads, back=False):
-    shift = me * heads if back else lax.rem(LANES - me * heads, LANES)
-    return pltpu.roll(array, shift, 1)
+def chosen_heads(me, heads, unit, n_ctx, turned=False):
+    here, there = iota2((LANES, LANES), 1), iota2((LANES, LANES), 0)
+    if turned:
+        here, there = there, here
+    head = (here // unit * n_ctx + me) * unit + here % unit
+    return jnp.where(jnp.logical_and(there == head, here < heads), 1.0, 0.0).astype(BF16)
 
 
 def column_valid(length_ref, block):
@@ -64,6 +67,8 @@
 
 def forward_kernel(
     heads,
+    unit,
+    n_ctx,
     length_ref,
     px_ref,
     ps_ref,
@@ -123,7 +128,8 @@
     rows_b, rows_c = active[:, :STATE].astype(BF16), active[:, STATE:].astype(BF16)
     b_ref[...] = rows_b
     c_ref[...] = rows_c
-    raw = own_lanes(shared[:, 2 * STATE :], lax.axis_index("ctx"), heads)
+    chosen = chosen_heads(lax.axis_index("ctx"), heads, unit, n_ctx)
+    raw = mm(ps_ref[:, 2 * STATE :], chosen)
     raw = raw + head_ref[0:1]
     own = iota2((1, LANES), 1) < heads
     step = jnp.where(own, valid * jax.nn.softplus(raw), 0.0)
@@ -173,7 +179,7 @@
     stat_ref[...] = both_sums.T[0:8]
 
 
-def scan_forward(length, px, ps, pz, upstream, w_o, taps_x, taps_s, gate_gain, skip, head):
+def scan_forward(unit, n_ctx, length, px, ps, pz, upstream, w_o, taps_x, taps_s, gate_gain, skip, head):
     tokens, width = px.shape
     heads = width // HEAD
     count = tokens // BLOCK
@@ -184,7 +190,7 @@
     low = lambda *shape: jax.ShapeDtypeStruct(shape, BF16)
     full = lambda *shape: jax.ShapeDtypeStruct(shape, F32)
     return pl.pallas_call(
-        functools.partial(forward_kernel, heads),
+        functools.partial(forward_kernel, heads, unit, n_ctx),
         grid=(count,),
         in_specs=[
             pl.BlockSpec(memory_space=pltpu.SMEM),
@@ -252,6 +258,8 @@
 
 def backward_kernel(
     heads,
+    unit,
+    n_ctx,
     channels,
     length_ref,
     px_ref,
@@ -441,7 +449,8 @@
         d_lam * lam, axis=0, keepdims=True
     )
     small_ref[head_row : head_row + 1, 2 * LANES : 3 * LANES] += total[2:3, :]
-    ds_ref[:, 2 * STATE :] = own_lanes(d_raw, lax.axis_index("ctx"), heads, True).astype(BF16)
+    chosen = chosen_heads(lax.axis_index("ctx"), heads, unit, n_ctx, True)
+    ds_ref[:, 2 * STATE :] = mm(d_raw.astype(BF16), chosen).astype(BF16)
 
     @pl.when(turn == 0)
     def _():
@@ -459,7 +468,7 @@
 
 
 def scan_backward(
-    channels, length, px, ps, pz, kept_parts, stats, w_o, w_z, w_x, w_s, taps_x, taps_s, gate_gain, skip, head
+    unit, n_ctx, channels, length, px, ps, pz, kept_parts, stats, w_o, w_z, w_x, w_s, taps_x, taps_s, gate_gain, skip, head
 ):
     x, rows_b, rows_c, slope_x, slope_s, lam, step, chain, kept, y, d_yn = kept_parts
     tokens, width = px.shape
@@ -476,7 +485,7 @@
     part = lambda a, b: pl.BlockSpec((1, a, b), lambda i: (count - 1 - i, 0, 0))
     small_shape = (8, width + 2 * STATE)
     return pl.pallas_call(
-        functools.partial(backward_kernel, heads, channels),
+        functools.partial(backward_kernel, heads, unit, n_ctx, channels),
         grid=(count,),
         in_specs=[
             pl.BlockSpec(memory_space=pltpu.SMEM),
@@ -593,6 +602,8 @@
 def gather_kernel(
     n,
     n_ctx,
+    unit,
+    direct,
     hidden,
     cotangent,
     in_weight_t,
@@ -623,6 +634,7 @@
     out_t,
     v_gain,
     load_sem,
+    column_sem,
     local_sem,
     store_sem,
     ring_send,
@@ -642,40 +654,56 @@
     other_core = (me + 1 - 2 * (me % 2), shard)
     other_row = (me + 2 - 4 * row, shard)
     piece = w_o.shape[1]
-    sent_as = shard * n_ctx + me
-    piece_to = (sent_as // n, sent_as % n)
-    held_as = me * n + shard
-    piece_from = (held_as % n_ctx, held_as // n_ctx)
-    moves = sent_as != held_as
+    piece_peer = (shard % n_ctx, shard // n_ctx * n_ctx + me)
+    moves = shard % n_ctx != me
 
     barrier = pltpu.get_barrier_semaphore()
     for device in (other_core, other_row, ring.neighbour(0), ring.neighbour(1)):
         pl.semaphore_signal(barrier, inc=1, device_id=device, device_id_type=MESH)
 
+    part = unit * HEAD
+
+    def load_columns(base, target, sems):
+        return [
+            pltpu.make_async_copy(
+                in_weight_t.at[pl.ds(pl.multiple_of(base + (a * n_ctx + me) * part, 16), part)],
+                target.at[pl.ds(a * part, part)],
+                sems.at[a],
+            )
+            for a in range(width // part)
+        ]
+
     loads = [
-        pltpu.make_async_copy(source, target, load_sem.at[i])
-        for i, (source, target) in enumerate(
-            (
-                (in_weight_t.at[pl.ds(pl.multiple_of(inner + me * width, width), width)], raw_x),
-                (in_weight_t.at[pl.ds(2 * inner, shared)], raw_s.at[pl.ds(0, shared)]),
-                (small, v_small.at[shard]),
-                (hidden, v_hidden.at[me]),
-                (in_weight_t.at[pl.ds(pl.multiple_of(me * width, width), width)], raw_z),
+        load_columns(inner, raw_x, column_sem.at[0]),
+        [
+            pltpu.make_async_copy(
+                in_weight_t.at[pl.ds(2 * inner, shared)], raw_s.at[pl.ds(0, shared)], load_sem.at[0]
             )
-        )
+        ],
+        [pltpu.make_async_copy(small, v_small.at[shard], load_sem.at[1])],
+        [pltpu.make_async_copy(hidden, v_hidden.at[me], load_sem.at[2])],
+        load_columns(0, raw_z, column_sem.at[1]),
     ]
-    for copy in loads:
-        copy.start()
-
-    @pl.when(moves)
-    def _():
-        for device in (piece_to, piece_from):
-            pl.semaphore_signal(barrier, inc=1, device_id=device, device_id_type=MESH)
-        pl.semaphore_wait(barrier, 6)
-
-    @pl.when(jnp.logical_not(moves))
-    def _():
+    for copies in loads:
+        for copy in copies:
+            copy.start()
+
+    def loaded(i):
+        for copy in loads[i]:
+            copy.wait()
+
+    if direct:
         pl.semaphore_wait(barrier, 4)
+    else:
+
+        @pl.when(moves)
+        def _():
+            pl.semaphore_signal(barrier, inc=1, device_id=piece_peer, device_id_type=MESH)
+            pl.semaphore_wait(barrier, 5)
+
+        @pl.when(jnp.logical_not(moves))
+        def _():
+            pl.semaphore_wait(barrier, 4)
 
     half, quarter = width // 2, w_o.shape[2] // 4
     rows = r // 2
@@ -725,21 +753,25 @@
     to_row(0, hidden, v_hidden).start()
     to_core(0, hidden, v_hidden).start()
     own_rows = pl.ds(pl.multiple_of(shard * r, 16), r)
-    loads[2].wait()
+    loaded(2)
     start_stream(phases[0][0])
-    loads[0].wait()
+    loaded(0)
     v_x[own_rows, :] = raw_x[...].T
     start_stream(phases[0][2])
     start_stream(phases[0][3])
-    loads[1].wait()
+    loaded(1)
     raw_s[shared:, :] = jnp.zeros((raw_s.shape[0] - shared, r), BF16)
     v_s[own_rows, :] = raw_s[...].T
     start_stream(phases[0][1])
     own_piece = out_weight.at[pl.ds(pl.multiple_of(me * piece, 16), piece)]
-    send_piece = remote(own_piece, w_o.at[piece_to[1]], piece_send, piece_recv, piece_to)
     keep_piece = pltpu.make_async_copy(own_piece, w_o.at[shard], piece_send)
 
     def move_piece(wait):
+        if direct:
+            keep_piece.wait() if wait else keep_piece.start()
+            return
+        send_piece = remote(own_piece, w_o.at[piece_peer[1]], piece_send, piece_recv, piece_peer)
+
         @pl.when(moves)
         def _():
             send_piece.wait() if wait else send_piece.start()
@@ -750,8 +782,8 @@
 
     keep_cotangent = pltpu.make_async_copy(cotangent, cotangent_all.at[me], local_sem)
     keep_cotangent.start()
-    loads[3].wait()
-    loads[4].wait()
+    loaded(3)
+    loaded(4)
     v_z[own_rows, :] = raw_z[...].T
 
     def run_phase(number, work, after):
@@ -849,7 +881,7 @@
         copy.wait()
 
 
-def gather_all(n, n_ctx, hidden, cotangent, in_weight_t, small, out_weight, shared_width):
+def gather_all(n, n_ctx, unit, direct, hidden, cotangent, in_weight_t, small, out_weight, shared_width):
     own, model = hidden.shape
     tokens = own * n_ctx
     width = out_weight.shape[0] * n // n_ctx
@@ -859,7 +891,7 @@
     v_low = lambda *shape: pltpu.VMEM(shape, BF16)
     dma = pltpu.SemaphoreType.DMA
     return pl.pallas_call(
-        functools.partial(gather_kernel, n, n_ctx),
+        functools.partial(gather_kernel, n, n_ctx, unit, direct),
         in_specs=[any_space] * 5,
         out_specs=[any_space] * 10,
         out_shape=[
@@ -889,7 +921,8 @@
             v_low(tokens, width),
             v_low(n_ctx, model, own),
             pltpu.VMEM((1, model), F32),
-            dma((5,)),
+            dma((3,)),
+            dma((2, width // (unit * HEAD))),
             dma,
             dma((8,)),
             dma((8, 2)),
@@ -909,6 +942,7 @@
 def reduce_kernel(
     n,
     n_ctx,
+    direct,
     normed_t,
     gate_t,
     upstream,
@@ -981,11 +1015,8 @@
     row_at = me + 2 - 4 * row
     both_at = row_at + 1 - 2 * core
     other_core, other_row, other_both = (core_at, shard), (row_at, shard), (both_at, shard)
-    held_as = me * n + shard
-    piece_to = (held_as % n_ctx, held_as // n_ctx)
-    sent_as = shard * n_ctx + me
-    piece_from = (sent_as // n, sent_as % n)
-    moves = sent_as != held_as
+    piece_peer = (shard % n_ctx, shard // n_ctx * n_ctx + me)
+    moves = shard % n_ctx != me
 
     barrier = pltpu.get_barrier_semaphore()
 
@@ -1024,15 +1055,18 @@
     for copy in loads:
         copy.start()
 
-    @pl.when(moves)
-    def _():
-        greet(piece_to)
-        greet(piece_from)
-        pl.semaphore_wait(barrier, n + 4)
-
-    @pl.when(jnp.logical_not(moves))
-    def _():
+    if direct:
         pl.semaphore_wait(barrier, n + 2)
+    else:
+
+        @pl.when(moves)
+        def _():
+            greet(piece_peer)
+            pl.semaphore_wait(barrier, n + 3)
+
+        @pl.when(jnp.logical_not(moves))
+        def _():
+            pl.semaphore_wait(barrier, n + 2)
 
     def to_core(i, which):
         source = (mixed_parts, normed_parts)[i].at[(core_at, both_at)[which]]
@@ -1135,7 +1169,7 @@
                 done, total = stream[4](way), arrived(stream, way, n - 2)
                 done[...] = (total.T if stream[5] else total).astype(BF16)
 
-    ctx_pairs = ((moved, g_o), (done_z, g_z), (done_x, g_x), (done_s, g_s))
+    ctx_pairs = ((done_o if direct else moved, g_o), (done_z, g_z), (done_x, g_x), (done_s, g_s))
 
     def share(i, kind):
         source, whole = ctx_pairs[i]
@@ -1165,10 +1199,12 @@
         share(i, 2).wait()
         keep(i).wait()
 
-    send_piece = remote(done_o, moved, piece_send, piece_recv, piece_to)
-    keep_piece = pltpu.make_async_copy(done_o, moved, piece_send)
-
     def move_piece(wait):
+        if direct:
+            return
+        keep_piece = pltpu.make_async_copy(done_o, moved, piece_send)
+        send_piece = remote(done_o, moved, piece_send, piece_recv, piece_peer)
+
         @pl.when(moves)
         def _():
             send_piece.wait() if wait else send_piece.start()
@@ -1278,7 +1314,7 @@
 
 
 def reduce_all(
-    n, n_ctx, normed_t, gate_t, upstream, d_z, d_x, d_s, mixed_parts, normed_parts, small, hidden, cotangent, gain
+    n, n_ctx, direct, normed_t, gate_t, upstream, d_z, d_x, d_s, mixed_parts, normed_parts, small, hidden, cotangent, gain
 ):
     model, tokens = normed_t.shape[1], d_z.shape[0]
     width, shared_width = d_z.shape[1], d_s.shape[1]
@@ -1290,7 +1326,7 @@
     v_low = lambda *shape: pltpu.VMEM(shape, BF16)
     v_full = lambda *shape: pltpu.VMEM(shape, F32)
     return pl.pallas_call(
-        functools.partial(reduce_kernel, n, n_ctx),
+        functools.partial(reduce_kernel, n, n_ctx, direct),
         in_specs=[any_space] * 12,
         out_specs=[any_space] * 7,
         out_shape=[
@@ -1357,16 +1393,24 @@
     )
 
 
-def assemble_kernel(n_ctx, z_ref, x_ref, s_ref, out_ref):
+def assemble_kernel(part, z_ref, x_ref, s_ref, out_ref):
     place = pl.program_id(0)
+    n_ctx, size = z_ref.shape[0], z_ref.shape[1]
+
+    def interleave(ref):
+        for a in range(size // part):
+            for c in range(n_ctx):
+                out_ref[(a * n_ctx + c) * part : (a * n_ctx + c + 1) * part, :] = ref[
+                    c, a * part : (a + 1) * part, :
+                ].astype(F32)
 
     @pl.when(place < n_ctx)
     def _():
-        out_ref[...] = z_ref[0].astype(F32)
+        interleave(z_ref)
 
     @pl.when(jnp.logical_and(place >= n_ctx, place < 2 * n_ctx))
     def _():
-        out_ref[...] = x_ref[0].astype(F32)
+        interleave(x_ref)
 
     @pl.when(place == 2 * n_ctx)
     def _():
@@ -1376,14 +1420,15 @@
         out_ref[0 : total.shape[0], :] = total
 
 
-def assemble(g_z, g_x, g_s, columns):
+def assemble(part, g_z, g_x, g_s, columns):
     n_ctx, width, rows = g_z.shape
+    block = (n_ctx, width // n_ctx, rows)
     return pl.pallas_call(
-        functools.partial(assemble_kernel, n_ctx),
+        functools.partial(assemble_kernel, part),
         grid=(2 * n_ctx + 1,),
         in_specs=[
-            pl.BlockSpec((1, width, rows), lambda i: (jnp.minimum(i, n_ctx - 1), 0, 0)),
-            pl.BlockSpec((1, width, rows), lambda i: (jnp.clip(i - n_ctx, 0, n_ctx - 1), 0, 0)),
+            pl.BlockSpec(block, lambda i: (0, jnp.minimum(i, n_ctx - 1), 0)),
+            pl.BlockSpec(block, lambda i: (0, jnp.clip(i - n_ctx, 0, n_ctx - 1), 0)),
             pl.BlockSpec(g_s.shape, lambda i: (0, 0, 0)),
         ],
         out_specs=pl.BlockSpec((width, rows), lambda i: (i, 0)),
@@ -1415,6 +1460,10 @@
     heads, width = heads_all // n_ctx, inner // n_ctx
     model = hidden.shape[2]
     both = 2 * STATE
+    held = dt_bias.shape[0]
+    direct = held % n_ctx == 0
+    unit = held // n_ctx if direct else 1
+    part = unit * HEAD
     shared_width = -(-(both + heads_all) // LANES) * LANES
 
     per_head = jnp.concatenate([dt_bias, a_log, d_skip])
@@ -1423,7 +1472,7 @@
     small = jnp.concatenate([jnp.pad(a, ((0, 0), (0, longest - a.shape[1]))) for a in lines])
     small = jnp.pad(small, ((0, SMALL_ROWS - small.shape[0]), (0, 0)))
     upstream, w_x, w_s, w_z, w_o, small_all, proj_x, proj_s, proj_z, normed_t = gather_all(
-        n_fsdp, n_ctx, hidden[0], cotangent[0], in_weight.T, small, out_weight, shared_width
+        n_fsdp, n_ctx, unit, direct, hidden[0], cotangent[0], in_weight.T, small, out_weight, shared_width
     )
     w_o = w_o.reshape(-1, model)
 
@@ -1432,47 +1481,52 @@
         return jnp.moveaxis(rows, 0, 1).reshape(count, -1).astype(F32)
 
     def own(lines, size):
-        return lax.dynamic_slice_in_dim(lines, me * size, size, axis=1)
+        by_part = lines.reshape(lines.shape[0], -1, n_ctx, size)
+        return lax.dynamic_index_in_dim(by_part, me, 2, False).reshape(lines.shape[0], -1)
 
     gain_norm = line(0, 1, norm_gain.shape[0])
     conv_lines = line(1, taps + 1, conv_bias.shape[0])
-    taps_x, taps_s = own(conv_lines[:, :inner], width), conv_lines[:, inner:]
-    gain_gate = own(line(taps + 2, 1, gate_gain.shape[0]), width)
+    taps_x, taps_s = own(conv_lines[:, :inner], part), conv_lines[:, inner:]
+    gain_gate = own(line(taps + 2, 1, gate_gain.shape[0]), part)
     each = small_all[:, taps + 3, : per_head.shape[0]].reshape(n_fsdp, 3, -1)
-    each = own(jnp.moveaxis(each, 0, 1).reshape(3, -1).astype(F32), heads)
+    each = own(jnp.moveaxis(each, 0, 1).reshape(3, -1).astype(F32), unit)
     head = jnp.pad(jnp.stack([each[0], jnp.exp(each[1])]), ((0, 0), (0, LANES - heads)))
     skip = jnp.repeat(each[2], HEAD)[None]
 
     *kept_parts, stats = scan_forward(
-        seq_lens, proj_x, proj_s, proj_z, upstream, w_o, taps_x, taps_s, gain_gate, skip, head
+        unit, n_ctx, seq_lens, proj_x, proj_s, proj_z, upstream, w_o, taps_x, taps_s, gain_gate, skip, head
     )
     stats = lax.psum(stats, "ctx")
     gate_t, mixed_parts, normed_parts, d_z, d_x, d_s, small_grads = scan_backward(
-        inner, seq_lens, proj_x, proj_s, proj_z, kept_parts, stats, w_o, w_z, w_x, w_s, taps_x, taps_s, gain_gate, skip, head
+        unit, n_ctx, inner, seq_lens, proj_x, proj_s, proj_z, kept_parts, stats, w_o, w_z, w_x, w_s, taps_x, taps_s, gain_gate, skip, head
     )
     g_z, g_x, g_s, g_o, layer_out, hidden_grad, sums = reduce_all(
-        n_fsdp, n_ctx, normed_t, gate_t, upstream, d_z, d_x, d_s, mixed_parts, normed_parts, small_grads, hidden[0], cotangent[0], gain_norm
+        n_fsdp, n_ctx, direct, normed_t, gate_t, upstream, d_z, d_x, d_s, mixed_parts, normed_parts, small_grads, hidden[0], cotangent[0], gain_norm
     )
-    grad_in_weight = assemble(g_z, g_x, g_s, 2 * inner + both + heads_all).T
+    grad_in_weight = assemble(part, g_z, g_x, g_s, 2 * inner + both + heads_all).T
     grad_out_weight = g_o.reshape(-1, model).astype(F32)
 
     def shard_of(lines):
         size = lines.shape[1] // n_fsdp
         return lax.dynamic_slice_in_dim(lines, shard * size, size, axis=1)
 
-    in_order = lambda a: jnp.moveaxis(a, 0, 1).reshape(a.shape[1], -1)
+    def in_order(sums_of, size):
+        lines = sums_of.shape[1]
+        by_part = sums_of.reshape(n_ctx, lines, -1, size)
+        return jnp.transpose(by_part, (1, 2, 0, 3)).reshape(lines, -1)
+
     conv_sums = shard_of(
         jnp.concatenate(
             [
-                in_order(sums[:, : taps + 1, :width]),
+                in_order(sums[:, : taps + 1, :width], part),
                 jnp.sum(sums[:, : taps + 1, width:], axis=0),
             ],
             axis=1,
         )
     )
-    gate_sums = shard_of(in_order(sums[:, taps + 1 : taps + 2, :width]))
+    gate_sums = shard_of(in_order(sums[:, taps + 1 : taps + 2, :width], part))
     head_sums_all = sums[:, taps + 2, : 3 * LANES].reshape(n_ctx, 3, LANES)[:, :, :heads]
-    head_grads = shard_of(in_order(head_sums_all))
+    head_grads = shard_of(in_order(head_sums_all, unit))
     norm_sums = jnp.sum(sums[:, 8 : 8 + model // width, :width], axis=0).reshape(1, -1)
     return (
         layer_out[None],

time: 525 us -> 466 us (0.89)
  Pallas kernels: 480 us -> 415 us
    pallas_call x5, Pallas kernels: 480 us -> 415 us  [the longest x1 173 us: reduce_all(): pl.pallas_call(functools.partial(reduce_kernel, n, n_ctx, direct), in_spe...]
where the time goes in v5:
time: 466 us; the launch traced here: 457 us
  Pallas kernels  415 us (89%)
  local copies, waits for them, and re-layouts  15.8 us (3%)
  blocking collectives  13.8 us (3%)
  other arithmetic  10.4 us (2%)
    pallas_call x1, Pallas kernels, reduce_all(): pl.pallas_call(functools.partial(reduce_kernel, n, n_ctx, direct), in_spe...  173 us
    pallas_call x1, Pallas kernels, gather_all(): pl.pallas_call(functools.partial(gather_kernel, n, n_ctx, unit, direct),...  143 us
    pallas_call x1, Pallas kernels, scan_backward(): pl.pallas_call(functools.partial(backward_kernel, heads, unit, n_ctx, cha...  61.3 us
    pallas_call x1, Pallas kernels, scan_forward(): pl.pallas_call(functools.partial(forward_kernel, heads, unit, n_ctx), gri...  30 us
    psum x1, blocking collectives, on_device(): stats = lax.psum(stats, 'ctx')  13.8 us

profile of v5, /device:TPU:17, one launch (start us, length us, event | category | flops | bytes accessed | tf_op | source)
XLA Modules:
  0.0 457.1 jit_solution(15339844407175716917)
XLA Ops:
  1.3 0.8 maximum_bitcast_fusion
  2.1 0.7 broadcast_in_dim.21
  2.7 0.7 broadcast_in_dim.23
  3.4 0.7 broadcast_in_dim.22
  4.1 0.7 pad.29
  4.9 0.6 pad.33.small
  5.5 142.7 %gather_all.1 = (bf16[4,256,2048]{2,1,0:T(8,128)(2,1)}, bf16[2048,1024]{1,0:T(8,128)(2,1)}, bf16[2048,384]{1,0:T(8,128)(2,1)}, bf16[2048,1024]{1,0:T(8,128)(2,1)...) custom-call(bf16[256,2048]{1,0:T(8,128)(2,1)} %bitcast.65, ...), custom_call_target="tpu_custom_call" | custom-call | tf_op jit(solution)/shard_map/gather_all/pallas_call | solution.py:893
  148.2 0.7 convert_reduce_fusion
  148.9 0.8 slice.74
  149.7 0.6 convert.8.gain
  150.3 0.1 reshape.134
  150.4 0.1 copy.40
  150.5 0.1 copy.42
  150.5 0.1 slice.72
  150.6 0.1 copy.41
  150.7 0.1 squeeze.38
  150.8 0.1 copy.43
  150.9 0.1 exp.14
  150.9 0.6 select_maximum_fusion.head_ref
  151.6 0.7 broadcast_in_dim_reshape.3.skip_ref
  152.3 0.9 slice_convert_fusion
  153.1 0.9 convert_bitcast_fusion
  154.1 0.6 dynamic-slice_bitcast_fusion.gate_gain_ref
  154.7 0.1 reshape.129
  154.8 0.6 slice.87.taps_s_ref
  155.5 0.6 copy.57
  156.2 30.0 %scan_forward.1 = (bf16[1024,1024]{1,0:T(8,128)(2,1)}, bf16[1024,128]{1,0:T(8,128)(2,1)}, bf16[1024,128]{1,0:T(8,128)(2,1)}, bf16[1024,1024]{1,0:T(8,128)(2,1)},...) custom-call(s32[1]{0:T(128)S(6)} %copy.61.length_ref, ...), custom_call_target="tpu_custom_call" | custom-call | flops 5905580032 | bytes 25165824 | tf_op jit(solution)/shard_map/scan_forward/pallas_call | solution.py:192
  186.2 13.8 %psum.7.stat_ref = f32[8,1024]{1,0:T(8,128)} all-reduce(f32[8,1024]{1,0:T(8,128)} %get-tuple-element.65), channel_id=1, replica_groups=mesh['ctx'=4,'fsdp'=8] {'ctx'}, use_global_device_ids=true, to_apply=%region_0.1 | all-reduce | flops 8192 | bytes 65536 | tf_op jit(solution)/shard_map/psum | solution.py:1499
  200.0 61.3 %scan_backward.1 = (bf16[1024,1024]{1,0:T(8,128)(2,1)}, bf16[4,256,2048]{2,1,0:T(8,128)(2,1)}, bf16[4,256,2048]{2,1,0:T(8,128)(2,1)}, bf16[1024,1024]{1,0:T(8,12...) custom-call(s32[1]{0:T(128)S(6)} %copy.61.length_ref, ...), custom_call_target="tpu_custom_call" | custom-call | flops 16374562816 | bytes 41943040 | tf_op jit(solution)/shard_map/scan_backward/pallas_call | solution.py:487
  261.3 173.3 %reduce_all.1 = (bf16[4,1024,256]{2,1,0:T(8,128)(2,1)}, bf16[4,1024,256]{2,1,0:T(8,128)(2,1)}, bf16[4,384,256]{2,1,0:T(8,128)(2,1)}, bf16[4,128,2048]{2,1,0:T(8,...) custom-call(bf16[4,2048,256]{2,1,0:T(8,128)(2,1)} %get-tuple-element.47.normed_t, ...), custom_call_target="tpu_custom_call" | custom-call | tf_op jit(solution)/shard_map/reduce_all/pallas_call | solution.py:1328
  434.6 0.8 slice.80
  435.4 0.8 slice_reduce_fusion
  436.2 0.9 slice_reduce_fusion.1
  437.1 0.6 constant_dynamic-slice_fusion.4
  437.7 0.9 slice.85
  438.6 0.9 slice.76
  439.6 0.6 constant_dynamic-slice_fusion.2
  440.2 0.1 copy.47
  440.3 0.3 copy.48
  440.5 0.1 reshape.126
  440.7 0.5 slice_bitcast_fusion
  441.3 0.1 fusion
  441.4 0.6 slice_reduce_fusion.2
  442.0 0.6 slice.88
  442.6 4.1 bitcast_convert_fusion
  446.7 8.2 %assemble.1 = f32[8512,256]{1,0:T(8,128)} custom-call(bf16[4,1024,256]{2,1,0:T(8,128)(2,1)} %get-tuple-element.79.z_ref, bf16[4,1024,256]{2,1,0:T(8,128)(2,1)} %get-tuple-element.80.x_ref, bf16[4,384,256]{2,1,0:T(8,128)(2,1)} %get-tuple-element.81.s_ref), custom_call_target="tpu_custom_call" | custom-call | tf_op jit(solution)/shard_map/assemble/pallas_call | solution.py:1426
  454.9 1.0 copy.62
  455.9 1.0 copy.63
  (22 shorter events, 0.5 us)
Async XLA Ops:
  446.7 8.2 %copy-start.1 = (bf16[256,2048]{1,0:T(8,128)(2,1)S(1)}, bf16[256,2048]{1,0:T(8,128)(2,1)}, u32[]{:S(2)}) copy-start(bf16[256,2048]{1,0:T(8,128)(2,1)} %get-tuple-element.76) | copy-start | bytes 3145732
  446.7 9.1 %copy-start = (bf16[256,2048]{1,0:T(8,128)(2,1)S(1)}, bf16[256,2048]{1,0:T(8,128)(2,1)}, u32[]{:S(2)}) copy-start(bf16[256,2048]{1,0:T(8,128)(2,1)} %get-tuple-element.77) | copy-start | bytes 3145732
